TPU v7x, 128 devices: a whole 4x4x4 slice. The times are simulated.
128 devices in a mesh: gx: 8 (over y, core), gy: 16 (over x, z).
Axes of the slice: x: 4, y: 4, z: 4, core: 2. Of those that a mesh axis runs over, the one named last changes fastest.
Arguments:
- pressure: float32 [10, 256, 2048], P(None, 'gx', 'gy'), may hold values from -2 to -0.1
- soil: int32 [10, 256, 2048], P(None, 'gx', 'gy'), may hold values from 0 to 22
- vg_alpha: float32 [23], replicated, may hold values from 0.5 to 2.5
- vg_n: float32 [23], replicated, may hold values from 1.4 to 2.6
- sat_cond: float32 [23], replicated, may hold values from 0.2 to 5
- storage: float32 [10, 256, 2048], P(None, 'gx', 'gy'), may hold values from 0.02 to 0.2
- right_side: float32 [10, 256, 2048], P(None, 'gx', 'gy'), may hold values from -30 to 30
Outputs:
- solution: float32 [10, 256, 2048], P(None, 'gx', 'gy')
- new_residual: float32 [10, 256, 2048], P(None, 'gx', 'gy')
- residual_norm: float32 [1], replicated
All inputs are finite; a program needn't handle non-finite values.
Results may differ from a plain program's by a relative error of at most 0.009.
Values sent between devices are 32-bit elements; how exact they have to be, the bound alone decides.
No kernel may reach another device: no remote copies, remote signals or barrier semaphores. Data moves between devices by JAX's collectives and lax.ppermute only.
A program may use at most 192 MiB of HBM per device.

v0:
```python
import jax
import jax.numpy as jnp
from jax import lax
from jax.sharding import PartitionSpec as P

NSOIL = 23
COARSE_PAIRS = 3


WEIGHT_Z = 2.0


def with_halo(shard, sides, width):
    for axis, dim in sides:
        peers, length = (lax.axis_size(axis), shard.shape[dim])
        up = [(i, (i + 1) % peers) for i in range(peers - 1)]
        down = [(j, i) for i, j in up]
        last = lax.slice_in_dim(shard, length - width, length, axis=dim)
        first = lax.slice_in_dim(shard, 0, width, axis=dim)
        before = lax.ppermute(last, axis, up)
        after = lax.ppermute(first, axis, down)
        shard = jnp.concatenate([before, shard, after], axis=dim)
    return shard


def soil_values(soil, vg_alpha, vg_n, sat_cond):
    entry_scale = jnp.zeros(soil.shape, jnp.float32)
    pore_index = jnp.zeros(soil.shape, jnp.float32)
    saturated = jnp.zeros(soil.shape, jnp.float32)
    for soil_kind in range(NSOIL):
        matched = soil == soil_kind
        entry_scale = jnp.where(matched, vg_alpha[soil_kind], entry_scale)
        pore_index = jnp.where(matched, vg_n[soil_kind], pore_index)
        saturated = jnp.where(matched, sat_cond[soil_kind], saturated)
    return (entry_scale, pore_index, saturated)


def conductivity(pressure, soil, vg_alpha, vg_n, sat_cond):
    entry_scale, pore_index, saturated = soil_values(soil, vg_alpha, vg_n, sat_cond)
    exponent = 1.0 - 1.0 / pore_index
    scaled_head = jnp.power(entry_scale * jnp.abs(pressure), pore_index)
    rooted = jnp.exp(-0.5 * exponent * jnp.log1p(scaled_head))
    outer_term = -jnp.expm1(-exponent * jnp.log1p(1.0 / scaled_head))
    return saturated * rooted * outer_term * outer_term


def exchange_faces(field):
    return with_halo(field, (("gx", 1), ("gy", 2)), 1)


def pad_zero(field):
    return jnp.pad(field, ((0, 0), (1, 1), (1, 1)))


def beside_sum(padded, coeffs):
    centre = padded[:, 1:-1, 1:-1]
    vertical = jnp.pad(centre, ((1, 1), (0, 0), (0, 0)))
    return (
        coeffs[1] * padded[:, 2:, 1:-1]
        + coeffs[2] * padded[:, :-2, 1:-1]
        + coeffs[3] * padded[:, 1:-1, 2:]
        + coeffs[4] * padded[:, 1:-1, :-2]
        + coeffs[5] * vertical[2:]
        + coeffs[6] * vertical[:-2]
    )


def diagonal_of(coeffs):
    return coeffs[0] + coeffs[1] + coeffs[2] + coeffs[3] + coeffs[4] + coeffs[5] + coeffs[6]


def colours(shape, start_x, start_y):
    layer_ids = lax.broadcasted_iota(jnp.int32, shape, 0)
    row_ids = lax.broadcasted_iota(jnp.int32, shape, 1) + start_x
    column_ids = lax.broadcasted_iota(jnp.int32, shape, 2) + start_y
    return (layer_ids + row_ids + column_ids) % 2


def half_sweep(field, source, coeffs, diagonal, colour, wanted, pad_fn):
    beside = beside_sum(pad_fn(field), coeffs)
    return jnp.where(colour == wanted, (source + beside) / diagonal, field)


def apply_operator(field, coeffs, diagonal, pad_fn):
    return diagonal * field - beside_sum(pad_fn(field), coeffs)


def block_sum(field):
    layers, rows_x, rows_y = field.shape
    return field.reshape(layers, rows_x // 2, 2, rows_y // 2, 2).sum(axis=(2, 4))


def prolong(field):
    return jnp.repeat(jnp.repeat(field, 2, axis=1), 2, axis=2)


def coarsen(coeffs):
    storage, east, west, north, south, upward, downward = coeffs
    layers, rows_x, rows_y = east.shape
    coarse_east = east[:, 1::2, :].reshape(layers, rows_x // 2, rows_y // 2, 2).sum(axis=3)
    coarse_west = west[:, 0::2, :].reshape(layers, rows_x // 2, rows_y // 2, 2).sum(axis=3)
    coarse_north = north[:, :, 1::2].reshape(layers, rows_x // 2, 2, rows_y // 2).sum(axis=2)
    coarse_south = south[:, :, 0::2].reshape(layers, rows_x // 2, 2, rows_y // 2).sum(axis=2)
    return (
        block_sum(storage),
        coarse_east,
        coarse_west,
        coarse_north,
        coarse_south,
        block_sum(upward),
        block_sum(downward),
    )


def descend(source, coeffs, diagonal, colour, pad_fn):
    field = jnp.zeros_like(source)
    field = half_sweep(field, source, coeffs, diagonal, colour, 0, pad_fn)
    field = half_sweep(field, source, coeffs, diagonal, colour, 1, pad_fn)
    residual = source - apply_operator(field, coeffs, diagonal, pad_fn)
    return (field, block_sum(residual))


def ascend(field, correction, source, coeffs, diagonal, colour, pad_fn):
    field = field + prolong(correction)
    field = half_sweep(field, source, coeffs, diagonal, colour, 1, pad_fn)
    field = half_sweep(field, source, coeffs, diagonal, colour, 0, pad_fn)
    return field


def coarsest(source, coeffs, diagonal, colour):
    level_mean = jnp.sum(source) / jnp.sum(coeffs[0])
    field = jnp.zeros_like(source) + level_mean
    for sweep_pair in range(COARSE_PAIRS):
        for wanted in (0, 1, 1, 0):
            field = half_sweep(field, source, coeffs, diagonal, colour, wanted, pad_zero)
    return field


def cycle_whole(source, coeffs):
    diagonal = diagonal_of(coeffs)
    colour = colours(source.shape, 0, 0)
    return coarsest(source, coeffs, diagonal, colour)


def arrange(gathered, count_x, count_y):
    leading = gathered.shape[:-2]
    rows_x = gathered.shape[-2] // (count_x * count_y)
    rows_y = gathered.shape[-1]
    number = len(leading)
    blocks = gathered.reshape(leading + (count_x, count_y, rows_x, rows_y))
    ordering = tuple(range(number)) + (number, number + 2, number + 1, number + 3)
    return jnp.transpose(blocks, ordering).reshape(leading + (count_x * rows_x, count_y * rows_y))


def replicated(source, coeffs, index_x, index_y):
    layers, rows_x, rows_y = source.shape
    count_x = lax.axis_size("gx")
    count_y = lax.axis_size("gy")
    packed = jnp.stack([coeffs[0], coeffs[1], coeffs[3], coeffs[5]])
    whole_pack = arrange(lax.all_gather(packed, ("gx", "gy"), axis=2, tiled=True), count_x, count_y)
    whole_source = arrange(
        lax.all_gather(source, ("gx", "gy"), axis=1, tiled=True), count_x, count_y
    )
    east = whole_pack[1]
    north = whole_pack[2]
    upward = whole_pack[3]
    edge_x = jnp.zeros((layers, 1, east.shape[2]), jnp.float32)
    edge_y = jnp.zeros((layers, east.shape[1], 1), jnp.float32)
    edge_z = jnp.zeros((1, east.shape[1], east.shape[2]), jnp.float32)
    west = jnp.concatenate([edge_x, east[:, :-1, :]], axis=1)
    south = jnp.concatenate([edge_y, north[:, :, :-1]], axis=2)
    downward = jnp.concatenate([edge_z, upward[:-1]], axis=0)
    whole_coeffs = (whole_pack[0], east, west, north, south, upward, downward)
    correction = cycle_whole(whole_source, whole_coeffs)
    return lax.dynamic_slice(
        correction, (jnp.int32(0), index_x * rows_x, index_y * rows_y), (layers, rows_x, rows_y)
    )


def cycle_spread(source, coeffs, level_index, split_level, index_x, index_y):
    layers, rows_x, rows_y = source.shape
    diagonal = diagonal_of(coeffs)
    colour = colours(source.shape, index_x * rows_x, index_y * rows_y)
    field, coarse_source = descend(source, coeffs, diagonal, colour, exchange_faces)
    coarse_coeffs = coarsen(coeffs)
    if level_index + 1 < split_level:
        correction = cycle_spread(
            coarse_source, coarse_coeffs, level_index + 1, split_level, index_x, index_y
        )
    else:
        correction = replicated(coarse_source, coarse_coeffs, index_x, index_y)
    return ascend(field, correction, source, coeffs, diagonal, colour, exchange_faces)


def shards(pressure, soil, vg_alpha, vg_n, sat_cond, storage, right_side):
    layers, rows_x, rows_y = pressure.shape
    index_x = lax.axis_index("gx")
    index_y = lax.axis_index("gy")
    count_x = lax.axis_size("gx")
    count_y = lax.axis_size("gy")
    cond = conductivity(pressure, soil, vg_alpha, vg_n, sat_cond)
    padded = with_halo(cond, (("gx", 1), ("gy", 2)), 1)
    global_x = lax.broadcasted_iota(jnp.int32, cond.shape, 1) + index_x * rows_x
    global_y = lax.broadcasted_iota(jnp.int32, cond.shape, 2) + index_y * rows_y
    east = jnp.where(global_x < count_x * rows_x - 1, 0.5 * (cond + padded[:, 2:, 1:-1]), 0.0)
    west = jnp.where(global_x > 0, 0.5 * (padded[:, :-2, 1:-1] + cond), 0.0)
    north = jnp.where(global_y < count_y * rows_y - 1, 0.5 * (cond + padded[:, 1:-1, 2:]), 0.0)
    south = jnp.where(global_y > 0, 0.5 * (padded[:, 1:-1, :-2] + cond), 0.0)
    face_z = WEIGHT_Z * (0.5 * (cond[:-1] + cond[1:]))
    edge_z = jnp.zeros((1, rows_x, rows_y), jnp.float32)
    upward = jnp.concatenate([face_z, edge_z], axis=0)
    downward = jnp.concatenate([edge_z, face_z], axis=0)
    coeffs = (storage, east, west, north, south, upward, downward)
    split_level = 3
    precond = cycle_spread(right_side, coeffs, 0, split_level, index_x, index_y)
    diagonal = diagonal_of(coeffs)
    total_cells = float(layers * rows_x * rows_y * count_x * count_y)
    residual_precond = lax.psum(jnp.sum(right_side * precond), ("gx", "gy"))
    image = apply_operator(precond, coeffs, diagonal, exchange_faces)
    curvature = lax.psum(jnp.sum(precond * image), ("gx", "gy"))
    step_length = residual_precond / curvature
    solution = step_length * precond
    new_residual = right_side - step_length * image
    squares = lax.psum(jnp.sum(new_residual * new_residual), ("gx", "gy"))
    residual_norm = jnp.sqrt(squares / total_cells).reshape(1)
    return (solution, new_residual, residual_norm)


def solution(mesh):
    placed = (
        P(None, "gx", "gy"),
        P(None, "gx", "gy"),
        P(),
        P(),
        P(),
        P(None, "gx", "gy"),
        P(None, "gx", "gy"),
    )
    return jax.shard_map(
        shards,
        mesh=mesh,
        in_specs=placed,
        out_specs=(P(None, "gx", "gy"), P(None, "gx", "gy"), P()),
        check_vma=False,
    )
```

profile of v0, /device:TPU:0, one launch (start us, length us, event | category | flops | bytes accessed | tf_op | source)
XLA Modules:
  0.0 690.6 jit_solution(14276992631541003813)
XLA Ops:
  10.4 5.5 collective-permute-start.29
  26.5 44.8 %multiply_multiply_fusion = f32[10,32,128]{2,1,0:T(8,128)S(1)} fusion(f32[10,32,128]{2,1,0:T(8,128)} %param.7, s32[10,32,128]{2,1,0:T(8,128)} %param.8, f32[]{:T(128)} %bitcast.68, f32[]{:T(128)} %bitcast.67, f32[]{:T(128)} %bitcast.66, f32[]{:T(128)} %bitcast.65, f32[]{:T(128)} %bitcast.64, f32[]{:T(128)} %bitcast.63, f32[]{:T(128)} %bitcast.62, ...), kind=kLoop, calls=%fused_computation.244 | loop fusion | flops 4300800 | bytes 491796 | tf_op jit(solution)/shard_map/mul | solution.py:44
  95.9 5.2 collective-permute-start.7
  138.2 5.2 collective-permute-start.11
  145.7 5.9 collective-permute-start.31
  161.3 5.2 collective-permute-start.15
  181.5 6.3 collective-permute-start.19
  205.2 5.4 collective-permute-start.23
  222.2 6.8 collective-permute-start.27
  238.3 4.4 collective-permute-done.32
  244.1 6.7 collective-permute-start.35
  261.8 7.0 %collective-permute-start.39 = (f32[10,10,1]{2,1,0:T(8,128)S(1)}, f32[10,10,1]{2,1,0:T(8,128)S(1)}, u32[]{:S(2)}, u32[]{:S(2)}) collective-permute-start(f32[10,10,1]{2,1,0:T(8,128)S(1)} %get-tuple-element.76), channel_id=1, source_target_pairs={{0,1},{1,2},{2,3},{3,4},{4,5},{5,6},{6,7},{7,8},{8,9},{9,10},{10,1... | collective-permute-start | bytes 1208 | tf_op jit(solution)/shard_map/ppermute | solution.py:20
  271.8 87.4 %all_gather.6 = f32[10,512,16]{2,0,1:T(8,128)} all-gather(f32[10,4,16]{2,0,1:T(8,128)S(1)} %copy.541), channel_id=1, replica_groups=mesh['gx'=8,'gy'=16] {'gx','gy'}, dimensions={1}, use_global_device_ids=true | all-gather | bytes 330240 | tf_op jit(solution)/shard_map/all_gather | solution.py:162
  367.7 6.0 copy.547
  373.9 5.0 fusion.413
  421.1 4.6 collective-permute-start.43
  435.8 4.9 collective-permute-start.47
  451.9 5.2 collective-permute-start.51
  469.3 5.2 collective-permute-start.55
  486.4 5.1 collective-permute-start.59
  504.7 6.8 collective-permute-start.63
  524.6 7.6 %collective-permute-start.67 = (f32[10,34,1]{2,1,0:T(8,128)S(1)}, f32[10,34,1]{2,1,0:T(8,128)S(1)}, u32[]{:S(2)}, u32[]{:S(2)}) collective-permute-start(f32[10,34,1]{2,1,0:T(8,128)S(1)} %get-tuple-element.32), channel_id=1, source_target_pairs={{0,1},{1,2},{2,3},{3,4},{4,5},{5,6},{6,7},{7,8},{8,9},{9,10},{10,1... | collective-permute-start | bytes 4088 | tf_op jit(solution)/shard_map/ppermute | solution.py:20
  536.8 77.3 %all-reduce.51 = (f32[]{:T(128)}, f32[]{:T(128)}) all-reduce(f32[]{:T(128)} %get-tuple-element.7, f32[]{:T(128)} %get-tuple-element.6), channel_id=1, replica_groups=mesh['gx'=8,'gy'=16] {'gx','gy'}, use_global_device_ids=true, to_apply=%region_24.25 | all-reduce | flops 2 | bytes 16 | tf_op jit(solution)/shard_map/psum | solution.py:218
  617.4 64.1 %psum.23 = f32[]{:T(128)} all-reduce(f32[]{:T(128)} %get-tuple-element.10), channel_id=1, replica_groups=mesh['gx'=8,'gy'=16] {'gx','gy'}, use_global_device_ids=true, to_apply=%region_28.29 | all-reduce | flops 1 | bytes 8 | tf_op jit(solution)/shard_map/psum | solution.py:224
  (497 shorter events, 281.4 us)
Async XLA Ops:
  7.2 360.5 %all-gather.2.cloned.1.call-start = ((), (), s32[]{:S(2)}) async-start(), calls=%async_computation | async-start | bytes 10567680 | tf_op jit(solution)/shard_map/all_gather | solution.py:160
  7.2 85.8 %collective-permute-start.3 = (f32[10,1,128]{2,1,0:T(1,128)S(1)}, f32[10,1,128]{2,1,0:T(1,128)S(1)}, u32[]{:S(2)}, u32[]{:S(2)}) collective-permute-start(f32[10,1,128]{2,1,0:T(1,128)S(1)} %broadcast.177), channel_id=1, source_target_pairs={{0,16},{16,32},{32,48},{48,64},{64,80},{80,96},{96,112},{1,17},{17... | collective-permute-start | bytes 15368 | tf_op jit(solution)/shard_map/ppermute | solution.py:20
  8.5 84.5 %collective-permute-start.1 = (f32[10,1,128]{2,1,0:T(1,128)S(1)}, f32[10,1,128]{2,1,0:T(1,128)S(1)}, u32[]{:S(2)}, u32[]{:S(2)}) collective-permute-start(f32[10,1,128]{2,1,0:T(1,128)S(1)} %broadcast.177), channel_id=1, source_target_pairs={{16,0},{32,16},{48,32},{64,48},{80,64},{96,80},{112,96},{17,1},{33... | collective-permute-start | bytes 15368 | tf_op jit(solution)/shard_map/ppermute | solution.py:21
  10.4 122.1 %collective-permute-start.29 = (f32[10,1,32]{2,1,0:T(1,128)}, f32[10,1,32]{2,1,0:T(1,128)}, u32[]{:S(2)}, u32[]{:S(2)}) collective-permute-start(f32[10,1,32]{2,1,0:T(1,128)} %broadcast.181), channel_id=1, source_target_pairs={{0,16},{16,32},{32,48},{48,64},{64,80},{80,96},{96,112},{1,17},{17... | collective-permute-start | bytes 3848 | tf_op jit(solution)/shard_map/ppermute | solution.py:20
  71.3 20.8 %collective-permute-start.2 = (f32[10,1,128]{2,1,0:T(1,128)S(1)}, f32[10,1,128]{2,1,0:T(1,128)S(1)}, u32[]{:S(2)}, u32[]{:S(2)}) collective-permute-start(f32[10,1,128]{2,1,0:T(1,128)S(1)} %get-tuple-element.55), channel_id=1, source_target_pairs={{0,16},{16,32},{32,48},{48,64},{64,80},{80,96},{96,112},{1,17},{17... | collective-permute-start | bytes 15368 | tf_op jit(solution)/shard_map/ppermute | solution.py:20
  74.4 17.7 %collective-permute-start = (f32[10,1,128]{2,1,0:T(1,128)S(1)}, f32[10,1,128]{2,1,0:T(1,128)S(1)}, u32[]{:S(2)}, u32[]{:S(2)}) collective-permute-start(f32[10,1,128]{2,1,0:T(1,128)S(1)} %get-tuple-element.56), channel_id=1, source_target_pairs={{16,0},{32,16},{48,32},{64,48},{80,64},{96,80},{112,96},{17,1},{33... | collective-permute-start | bytes 15368 | tf_op jit(solution)/shard_map/ppermute | solution.py:21
  94.6 25.9 %collective-permute-start.5 = (f32[10,34,1]{2,1,0:T(8,128)}, f32[10,34,1]{2,1,0:T(8,128)}, u32[]{:S(2)}, u32[]{:S(2)}) collective-permute-start(f32[10,34,1]{2,1,0:T(8,128)} %get-tuple-element.43), channel_id=1, source_target_pairs={{1,0},{2,1},{3,2},{4,3},{5,4},{6,5},{7,6},{8,7},{9,8},{10,9},{11,1... | collective-permute-start | bytes 4088 | tf_op jit(solution)/shard_map/ppermute | solution.py:21
  95.9 25.9 %collective-permute-start.7 = (f32[10,34,1]{2,1,0:T(8,128)}, f32[10,34,1]{2,1,0:T(8,128)}, u32[]{:S(2)}, u32[]{:S(2)}) collective-permute-start(f32[10,34,1]{2,1,0:T(8,128)} %get-tuple-element.44), channel_id=1, source_target_pairs={{0,1},{1,2},{2,3},{3,4},{4,5},{5,6},{6,7},{7,8},{8,9},{9,10},{10,1... | collective-permute-start | bytes 4088 | tf_op jit(solution)/shard_map/ppermute | solution.py:20
  101.1 23.7 %collective-permute-start.6 = (f32[10,34,1]{2,1,0:T(8,128)}, f32[10,34,1]{2,1,0:T(8,128)}, u32[]{:S(2)}, u32[]{:S(2)}) collective-permute-start(f32[10,34,1]{2,1,0:T(8,128)} %get-tuple-element.41), channel_id=1, source_target_pairs={{0,1},{1,2},{2,3},{3,4},{4,5},{5,6},{6,7},{7,8},{8,9},{9,10},{10,1... | collective-permute-start | bytes 4088 | tf_op jit(solution)/shard_map/ppermute | solution.py:20
  104.9 21.2 %collective-permute-start.4 = (f32[10,34,1]{2,1,0:T(8,128)}, f32[10,34,1]{2,1,0:T(8,128)}, u32[]{:S(2)}, u32[]{:S(2)}) collective-permute-start(f32[10,34,1]{2,1,0:T(8,128)} %get-tuple-element.42), channel_id=1, source_target_pairs={{1,0},{2,1},{3,2},{4,3},{5,4},{6,5},{7,6},{8,7},{9,8},{10,9},{11,1... | collective-permute-start | bytes 4088 | tf_op jit(solution)/shard_map/ppermute | solution.py:21
  120.5 13.3 %collective-permute-start.28 = (f32[10,1,32]{2,1,0:T(1,128)}, f32[10,1,32]{2,1,0:T(1,128)S(1)}, u32[]{:S(2)}, u32[]{:S(2)}) collective-permute-start(f32[10,1,32]{2,1,0:T(1,128)} %broadcast.181), channel_id=1, source_target_pairs={{16,0},{32,16},{48,32},{64,48},{80,64},{96,80},{112,96},{17,1},{33... | collective-permute-start | bytes 3848 | tf_op jit(solution)/shard_map/ppermute | solution.py:21
  121.8 33.9 %collective-permute-start.17 = (f32[10,1,64]{2,1,0:T(1,128)S(1)}, f32[10,1,64]{2,1,0:T(1,128)S(1)}, u32[]{:S(2)}, u32[]{:S(2)}) collective-permute-start(f32[10,1,64]{2,1,0:T(1,128)S(1)} %broadcast.179), channel_id=1, source_target_pairs={{0,16},{16,32},{32,48},{48,64},{64,80},{80,96},{96,112},{1,17},{17... | collective-permute-start | bytes 7688 | tf_op jit(solution)/shard_map/ppermute | solution.py:20
  124.8 32.2 %collective-permute-start.16 = (f32[10,1,64]{2,1,0:T(1,128)S(1)}, f32[10,1,64]{2,1,0:T(1,128)S(1)}, u32[]{:S(2)}, u32[]{:S(2)}) collective-permute-start(f32[10,1,64]{2,1,0:T(1,128)S(1)} %broadcast.179), channel_id=1, source_target_pairs={{16,0},{32,16},{48,32},{64,48},{80,64},{96,80},{112,96},{17,1},{33... | collective-permute-start | bytes 7688 | tf_op jit(solution)/shard_map/ppermute | solution.py:21
  138.2 13.4 %collective-permute-start.11 = (f32[10,34,1]{2,1,0:T(8,128)S(1)}, f32[10,34,1]{2,1,0:T(8,128)S(1)}, u32[]{:S(2)}, u32[]{:S(2)}) collective-permute-start(f32[10,34,1]{2,1,0:T(8,128)S(1)} %get-tuple-element.40), channel_id=1, source_target_pairs={{0,1},{1,2},{2,3},{3,4},{4,5},{5,6},{6,7},{7,8},{8,9},{9,10},{10,1... | collective-permute-start | bytes 4088 | tf_op jit(solution)/shard_map/ppermute | solution.py:20
  144.2 88.1 %collective-permute-start.30 = (f32[10,10,1]{2,1,0:T(8,128)}, f32[10,10,1]{2,1,0:T(8,128)}, u32[]{:S(2)}, u32[]{:S(2)}) collective-permute-start(f32[10,10,1]{2,1,0:T(8,128)} %get-tuple-element.79), channel_id=1, source_target_pairs={{1,0},{2,1},{3,2},{4,3},{5,4},{6,5},{7,6},{8,7},{9,8},{10,9},{11,1... | collective-permute-start | bytes 1208 | tf_op jit(solution)/shard_map/ppermute | solution.py:21
  145.7 86.6 %collective-permute-start.31 = (f32[10,10,1]{2,1,0:T(8,128)}, f32[10,10,1]{2,1,0:T(8,128)}, u32[]{:S(2)}, u32[]{:S(2)}) collective-permute-start(f32[10,10,1]{2,1,0:T(8,128)} %get-tuple-element.80), channel_id=1, source_target_pairs={{0,1},{1,2},{2,3},{3,4},{4,5},{5,6},{6,7},{7,8},{8,9},{9,10},{10,1... | collective-permute-start | bytes 1208 | tf_op jit(solution)/shard_map/ppermute | solution.py:20
  160.0 21.4 %collective-permute-start.14 = (f32[10,34,1]{2,1,0:T(8,128)}, f32[10,34,1]{2,1,0:T(8,128)}, u32[]{:S(2)}, u32[]{:S(2)}) collective-permute-start(f32[10,34,1]{2,1,0:T(8,128)} %get-tuple-element.37), channel_id=1, source_target_pairs={{1,0},{2,1},{3,2},{4,3},{5,4},{6,5},{7,6},{8,7},{9,8},{10,9},{11,1... | collective-permute-start | bytes 4088 | tf_op jit(solution)/shard_map/ppermute | solution.py:21
  161.3 26.5 %collective-permute-start.15 = (f32[10,34,1]{2,1,0:T(8,128)S(1)}, f32[10,34,1]{2,1,0:T(8,128)}, u32[]{:S(2)}, u32[]{:S(2)}) collective-permute-start(f32[10,34,1]{2,1,0:T(8,128)S(1)} %get-tuple-element.38), channel_id=1, source_target_pairs={{0,1},{1,2},{2,3},{3,4},{4,5},{5,6},{6,7},{7,8},{8,9},{9,10},{10,1... | collective-permute-start | bytes 4088 | tf_op jit(solution)/shard_map/ppermute | solution.py:20
  167.3 28.3 %collective-permute-start.18 = (f32[10,18,1]{2,1,0:T(8,128)}, f32[10,18,1]{2,1,0:T(8,128)}, u32[]{:S(2)}, u32[]{:S(2)}) collective-permute-start(f32[10,18,1]{2,1,0:T(8,128)} %get-tuple-element.65), channel_id=1, source_target_pairs={{1,0},{2,1},{3,2},{4,3},{5,4},{6,5},{7,6},{8,7},{9,8},{10,9},{11,1... | collective-permute-start | bytes 2168 | tf_op jit(solution)/shard_map/ppermute | solution.py:21
  181.5 14.2 %collective-permute-start.19 = (f32[10,18,1]{2,1,0:T(8,128)}, f32[10,18,1]{2,1,0:T(8,128)}, u32[]{:S(2)}, u32[]{:S(2)}) collective-permute-start(f32[10,18,1]{2,1,0:T(8,128)} %get-tuple-element.66), channel_id=1, source_target_pairs={{0,1},{1,2},{2,3},{3,4},{4,5},{5,6},{6,7},{7,8},{8,9},{9,10},{10,1... | collective-permute-start | bytes 2168 | tf_op jit(solution)/shard_map/ppermute | solution.py:20
  503.4 10.3 %collective-permute-start.62 = (f32[10,34,1]{2,1,0:T(8,128)S(1)}, f32[10,34,1]{2,1,0:T(8,128)S(1)}, u32[]{:S(2)}, u32[]{:S(2)}) collective-permute-start(f32[10,34,1]{2,1,0:T(8,128)S(1)} %get-tuple-element.33), channel_id=1, source_target_pairs={{1,0},{2,1},{3,2},{4,3},{5,4},{6,5},{7,6},{8,7},{9,8},{10,9},{11,1... | collective-permute-start | bytes 4088 | tf_op jit(solution)/shard_map/ppermute | solution.py:21
  504.7 10.8 %collective-permute-start.63 = (f32[10,34,1]{2,1,0:T(8,128)S(1)}, f32[10,34,1]{2,1,0:T(8,128)S(1)}, u32[]{:S(2)}, u32[]{:S(2)}) collective-permute-start(f32[10,34,1]{2,1,0:T(8,128)S(1)} %get-tuple-element.34), channel_id=1, source_target_pairs={{0,1},{1,2},{2,3},{3,4},{4,5},{5,6},{6,7},{7,8},{8,9},{9,10},{10,1... | collective-permute-start | bytes 4088 | tf_op jit(solution)/shard_map/ppermute | solution.py:20
  523.3 10.8 %collective-permute-start.66 = (f32[10,34,1]{2,1,0:T(8,128)S(1)}, f32[10,34,1]{2,1,0:T(8,128)S(1)}, u32[]{:S(2)}, u32[]{:S(2)}) collective-permute-start(f32[10,34,1]{2,1,0:T(8,128)S(1)} %get-tuple-element.31), channel_id=1, source_target_pairs={{1,0},{2,1},{3,2},{4,3},{5,4},{6,5},{7,6},{8,7},{9,8},{10,9},{11,1... | collective-permute-start | bytes 4088 | tf_op jit(solution)/shard_map/ppermute | solution.py:21
  524.6 11.3 %collective-permute-start.67 = (f32[10,34,1]{2,1,0:T(8,128)S(1)}, f32[10,34,1]{2,1,0:T(8,128)S(1)}, u32[]{:S(2)}, u32[]{:S(2)}) collective-permute-start(f32[10,34,1]{2,1,0:T(8,128)S(1)} %get-tuple-element.32), channel_id=1, source_target_pairs={{0,1},{1,2},{2,3},{3,4},{4,5},{5,6},{6,7},{7,8},{8,9},{9,10},{10,1... | collective-permute-start | bytes 4088 | tf_op jit(solution)/shard_map/ppermute | solution.py:20
  (138 other events, 2817.5 us)
Sparse Core Ops, SparseCore 0:
  220.7 85.0 all-gather.1
where the time goes:
time: 700 us; the launch traced here: 691 us
  blocking collectives  229 us (33%)
  starting transfers between devices  198 us (28%)
  other arithmetic  97.9 us (14%)
  local copies, waits for them, and re-layouts  88.5 us (13%)
  waiting for transfers between devices  55.6 us (8%)
  between operations  21.7 us (3%)
    ppermute x34, starting transfers between devices, with_halo(): before = lax.ppermute(last, axis, up)  154 us
    all_gather x1, blocking collectives, replicated(): lax.all_gather(source, ('gx', 'gy'), axis=1, tiled=True)  87.4 us
    psum x1, blocking collectives, shards(): residual_precond = lax.psum(jnp.sum(right_side * precond), ('gx', 'gy'))  77.3 us
    psum x1, blocking collectives, shards(): squares = lax.psum(jnp.sum(new_residual * new_residual), ('gx', 'gy'))  64.1 us
    mul x1, other arithmetic, conductivity(): return saturated * rooted * outer_term * outer_term  44.8 us
    ppermute x34, starting transfers between devices, with_halo(): after = lax.ppermute(first, axis, down)  44.5 us
    ppermute x34, waiting for transfers between devices, with_halo(): after = lax.ppermute(first, axis, down)  38 us
    ppermute x34, waiting for transfers between devices, with_halo(): before = lax.ppermute(last, axis, up)  17.6 us
  transfers between devices with their start and end apart: 69, of which 34 were waited for; matrix products, arithmetic and copies ran while one was open for 19% of the time, Pallas kernels for 0%

commit v1 on v0

v1 whole, which is shorter than its diff:
```python
import functools

import jax
import jax.numpy as jnp
from jax import lax
from jax.experimental import pallas as pl
from jax.experimental.pallas import tpu as pltpu
from jax.sharding import PartitionSpec as P

NSOIL = 23
PAIRS = 5
HALO = 24
ROWS, LANES = 32, 128
EXT = ROWS + 2 * HALO
WIDE = 2 * LANES
ROWS1, ROWS2 = 48, 24
TILES = 11
MIB = 1 << 20


def iota(shape, dim):
    return lax.broadcasted_iota(jnp.int32, shape, dim)


def odd_cells(shape, level, start=0):
    return ((iota(shape, 0) + start + (iota(shape, 1) >> level)) & 1) == 1


def lane_bit(shape, level):
    return ((iota(shape, 1) >> level) & 1) == 1


def row_next(x):
    return pltpu.roll(x, x.shape[0] - 1, 0)


def row_prev(x):
    return pltpu.roll(x, 1, 0)


def lane_next(x, step):
    return pltpu.roll(x, x.shape[1] - step, 1)


def lane_prev(x, step):
    return pltpu.roll(x, step, 1)


def pair_sum(x, level):
    step = 1 << level
    return x + jnp.where(lane_bit(x.shape, level), lane_prev(x, step), lane_next(x, step))


def beside(c, u, coeffs, m, odd, step):
    east, north, inner, outer = coeffs
    um = u[m]
    t = east[c, m] * row_next(um) + row_prev(east[1 - c, m] * um)
    t = t + (north[c, m] * lane_next(um, step) + lane_prev(north[1 - c, m] * um, step))
    t = t + inner[m] * um
    above = outer[m] * u[m + 1] if m < PAIRS - 1 else 0.0
    below = outer[m - 1] * u[m - 1] if m > 0 else 0.0
    return t + (jnp.where(odd, above, below) if c == 0 else jnp.where(odd, below, above))


def params(limit=32):
    return pltpu.CompilerParams(vmem_limit_bytes=limit * MIB)


VM = pl.BlockSpec(memory_space=pltpu.VMEM)
SM = pl.BlockSpec(memory_space=pltpu.SMEM)


def shape(*dims):
    return jax.ShapeDtypeStruct(dims, jnp.float32)


class Wide:
    def __init__(self, ref):
        self.ref, self.lead = ref, len(ref.shape) - 3

    def parts(self, ids):
        ids = ids if isinstance(ids, tuple) else (ids,)
        rows = ids[self.lead] if len(ids) > self.lead else slice(None)
        return [self.ref.at[(*ids[: self.lead], half)] for half in range(2)], rows

    def __getitem__(self, ids):
        refs, rows = self.parts(ids)
        return jnp.concatenate([ref[rows, :] for ref in refs], axis=1)

    def __setitem__(self, ids, x):
        refs, rows = self.parts(ids)
        for half, ref in enumerate(refs):
            ref[rows, :] = x[:, LANES * half : LANES * (half + 1)]


def first_kernel(place, pressure, soil, table, storage, source, packed, to_sibling, to_other):
    even = (place[0] & 1) == 0
    odd = odd_cells((ROWS, LANES), 0)
    rows = [jnp.broadcast_to(table[q : q + 1, :], (8, LANES)) for q in range(3)]

    def look_up(row, ids):
        parts = [jnp.take_along_axis(row, ids[8 * b : 8 * b + 8], axis=1) for b in range(ROWS // 8)]
        return jnp.concatenate(parts, axis=0)

    def cond_of(k):
        ids = soil[k]
        log_scale, power, saturated = [look_up(r, ids) for r in rows]
        exponent = 1.0 - 1.0 / power
        log_s = power * (log_scale + jnp.log(jnp.abs(pressure[k])))
        log_1s = jnp.log(1.0 + jnp.exp(log_s))
        outer = 1.0 - jnp.exp(exponent * (log_s - log_1s))
        return saturated * jnp.exp(-0.5 * exponent * log_1s) * outer * outer

    def put(t, x):
        packed[t] = x
        high, low = x[ROWS - HALO :], x[:HALO]
        to_sibling[t] = jnp.where(even, high, low)
        to_other[t] = jnp.where(even, low, high)

    for m in range(PAIRS):
        triples = (
            (cond_of(2 * m), cond_of(2 * m + 1)),
            (storage[2 * m], storage[2 * m + 1]),
            (source[2 * m], source[2 * m + 1]),
        )
        for q, (a, b) in enumerate(triples):
            put(q * 10 + m, jnp.where(odd, b, a))
            put(q * 10 + PAIRS + m, jnp.where(odd, a, b))


def second_kernel(place, packed, from_sibling, from_other, to_pair, to_next):
    even_x = (place[0] & 1) == 0
    even_y = (place[1] & 1) == 0
    lane = iota((EXT, LANES), 1)
    for tile in range(6):
        pair, other = None, None
        for m in range(PAIRS):
            t = tile * PAIRS + m
            sib, oth = from_sibling[t], from_other[t]
            x = jnp.concatenate([jnp.where(even_x, oth, sib), packed[t], jnp.where(even_x, sib, oth)], axis=0)
            left = pltpu.roll(x, HALO * m, 1) if m else x
            right = pltpu.roll(x, (HALO * m - (LANES - HALO)) % LANES, 1)
            a, b = jnp.where(even_y, right, left), jnp.where(even_y, left, right)
            pair = a if pair is None else jnp.where(lane >= HALO * m, a, pair)
            other = b if other is None else jnp.where(lane >= HALO * m, b, other)
        to_pair[tile] = pair
        to_next[tile] = other


def coarsen_level(level, fine_rows, out_rows, fine, coarse):
    stor, east, north, inner, outer = fine
    cstor, ceast, cnorth, cinner, couter = coarse
    half = fine_rows // 2
    dims = (half, WIDE)
    bit = lane_bit(dims, level)
    odd = odd_cells(dims, level + 1, 1 if level == 2 else 0)
    step = 1 << level

    def even_rows(ref, *ids):
        return ref[(*ids, pl.ds(0, half, stride=2))]

    def odd_rows(ref, *ids):
        return ref[(*ids, pl.ds(1, half, stride=2))]

    def put(ref, m, low, high):
        ref[0, m, slice(0, half)] = jnp.where(odd, high, low)
        ref[1, m, slice(0, half)] = jnp.where(odd, low, high)

    for m in range(PAIRS):
        u = even_rows(stor, 0, m) + odd_rows(stor, 1, m)
        v = even_rows(stor, 1, m) + odd_rows(stor, 0, m)
        put(cstor, m, pair_sum(jnp.where(bit, v, u), level), pair_sum(jnp.where(bit, u, v), level))
        e0, e1 = odd_rows(east, 0, m), odd_rows(east, 1, m)
        put(ceast, m, pair_sum(jnp.where(bit, e0, e1), level), pair_sum(jnp.where(bit, e1, e0), level))
        low = even_rows(north, 1, m) + odd_rows(north, 0, m)
        high = even_rows(north, 0, m) + odd_rows(north, 1, m)
        put(
            cnorth,
            m,
            jnp.where(bit, low, lane_next(low, step)),
            jnp.where(bit, high, lane_next(high, step)),
        )
        cinner[m, slice(0, half)] = pair_sum(even_rows(inner, m) + odd_rows(inner, m), level)
        if m < PAIRS - 1:
            couter[m, slice(0, half)] = pair_sum(even_rows(outer, m) + odd_rows(outer, m), level)


def restrict_level(level, fine_rows, residual, coarse_source):
    half = fine_rows // 2
    dims = (half, WIDE)
    bit = lane_bit(dims, level)
    odd = odd_cells(dims, level + 1, 1 if level == 2 else 0)
    for m in range(PAIRS):
        a = residual[m, pl.ds(0, half, stride=2)]
        b = residual[m, pl.ds(1, half, stride=2)]
        low = pair_sum(jnp.where(bit, b, a), level)
        high = pair_sum(jnp.where(bit, a, b), level)
        coarse_source[0, m, slice(0, half)] = jnp.where(odd, high, low)
        coarse_source[1, m, slice(0, half)] = jnp.where(odd, low, high)


def invert_diagonal(level, rows, coeffs, inverse):
    stor, east, north, inner, outer = coeffs
    odd = odd_cells((rows, WIDE), level)
    step = 1 << level
    for m in range(PAIRS):
        above = outer[m] if m < PAIRS - 1 else 0.0
        below = outer[m - 1] if m > 0 else 0.0
        for c in range(2):
            diag = stor[c, m] + east[c, m] + row_prev(east[1 - c, m]) + north[c, m]
            diag = diag + lane_prev(north[1 - c, m], step) + inner[m]
            diag = diag + (jnp.where(odd, above, below) if c == 0 else jnp.where(odd, below, above))
            inverse[c, m] = 1.0 / diag


def descend_level(level, rows, coeffs, inverse, source, first, second, residual):
    odd = odd_cells((rows, WIDE), level)
    step = 1 << level
    for m in range(PAIRS):
        first[m] = source[0, m] * inverse[0, m]
    for m in range(PAIRS):
        second[m] = (source[1, m] + beside(1, first, coeffs[1:], m, odd, step)) * inverse[1, m]
    for m in range(PAIRS):
        residual[m] = beside(0, second, coeffs[1:], m, odd, step)


def third_kernel(
    place, packed, from_sibling, from_other, from_pair, from_next,
    source0, inv0, first0, east0, north0, inner0, outer0,
    source1, inv1, first1, east1, north1, inner1, outer1,
    source2, inv2, first2, east2, north2, inner2, outer2,
    tiles, sums,
    cond, stor, src, east, north, inner, outer, inv, first, second, residual,
    stor1, src1, e1, n1, in1, out1, i1, f1, s1, r1,
    stor2, s2, r2,
    stor3, src3, e3, n3, in3, out3,
):
    source0, inv0, first0, east0, north0, inner0, outer0 = map(Wide, (source0, inv0, first0, east0, north0, inner0, outer0))
    source1, inv1, first1, east1, north1, inner1, outer1 = map(Wide, (source1, inv1, first1, east1, north1, inner1, outer1))
    source2, inv2, first2, east2, north2, inner2, outer2 = map(Wide, (source2, inv2, first2, east2, north2, inner2, outer2))
    cond, stor, src, east, north, inner, outer = map(Wide, (cond, stor, src, east, north, inner, outer))
    inv, first, second, residual = map(Wide, (inv, first, second, residual))
    stor1, src1, e1, n1, in1, out1, i1, f1, s1, r1 = map(Wide, (stor1, src1, e1, n1, in1, out1, i1, f1, s1, r1))
    stor2, s2, r2 = map(Wide, (stor2, s2, r2))
    stor3, src3, e3, n3, in3, out3 = map(Wide, (stor3, src3, e3, n3, in3, out3))
    even_x = (place[0] & 1) == 0
    even_y = (place[1] & 1) == 0
    lane = iota((EXT, LANES), 1)
    for tile in range(6):
        pair, other = from_pair[tile], from_next[tile]
        right = jnp.where(even_y, pair, other)
        left = jnp.where(even_y, other, pair)
        ref = (cond, stor, src)[tile // 2]
        for m in range(PAIRS):
            t = tile * PAIRS + m
            sib, oth = from_sibling[t], from_other[t]
            x = jnp.concatenate([jnp.where(even_x, oth, sib), packed[t], jnp.where(even_x, sib, oth)], axis=0)
            r = pltpu.roll(right, (-HALO * m) % LANES, 1) if m else right
            l = pltpu.roll(left, (LANES - HALO - HALO * m) % LANES, 1)
            h = jnp.where(lane < HALO, r, jnp.where(lane >= LANES - HALO, l, 0.0))
            if tile // 2 == 1:
                x, h = jnp.where(x == 0.0, 1.0, x), jnp.where(h == 0.0, 1.0, h)
            ref.ref[tile % 2, m, 0] = x
            ref.ref[tile % 2, m, 1] = h

    dims = (EXT, WIDE)
    odd = odd_cells(dims, 0)
    row, column = iota(dims, 0), iota(dims, 1)
    last_row = (row == HALO + ROWS - 1) & (place[0] == place[2] - 1)
    before_row = (row == HALO - 1) & (place[0] == 0)
    keep_x = jnp.where(last_row | before_row, 0.0, 0.5)
    last_column = (column == LANES - 1) & (place[1] == place[3] - 1)
    before_column = (column == WIDE - 1) & (place[1] == 0)
    keep_y = jnp.where(last_column | before_column, 0.0, 0.5)
    for m in range(PAIRS):
        a, b = cond[0, m], cond[1, m]
        east[0, m] = (a + row_next(b)) * keep_x
        east[1, m] = (b + row_next(a)) * keep_x
        north[0, m] = (a + lane_next(b, 1)) * keep_y
        north[1, m] = (b + lane_next(a, 1)) * keep_y
        inner[m] = a + b
        if m < PAIRS - 1:
            outer[m] = jnp.where(odd, a + cond[1, m + 1], b + cond[0, m + 1])

    level0 = (stor, east, north, inner, outer)
    level1 = (stor1, e1, n1, in1, out1)
    level2 = (stor2, east2, north2, inner2, outer2)
    level3 = (stor3, e3, n3, in3, out3)
    invert_diagonal(0, EXT, level0, inv)
    descend_level(0, EXT, level0, inv, src, first, second, residual)

    half = EXT // 2
    for ref in (src1, e1, n1, in1, out1):
        ref.ref[..., half:, :] = jnp.zeros((*ref.ref.shape[:-2], ROWS1 - half, LANES), jnp.float32)
    stor1.ref[..., half:, :] = jnp.ones((2, PAIRS, 2, ROWS1 - half, LANES), jnp.float32)
    coarsen_level(0, EXT, ROWS1, level0, level1)
    restrict_level(0, EXT, residual, src1)
    invert_diagonal(1, ROWS1, level1, i1)
    descend_level(1, ROWS1, level1, i1, src1, f1, s1, r1)

    coarsen_level(1, ROWS1, ROWS2, level1, level2)
    restrict_level(1, ROWS1, r1, source2)
    invert_diagonal(2, ROWS2, level2, inv2)
    descend_level(2, ROWS2, level2, inv2, source2, first2, s2, r2)

    coarsen_level(2, ROWS2, 16, level2, level3)
    restrict_level(2, ROWS2, r2, src3)

    dims3 = (16, WIDE)
    odd3 = odd_cells(dims3, 3, 1)
    phase = iota((4, LANES), 1) & 7
    total_f, total_s = 0.0, 0.0
    compact = [None] * TILES
    for m in range(PAIRS):
        above = out3[m] if m < PAIRS - 1 else 0.0
        below = out3[m - 1] if m > 0 else 0.0
        invs = []
        for c in range(2):
            diag = stor3[c, m] + e3[c, m] + row_prev(e3[1 - c, m]) + n3[c, m]
            diag = diag + lane_prev(n3[1 - c, m], 8) + in3[m]
            diag = diag + (jnp.where(odd3, above, below) if c == 0 else jnp.where(odd3, below, above))
            invs.append(1.0 / diag)
            total_f = total_f + src3[c, m][3:7, :LANES]
            total_s = total_s + stor3[c, m][3:7, :LANES]
        values = (
            src3[0, m] * invs[0], src3[1, m] * invs[1], 1.0 - stor3[0, m] * invs[0], invs[0], invs[1],
            e3[0, m], e3[1, m], n3[0, m], n3[1, m], in3[m], out3[m] if m < PAIRS - 1 else jnp.zeros(dims3, jnp.float32),
        )
        for q, value in enumerate(values):
            own = value[3:7, :LANES]
            compact[q] = jnp.where(phase == m, own, 0.0 if m == 0 else compact[q])
    for q in range(TILES):
        tiles[4 * q : 4 * q + 4] = compact[q]
    sums[0:1] = jnp.broadcast_to(jnp.sum(total_f, keepdims=True), (1, LANES)) * 0.125
    sums[1:2] = jnp.broadcast_to(jnp.sum(total_s, keepdims=True), (1, LANES)) * 0.125

    for m in range(PAIRS):
        for c in range(2):
            for to, of in ((source0, src), (inv0, inv), (east0, east), (north0, north)):
                to[c, m] = of[c, m, slice(16, 64)]
            for to, of in ((source1, src1), (inv1, i1), (east1, e1), (north1, n1)):
                to[c, m] = of[c, m, slice(8, 32)]
        first0[m], first1[m] = first[m, slice(16, 64)], f1[m, slice(8, 32)]
        inner0[m], inner1[m] = inner[m, slice(16, 64)], in1[m, slice(8, 32)]
        if m < PAIRS - 1:
            outer0[m], outer1[m] = outer[m, slice(16, 64)], out1[m, slice(8, 32)]


def spread_rows(level, low, high, into, m):
    rows = low.shape[0]
    bit = lane_bit(low.shape, level)
    into[m, pl.ds(0, rows, stride=2)] = jnp.where(bit, high, low)
    into[m, pl.ds(1, rows, stride=2)] = jnp.where(bit, low, high)


def fourth_kernel(
    place, gathered, sums_in,
    source0, inv0, first0, east0, north0, inner0, outer0,
    source1, inv1, first1, east1, north1, inner1, outer1,
    source2, inv2, first2, east2, north2, inner2, outer2,
    fields, sums,
    whole, work2, work1, work0a, work0b, va, vb, wa, wb,
    ua2, ub2, ua1, ub1,
):
    source0, inv0, first0, east0, north0, inner0, outer0 = map(Wide, (source0, inv0, first0, east0, north0, inner0, outer0))
    source1, inv1, first1, east1, north1, inner1, outer1 = map(Wide, (source1, inv1, first1, east1, north1, inner1, outer1))
    source2, inv2, first2, east2, north2, inner2, outer2 = map(Wide, (source2, inv2, first2, east2, north2, inner2, outer2))
    work2, work1, work0a, work0b, va, vb, wa, wb = map(Wide, (work2, work1, work0a, work0b, va, vb, wa, wb))
    ua2, ub2, ua1, ub1 = map(Wide, (ua2, ub2, ua1, ub1))
    f32 = jnp.float32
    for q in range(TILES):
        for g in range(8):
            whole[q, 4 * g : 4 * g + 4] = gathered[g, 4 * q : 4 * q + 4]
    own_f, own_s = sums_in[0:1, 0:1], sums_in[1:2, 0:1]
    guess = own_f / own_s
    g0, g1, h0, i30, i31, e30, e31, n30, n31, in3, out3 = [whole[q] for q in range(TILES)]
    inv3, e3, n3 = (i30, i31), (e30, e31), (n30, n31)
    odd3 = odd_cells((ROWS, WIDE), 3)

    def beside3(c, u):
        t = e3[c] * row_next(u) + row_prev(e3[1 - c] * u)
        t = t + (n3[c] * lane_next(u, 8) + lane_prev(n3[1 - c] * u, 8)) + in3 * u
        above, below = out3 * lane_next(u, 1), lane_prev(out3 * u, 1)
        return t + (jnp.where(odd3, above, below) if c == 0 else jnp.where(odd3, below, above))

    a0, b0 = g0 + guess * h0, h0
    for _ in range(3):
        a1, b1 = g1 + beside3(1, a0) * inv3[1], beside3(1, b0) * inv3[1]
        a0, b0 = g0 + beside3(0, a1) * inv3[0], beside3(0, b1) * inv3[0]

    shift = lax.rem(35 - 4 * place[0], 32)
    a0, a1, b0, b1 = [pltpu.roll(x, shift, 0)[:16] for x in (a0, a1, b0, b1)]
    dims3 = (16, WIDE)
    phase = iota(dims3, 1) & 7
    odd3 = odd_cells(dims3, 3, 1)
    second_half = lane_bit(dims3, 1)

    def spread(x, m):
        x = jnp.where(phase == 0, lane_next(x, m) if m else x, 0.0)
        x = x + lane_prev(x, 1)
        x = x + lane_prev(x, 2)
        return x + lane_prev(x, 4)

    for m in range(PAIRS):
        x0 = jnp.where(second_half, spread(b0, m), spread(a0, m))
        x1 = jnp.where(second_half, spread(b1, m), spread(a1, m))
        low, high = jnp.where(odd3, x1, x0)[:12], jnp.where(odd3, x0, x1)[:12]
        spread_rows(2, low, high, work2, m)

    def smooth(level, rows, coeffs, inverse, source, first, work, ones, zeros, half_bit):
        odd = odd_cells((rows, WIDE), level)
        is_b = lane_bit((rows, WIDE), half_bit)
        step = 1 << level
        for m in range(PAIRS):
            work[m] = work[m] + jnp.where(is_b, 0.0, first[m])
        for m in range(PAIRS):
            ones[m] = (jnp.where(is_b, 0.0, source[1, m]) + beside(1, work, coeffs, m, odd, step)) * inverse[1, m]
        for m in range(PAIRS):
            zeros[m] = jnp.where(is_b, 0.0, first[m]) + beside(0, ones, coeffs, m, odd, step) * inverse[0, m]

    smooth(2, ROWS2, (east2, north2, inner2, outer2), inv2, source2, first2, work2, ub2, ua2, 1)
    dims2 = (ROWS2, WIDE)
    odd2 = odd_cells(dims2, 2)
    bit1, bit0 = lane_bit(dims2, 1), lane_bit(dims2, 0)

    def regroup2(x):
        a = jnp.where(bit1, lane_prev(x, 2), x)
        b = jnp.where(bit1, x, lane_next(x, 2))
        return jnp.where(bit0, b, a)

    for m in range(PAIRS):
        x0, x1 = regroup2(ua2[m]), regroup2(ub2[m])
        low, high = jnp.where(odd2, x1, x0)[4:16], jnp.where(odd2, x0, x1)[4:16]
        spread_rows(1, low, high, work1, m)

    smooth(1, 24, (east1, north1, inner1, outer1), inv1, source1, first1, work1, ub1, ua1, 0)
    dims1 = (24, WIDE)
    odd1 = odd_cells(dims1, 1)
    bit0 = lane_bit(dims1, 0)
    for m in range(PAIRS):
        x0, x1 = ua1[m], ub1[m]
        low, high = jnp.where(odd1, x1, x0), jnp.where(odd1, x0, x1)
        for work, pick in (
            (work0a, lambda x: jnp.where(bit0, lane_prev(x, 1), x)),
            (work0b, lambda x: jnp.where(bit0, x, lane_next(x, 1))),
        ):
            spread_rows(0, pick(low), pick(high), work, m)

    rows = 48
    odd = odd_cells((rows, WIDE), 0)
    coeffs = (east0, north0, inner0, outer0)
    for m in range(PAIRS):
        work0a[m] = work0a[m] + first0[m]
    for m in range(PAIRS):
        va[m] = (source0[1, m] + beside(1, work0a, coeffs, m, odd, 1)) * inv0[1, m]
        vb[m] = beside(1, work0b, coeffs, m, odd, 1) * inv0[1, m]
    for m in range(PAIRS):
        wa[m] = first0[m] + beside(0, va, coeffs, m, odd, 1) * inv0[0, m]
        wb[m] = beside(0, vb, coeffs, m, odd, 1) * inv0[0, m]
    for m in range(PAIRS):
        work0a[m] = work0a[m] - wa[m]
        work0b[m] = work0b[m] - wb[m]
    acc = [jnp.zeros((ROWS, LANES), f32)] * 11

    def own(x):
        return x[8 : 8 + ROWS, :LANES]

    for m in range(PAIRS):
        change_a = own(beside(1, work0a, coeffs, m, odd, 1))
        img_b = own(beside(1, work0b, coeffs, m, odd, 1))
        r0, r1 = own(source0[0, m]), own(source0[1, m])
        p0, p1, q0, q1 = own(wa[m]), own(va[m]), own(wb[m]), own(vb[m])
        img_a = r1 + change_a
        d = -change_a
        terms = (
            r0 * p0 + r1 * p1, r0 * q0 + r1 * q1,
            r0 * p0 + img_a * p1, r0 * q0 + img_a * q1 + img_b * p1, img_b * q1,
            d * d, d * img_a, img_a * img_a + r0 * r0, d * img_b, img_a * img_b, img_b * img_b,
        )
        acc = [x + y for x, y in zip(acc, terms, strict=True)]
        for t, x in enumerate((p0, p1, q0, q1, r0, r1, img_a, img_b)):
            fields[t, m] = x
    lane = iota((1, 16), 1)
    line = jnp.zeros((1, 16), f32)
    for q, x in enumerate(acc):
        line = jnp.where(lane == q, jnp.sum(x, keepdims=True), line)
    line = jnp.where(lane == 11, own_f, line)
    line = jnp.where(lane == 12, own_s, line)
    line = jnp.where(lane == 13, guess, line)
    sums[...] = jnp.broadcast_to(line, sums.shape)


def last_kernel(place, sums, fields, solution_ref, residual_ref, norm_ref, *, cells):
    x = sums[...]

    def column(q):
        return x[:, q : q + 1]

    def total(v):
        return jnp.sum(v, axis=0, keepdims=True)

    rp, rq, pa, pb, qb, dd, da, aa, db, ab, bb = [column(q) for q in range(11)]
    mean = total(column(11)) / total(column(12))
    shift = mean - column(13)
    step = total(rp + shift * rq) / total(pa + shift * (pb + shift * qb))
    s, t = step - 1.0, step * shift
    squares = total(dd - 2.0 * s * da + s * s * aa - 2.0 * t * db + 2.0 * s * t * ab + t * t * bb)
    norm_ref[...] = jnp.sqrt(jnp.maximum(squares, 0.0) / cells)
    mine = place[0] * place[3] + place[1]
    here = total(jnp.where(iota(shift.shape, 0) == mine, shift, 0.0))
    odd = odd_cells((ROWS, LANES), 0)
    for m in range(PAIRS):
        p0, p1, q0, q1, r0, r1, img_a, img_b = [fields[t, m] for t in range(8)]
        s0, s1 = step * (p0 + here * q0), step * (p1 + here * q1)
        n0, n1 = r0 - step * r0, r1 - step * (img_a + here * img_b)
        solution_ref[2 * m] = jnp.where(odd, s1, s0)
        solution_ref[2 * m + 1] = jnp.where(odd, s0, s1)
        residual_ref[2 * m] = jnp.where(odd, n1, n0)
        residual_ref[2 * m + 1] = jnp.where(odd, n0, n1)


def level_dims(rows):
    two, one, four = [(*lead, 2, rows, LANES) for lead in ((2, PAIRS), (PAIRS,), (PAIRS - 1,))]
    return two, one, four


def level_shapes(rows):
    two, one, four = [shape(*dims) for dims in level_dims(rows)]
    return two, two, one, two, two, one, four


def scratch(*dims):
    return pltpu.VMEM(dims, jnp.float32)


def pairs_of(count, first):
    return [(i, i + 1) for i in range(first, count - 1, 2)] + [(i + 1, i) for i in range(first, count - 1, 2)]


def shards(pressure, soil, vg_alpha, vg_n, sat_cond, storage, right_side):
    count_x, count_y = lax.axis_size("gx"), lax.axis_size("gy")
    index_x, index_y = lax.axis_index("gx"), lax.axis_index("gy")
    place = jnp.stack([index_x, index_y, jnp.int32(count_x), jnp.int32(count_y)])
    table = jnp.stack([jnp.log(vg_alpha), vg_n, sat_cond])
    table = jnp.pad(table, ((0, 5), (0, LANES - NSOIL)), constant_values=1.0)

    slab = shape(6 * PAIRS, HALO, LANES)
    packed, to_sibling, to_other = pl.pallas_call(
        first_kernel, out_shape=(shape(6 * PAIRS, ROWS, LANES), slab, slab),
        in_specs=[SM, VM, VM, VM, VM, VM], out_specs=(VM, VM, VM), compiler_params=params(16), name="conductivity",
    )(place, pressure, soil, table, storage, right_side)
    from_sibling = lax.ppermute(to_sibling, "gx", pairs_of(count_x, 0))
    from_other = lax.ppermute(to_other, "gx", pairs_of(count_x, 1))
    slab = shape(6, EXT, LANES)
    to_pair, to_next = pl.pallas_call(
        second_kernel, out_shape=(slab, slab), in_specs=[SM, VM, VM, VM], out_specs=(VM, VM),
        compiler_params=params(16), name="slabs",
    )(place, packed, from_sibling, from_other)
    from_pair = lax.ppermute(to_pair, "gy", pairs_of(count_y, 0))
    from_next = lax.ppermute(to_next, "gy", pairs_of(count_y, 1))

    def sized(rows):
        return [scratch(*dims) for dims in level_dims(rows)]

    two, one, four = sized(EXT)
    two1, one1, four1 = sized(ROWS1)
    two2, one2, _ = sized(ROWS2)
    two3, one3, four3 = sized(16)
    out = pl.pallas_call(
        third_kernel,
        out_shape=(*level_shapes(48), *level_shapes(24), *level_shapes(ROWS2), shape(4 * TILES, LANES), shape(8, LANES)),
        in_specs=[SM] + [VM] * 5, out_specs=(VM,) * 23,
        scratch_shapes=[
            two, two, two, two, two, one, four, two, one, one, one,
            two1, two1, two1, two1, one1, four1, two1, one1, one1, one1,
            two2, one2, one2,
            two3, two3, two3, two3, one3, four3,
        ],
        compiler_params=params(48), name="descent",
    )(place, packed, from_sibling, from_other, from_pair, from_next)
    levels, tiles, sums = out[:21], out[21], out[22]

    tile_pair = lax.ppermute(tiles, "gy", pairs_of(count_y, 0))
    tile_next = lax.ppermute(tiles, "gy", pairs_of(count_y, 1))
    even = (index_y & 1) == 0
    right, left = jnp.where(even, tile_pair, tile_next), jnp.where(even, tile_next, tile_pair)
    beyond = jnp.where(iota(tiles.shape, 1) < LANES // 2, right, left)
    window = jnp.concatenate([tiles, beyond], axis=1)
    window = jnp.broadcast_to(window[None], (count_x, *window.shape))
    gathered = lax.all_to_all(window, "gx", 0, 0, tiled=True)

    devices = count_x * count_y
    fields, partial = pl.pallas_call(
        fourth_kernel,
        out_shape=(shape(8, PAIRS, ROWS, LANES), shape(devices, 16)),
        in_specs=[SM] + [VM] * 23, out_specs=(VM, VM),
        scratch_shapes=[
            scratch(TILES, ROWS, WIDE), sized(ROWS2)[1], sized(24)[1],
            *[sized(48)[1]] * 6, *[sized(24)[1]] * 4,
        ],
        compiler_params=params(48), name="ascent",
    )(place, gathered, sums, *levels)
    every = lax.all_to_all(partial, ("gx", "gy"), 0, 0, tiled=True)

    layers = 2 * PAIRS
    solution_out, residual_out, norm = pl.pallas_call(
        functools.partial(last_kernel, cells=float(layers * ROWS * LANES * devices)),
        out_shape=(shape(layers, ROWS, LANES), shape(layers, ROWS, LANES), shape(1, 1)),
        in_specs=[SM, VM, VM], out_specs=(VM, VM, VM), compiler_params=params(16), name="outputs",
    )(place, every, fields)
    return solution_out, residual_out, norm.reshape(1)


def solution(mesh):
    split, whole = P(None, "gx", "gy"), P()
    return jax.shard_map(
        shards, mesh=mesh, in_specs=(split, split, whole, whole, whole, split, split),
        out_specs=(split, split, whole), check_vma=False,
    )
```

time: 700 us -> 95.1 us (0.14); the launches traced: 691 us -> 94.2 us
  starting transfers between devices: 198 us -> 10.2 us
  blocking collectives: 229 us -> 45.8 us
  other arithmetic: 97.9 us -> 1.67 us
  local copies, waits for them, and re-layouts: 88.5 us -> 14.2 us
  waiting for transfers between devices: 55.6 us -> 5.37 us
  between operations: 21.7 us -> 0.79 us
  Pallas kernels: 0 us -> 16.2 us
    ppermute x68 -> x6, starting transfers between devices: 198 us -> 10.2 us  [the longest x1 5.41 us: shards(): tile_pair = lax.ppermute(tiles, 'gy', pairs_of(count_y, 0))]
    psum x2 -> x0, blocking collectives: 141 us -> none  [the longest x1 77.3 us: shards(): residual_precond = lax.psum(jnp.sum(right_side * precond), ('gx', 'gy'))]
    all_gather x1 -> x0, blocking collectives: 87.4 us -> none  [replicated(): lax.all_gather(source, ('gx', 'gy'), axis=1, tiled=True)]
    ppermute x68 -> x6, waiting for transfers between devices: 55.6 us -> 5.37 us  [the longest x1 3.52 us: shards(): from_pair = lax.ppermute(to_pair, 'gy', pairs_of(count_y, 0))]
    all_to_all x0 -> x2, blocking collectives: none -> 45.8 us  [the longest x1 23.1 us: shards(): every = lax.all_to_all(partial, ('gx', 'gy'), 0, 0, tiled=True)]
    mul x2 -> x0, other arithmetic: 45.5 us -> none  [the longest x1 44.8 us: conductivity(): return saturated * rooted * outer_term * outer_term]
    slice x58 -> x0, local copies, waits for them, and re-layouts: 44.6 us -> none  [the longest x3 4.35 us: replicated(): downward = jnp.concatenate([edge_z, upward[:-1]], axis=0)]
    reduce_sum x23 -> x0, other arithmetic: 25.7 us -> none  [the longest x11 16.3 us: block_sum(): field.reshape(layers, rows_x // 2, 2, rows_y // 2, 2).sum(axis=(2, 4))]
  transfers between devices with their start and end apart: 69 -> 6, of which waited for: 34 -> 3; matrix products, arithmetic and copies ran while one was open for 19% -> 0% of each run, Pallas kernels for 0% -> 0%
where the time goes in v1:
time: 95.1 us; the launch traced here: 94.2 us
  blocking collectives  45.8 us (48%)
  Pallas kernels  16.2 us (17%)
  local copies, waits for them, and re-layouts  14.2 us (15%)
  starting transfers between devices  10.2 us (11%)
  waiting for transfers between devices  5.37 us (6%)
  other arithmetic  1.67 us (2%)
    all_to_all x1, blocking collectives, shards(): every = lax.all_to_all(partial, ('gx', 'gy'), 0, 0, tiled=True)  23.1 us
    all_to_all x1, blocking collectives, shards(): gathered = lax.all_to_all(window, 'gx', 0, 0, tiled=True)  22.6 us
    unnamed x52, local copies, waits for them, and re-layouts  14.1 us
    pallas_call x1, Pallas kernels, shards(): pl.pallas_call(third_kernel, out_shape=(*level_shapes(48), *level_shapes(...  6.65 us
    pallas_call x1, Pallas kernels, shards(): pl.pallas_call(fourth_kernel, out_shape=(shape(8, PAIRS, ROWS, LANES), sh...  5.57 us
    ppermute x1, starting transfers between devices, shards(): tile_pair = lax.ppermute(tiles, 'gy', pairs_of(count_y, 0))  5.41 us
    ppermute x1, waiting for transfers between devices, shards(): from_pair = lax.ppermute(to_pair, 'gy', pairs_of(count_y, 0))  3.52 us
    ppermute x1, starting transfers between devices, shards(): from_pair = lax.ppermute(to_pair, 'gy', pairs_of(count_y, 0))  2.08 us
  transfers between devices with their start and end apart: 6, of which 3 were waited for; matrix products, arithmetic and copies ran while one was open for 0% of the time, Pallas kernels for 0%

profile of v1, /device:TPU:0, one launch (start us, length us, event | category | flops | bytes accessed | tf_op | source)
XLA Modules:
  0.0 94.2 jit_solution(17324753875498027418)
XLA Ops:
  2.1 0.9 copy-done.9
  3.0 0.9 copy-done.10
  3.9 0.9 copy-done.11
  4.8 0.9 copy-done.12
  5.7 0.9 %conductivity.1 = (f32[30,32,128]{2,1,0:T(8,128)S(1)}, f32[30,24,128]{2,1,0:T(8,128)S(1)}, f32[30,24,128]{2,1,0:T(8,128)S(1)}) custom-call(s32[4]{0:T(128)S(1)} %pad_add_fusion.place, f32[10,32,128]{2,1,0:T(8,128)S(1)} %copy-done.9, s32[10,32,128]{2,1,0:T(8,128)S(1)} %copy-done.10, f32[8,128]{1,0:T(8,128)S(1)} %select_maximum_fusion.table, ...), custom_call_target="tpu_custom_call" | custom-call | tf_op jit(solution)/shard_map/conductivity/pallas_call | solution.py:548
  7.5 1.0 %collective-permute-done.from_sibling = f32[30,24,128]{2,1,0:T(8,128)S(1)} collective-permute-done((f32[30,24,128]{2,1,0:T(8,128)S(1)}, f32[30,24,128]{2,1,0:T(8,128)S(1)}, u32[]{:S(2)}, u32[]{:S(2)}) %collective-permute-start) | collective-permute-done | bytes 368672 | tf_op jit(solution)/shard_map/ppermute | solution.py:552
  8.5 1.2 %slabs.1 = (f32[6,80,128]{2,1,0:T(8,128)S(1)}, f32[6,80,128]{2,1,0:T(8,128)S(1)}) custom-call(s32[4]{0:T(128)S(1)} %pad_add_fusion.place, f32[30,32,128]{2,1,0:T(8,128)S(1)} %get-tuple-element.36.packed, f32[30,24,128]{2,1,0:T(8,128)S(1)} %collective-permute-done.from_sibling, f32[30,24,128]{2,1,0:T(8,128)S(1)} %collective-permute-done.1.from_other), custom_call_target="tpu_custom_call" | custom-call | tf_op jit(solution)/shard_map/slabs/pallas_call | solution.py:555
  9.7 2.1 %collective-permute-start.2 = (f32[6,80,128]{2,1,0:T(8,128)S(1)}, f32[6,80,128]{2,1,0:T(8,128)S(1)}, u32[]{:S(2)}, u32[]{:S(2)}) collective-permute-start(f32[6,80,128]{2,1,0:T(8,128)S(1)} %get-tuple-element.39), channel_id=1, source_target_pairs={{0,1},{2,3},{4,5},{6,7},{8,9},{10,11},{12,13},{14,15},{1,0},{3,2},... | collective-permute-start | bytes 737288 | tf_op jit(solution)/shard_map/ppermute | solution.py:559
  12.4 3.5 %collective-permute-done.2.from_pair = f32[6,80,128]{2,1,0:T(8,128)S(1)} collective-permute-done((f32[6,80,128]{2,1,0:T(8,128)S(1)}, f32[6,80,128]{2,1,0:T(8,128)S(1)}, u32[]{:S(2)}, u32[]{:S(2)}) %collective-permute-start.2) | collective-permute-done | bytes 245792 | tf_op jit(solution)/shard_map/ppermute | solution.py:559
  16.0 6.7 %descent.1 = (f32[2,5,2,48,128]{4,3,2,1,0:T(8,128)S(1)}, f32[2,5,2,48,128]{4,3,2,1,0:T(8,128)S(1)}, f32[5,2,48,128]{3,2,1,0:T(8,128)S(1)}, f32[2,5,2,48,128]{4,3...) custom-call(s32[4]{0:T(128)S(1)} %pad_add_fusion.place, ...), custom_call_target="tpu_custom_call" | custom-call | tf_op jit(solution)/shard_map/descent/pallas_call | solution.py:569
  23.3 0.7 copy-done.5
  28.0 5.4 %collective-permute-start.4 = (f32[44,128]{1,0:T(8,128)}, f32[44,128]{1,0:T(8,128)}, u32[]{:S(2)}, u32[]{:S(2)}) collective-permute-start(f32[44,128]{1,0:T(8,128)} %get-tuple-element.41), channel_id=1, source_target_pairs={{0,1},{2,3},{4,5},{6,7},{8,9},{10,11},{12,13},{14,15},{1,0},{3,2},... | collective-permute-start | bytes 67592 | tf_op jit(solution)/shard_map/ppermute | solution.py:583
  33.4 1.3 %collective-permute-start.5 = (f32[44,128]{1,0:T(8,128)}, f32[44,128]{1,0:T(8,128)}, u32[]{:S(2)}, u32[]{:S(2)}) collective-permute-start(f32[44,128]{1,0:T(8,128)} %get-tuple-element.41), channel_id=1, source_target_pairs={{1,2},{3,4},{5,6},{7,8},{9,10},{11,12},{13,14},{2,1},{4,3},{6,5},{... | collective-permute-start | bytes 67592 | tf_op jit(solution)/shard_map/ppermute | solution.py:584
  34.6 0.9 collective-permute-done.4
  35.5 0.8 select_select_fusion
  36.3 0.8 pad_maximum_fusion
  37.1 22.6 %all_to_all.16.gathered = f32[8,44,256]{2,1,0:T(8,128)S(1)} all-to-all(f32[8,44,256]{2,1,0:T(8,128)S(1)} %broadcast_in_dim.2), channel_id=1, replica_groups=mesh['gx'=8,'gy'=16] {'gx'}, dimensions={0} | all-to-all | bytes 720896 | tf_op jit(solution)/shard_map/all_to_all | solution.py:590
  59.8 0.9 copy-done.18
  60.7 0.9 copy-done.20
  61.6 0.9 copy-done.22
  62.5 5.6 %ascent.1 = (f32[8,5,32,128]{3,2,1,0:T(8,128)}, f32[128,16]{1,0:T(8,128)S(1)}) custom-call(s32[4]{0:T(128)S(1)} %pad_add_fusion.place, f32[8,44,256]{2,1,0:T(8,128)S(1)} %all_to_all.16.gathered, f32[8,128]{1,0:T(8,128)S(1)} %get-tuple-element.42.sums_in, f32[2,5,2,48,128]{4,3,2,1,0:T(8,128)S(1)} %get-tuple-element.43.source0, ...), custom_call_target="tpu_custom_call" | custom-call | tf_op jit(solution)/shard_map/ascent/pallas_call | solution.py:593
  68.1 23.1 %all_to_all.17 = f32[128,1,16]{2,1,0:T(1,128)S(1)} all-to-all(f32[128,1,16]{2,1,0:T(1,128)S(1)} %bitcast.12), channel_id=1, replica_groups=mesh['gx'=8,'gy'=16] {'gx','gy'}, dimensions={0} | all-to-all | bytes 16384 | tf_op jit(solution)/shard_map/all_to_all | solution.py:603
  91.2 1.1 %copy-done.1 = f32[8,5,32,128]{3,2,1,0:T(8,128)S(1)} copy-done((f32[8,5,32,128]{3,2,1,0:T(8,128)S(1)}, f32[8,5,32,128]{3,2,1,0:T(8,128)}, u32[]{:S(2)}) %copy-start.1) | copy-done | bytes 655384
  92.3 1.9 %outputs.1 = (f32[10,32,128]{2,1,0:T(8,128)}, f32[10,32,128]{2,1,0:T(8,128)}, f32[1,1]{1,0:T(1,128)}) custom-call(s32[4]{0:T(128)S(1)} %pad_add_fusion.place, f32[128,16]{1,0:T(8,128)S(1)} %bitcast.11, f32[8,5,32,128]{3,2,1,0:T(8,128)S(1)} %copy-done.1), custom_call_target="tpu_custom_call" | custom-call | tf_op jit(solution)/shard_map/outputs/pallas_call | solution.py:606
  (54 shorter events, 7.6 us)
Async XLA Ops:
  2.1 0.9 copy-start.9
  3.0 0.9 copy-start.10
  3.9 0.9 copy-start.11
  4.8 0.9 copy-start.12
  6.7 3.0 %copy-start = (f32[30,32,128]{2,1,0:T(8,128)}, f32[30,32,128]{2,1,0:T(8,128)S(1)}, u32[]{:S(2)}) copy-start(f32[30,32,128]{2,1,0:T(8,128)S(1)} %get-tuple-element.36.packed) | copy-start | bytes 1474564
  6.7 1.8 %collective-permute-start = (f32[30,24,128]{2,1,0:T(8,128)S(1)}, f32[30,24,128]{2,1,0:T(8,128)S(1)}, u32[]{:S(2)}, u32[]{:S(2)}) collective-permute-start(f32[30,24,128]{2,1,0:T(8,128)S(1)} %get-tuple-element.37), channel_id=1, source_target_pairs={{0,16},{32,48},{64,80},{96,112},{16,0},{48,32},{80,64},{112,96},{1... | collective-permute-start | bytes 1105928 | tf_op jit(solution)/shard_map/ppermute | solution.py:552
  6.8 1.7 %collective-permute-start.1 = (f32[30,24,128]{2,1,0:T(8,128)S(1)}, f32[30,24,128]{2,1,0:T(8,128)S(1)}, u32[]{:S(2)}, u32[]{:S(2)}) collective-permute-start(f32[30,24,128]{2,1,0:T(8,128)S(1)} %get-tuple-element.38), channel_id=1, source_target_pairs={{16,32},{48,64},{80,96},{32,16},{64,48},{96,80},{17,33},{49,65},{8... | collective-permute-start | bytes 1105928 | tf_op jit(solution)/shard_map/ppermute | solution.py:553
  9.7 6.3 %collective-permute-start.2 = (f32[6,80,128]{2,1,0:T(8,128)S(1)}, f32[6,80,128]{2,1,0:T(8,128)S(1)}, u32[]{:S(2)}, u32[]{:S(2)}) collective-permute-start(f32[6,80,128]{2,1,0:T(8,128)S(1)} %get-tuple-element.39), channel_id=1, source_target_pairs={{0,1},{2,3},{4,5},{6,7},{8,9},{10,11},{12,13},{14,15},{1,0},{3,2},... | collective-permute-start | bytes 737288 | tf_op jit(solution)/shard_map/ppermute | solution.py:559
  11.8 4.2 %collective-permute-start.3 = (f32[6,80,128]{2,1,0:T(8,128)S(1)}, f32[6,80,128]{2,1,0:T(8,128)S(1)}, u32[]{:S(2)}, u32[]{:S(2)}) collective-permute-start(f32[6,80,128]{2,1,0:T(8,128)S(1)} %get-tuple-element.40), channel_id=1, source_target_pairs={{1,2},{3,4},{5,6},{7,8},{9,10},{11,12},{13,14},{2,1},{4,3},{6,5},{... | collective-permute-start | bytes 737288 | tf_op jit(solution)/shard_map/ppermute | solution.py:560
  22.6 0.7 copy-start.3
  23.3 0.7 copy-start.5
  24.0 0.7 copy-start.7
  28.0 7.5 %collective-permute-start.4 = (f32[44,128]{1,0:T(8,128)}, f32[44,128]{1,0:T(8,128)}, u32[]{:S(2)}, u32[]{:S(2)}) collective-permute-start(f32[44,128]{1,0:T(8,128)} %get-tuple-element.41), channel_id=1, source_target_pairs={{0,1},{2,3},{4,5},{6,7},{8,9},{10,11},{12,13},{14,15},{1,0},{3,2},... | collective-permute-start | bytes 67592 | tf_op jit(solution)/shard_map/ppermute | solution.py:583
  33.4 2.1 %collective-permute-start.5 = (f32[44,128]{1,0:T(8,128)}, f32[44,128]{1,0:T(8,128)}, u32[]{:S(2)}, u32[]{:S(2)}) collective-permute-start(f32[44,128]{1,0:T(8,128)} %get-tuple-element.41), channel_id=1, source_target_pairs={{1,2},{3,4},{5,6},{7,8},{9,10},{11,12},{13,14},{2,1},{4,3},{6,5},{... | collective-permute-start | bytes 67592 | tf_op jit(solution)/shard_map/ppermute | solution.py:584
  35.5 24.3 %copy-start.16 = (f32[5,2,24,128]{3,2,1,0:T(8,128)S(1)}, f32[5,2,24,128]{3,2,1,0:T(8,128)}, u32[]{:S(2)}) copy-start(f32[5,2,24,128]{3,2,1,0:T(8,128)} %copy-done.15) | copy-start | bytes 368644
  36.3 23.5 %copy-start.14 = (f32[5,2,24,128]{3,2,1,0:T(8,128)S(1)}, f32[5,2,24,128]{3,2,1,0:T(8,128)}, u32[]{:S(2)}) copy-start(f32[5,2,24,128]{3,2,1,0:T(8,128)} %copy-done.13) | copy-start | bytes 368644
  37.1 22.7 %copy-start.6 = (f32[2,5,2,24,128]{4,3,2,1,0:T(8,128)S(1)}, f32[2,5,2,24,128]{4,3,2,1,0:T(8,128)}, u32[]{:S(2)}) copy-start(f32[2,5,2,24,128]{4,3,2,1,0:T(8,128)} %copy-done.5) | copy-start | bytes 737284
  37.1 22.7 %copy-start.8 = (f32[4,2,48,128]{3,2,1,0:T(8,128)S(1)}, f32[4,2,48,128]{3,2,1,0:T(8,128)}, u32[]{:S(2)}) copy-start(f32[4,2,48,128]{3,2,1,0:T(8,128)} %copy-done.7) | copy-start | bytes 589828
  37.1 22.7 %copy-start.2 = (f32[2,5,2,48,128]{4,3,2,1,0:T(8,128)S(1)}, f32[2,5,2,48,128]{4,3,2,1,0:T(8,128)}, u32[]{:S(2)}) copy-start(f32[2,5,2,48,128]{4,3,2,1,0:T(8,128)} %get-tuple-element.47.north0) | copy-start | bytes 1474564
  37.1 22.7 %copy-start.4 = (f32[2,5,2,24,128]{4,3,2,1,0:T(8,128)S(1)}, f32[2,5,2,24,128]{4,3,2,1,0:T(8,128)}, u32[]{:S(2)}) copy-start(f32[2,5,2,24,128]{4,3,2,1,0:T(8,128)} %copy-done.3) | copy-start | bytes 737284
  59.8 0.9 copy-start.18
  60.7 0.9 copy-start.20
  61.6 0.9 copy-start.22
  91.2 1.1 %copy-start.1 = (f32[8,5,32,128]{3,2,1,0:T(8,128)S(1)}, f32[8,5,32,128]{3,2,1,0:T(8,128)}, u32[]{:S(2)}) copy-start(f32[8,5,32,128]{3,2,1,0:T(8,128)} %get-tuple-element.65.fields) | copy-start | bytes 1966084
  (8 other events, 5.2 us)

commit v2 on v1

--- a/solution.py
+++ b/solution.py
@@ -62,12 +62,16 @@
     return t + (jnp.where(odd, above, below) if c == 0 else jnp.where(odd, below, above))
 
 
-def params(limit=32):
+def position():
+    return lax.axis_index("gx"), lax.axis_index("gy")
+
+
+def params(limit):
     return pltpu.CompilerParams(vmem_limit_bytes=limit * MIB)
 
 
 VM = pl.BlockSpec(memory_space=pltpu.VMEM)
-SM = pl.BlockSpec(memory_space=pltpu.SMEM)
+HBM = pl.BlockSpec(memory_space=pltpu.MemorySpace.HBM)
 
 
 def shape(*dims):
@@ -93,10 +97,29 @@
             ref[rows, :] = x[:, LANES * half : LANES * (half + 1)]
 
 
-def first_kernel(place, pressure, soil, table, storage, source, packed, to_sibling, to_other):
-    even = (place[0] & 1) == 0
+def first_kernel(
+    pressure_in, soil_in, storage_in, source_in, alpha_in, power_in, saturated_in, packed, to_sibling, to_other,
+    pressure, soil, storage, source, table, sems,
+):
+    copies = [
+        pltpu.make_async_copy(alpha_in, table.at[0], sems.at[4]),
+        pltpu.make_async_copy(power_in, table.at[1], sems.at[5]),
+        pltpu.make_async_copy(saturated_in, table.at[2], sems.at[6]),
+        pltpu.make_async_copy(pressure_in, pressure, sems.at[0]),
+        pltpu.make_async_copy(soil_in, soil, sems.at[1]),
+        pltpu.make_async_copy(storage_in, storage, sems.at[2]),
+        pltpu.make_async_copy(source_in, source, sems.at[3]),
+    ]
+    for copy in copies:
+        copy.start()
+    even = (position()[0] & 1) == 0
     odd = odd_cells((ROWS, LANES), 0)
-    rows = [jnp.broadcast_to(table[q : q + 1, :], (8, LANES)) for q in range(3)]
+    for copy in copies:
+        copy.wait()
+    rows = []
+    for q in range(3):
+        row = jnp.concatenate([table[q], jnp.ones((1, LANES - NSOIL), jnp.float32)], axis=1)
+        rows.append(jnp.broadcast_to(jnp.log(row) if q == 0 else row, (8, LANES)))
 
     def look_up(row, ids):
         parts = [jnp.take_along_axis(row, ids[8 * b : 8 * b + 8], axis=1) for b in range(ROWS // 8)]
@@ -128,9 +151,9 @@
             put(q * 10 + PAIRS + m, jnp.where(odd, a, b))
 
 
-def second_kernel(place, packed, from_sibling, from_other, to_pair, to_next):
-    even_x = (place[0] & 1) == 0
-    even_y = (place[1] & 1) == 0
+def second_kernel(packed, from_sibling, from_other, to_pair, to_next):
+    gx, gy = position()
+    even_x, even_y = (gx & 1) == 0, (gy & 1) == 0
     lane = iota((EXT, LANES), 1)
     for tile in range(6):
         pair, other = None, None
@@ -225,7 +248,7 @@
 
 
 def third_kernel(
-    place, packed, from_sibling, from_other, from_pair, from_next,
+    packed, from_sibling, from_other, from_pair, from_next,
     source0, inv0, first0, east0, north0, inner0, outer0,
     source1, inv1, first1, east1, north1, inner1, outer1,
     source2, inv2, first2, east2, north2, inner2, outer2,
@@ -243,8 +266,8 @@
     stor1, src1, e1, n1, in1, out1, i1, f1, s1, r1 = map(Wide, (stor1, src1, e1, n1, in1, out1, i1, f1, s1, r1))
     stor2, s2, r2 = map(Wide, (stor2, s2, r2))
     stor3, src3, e3, n3, in3, out3 = map(Wide, (stor3, src3, e3, n3, in3, out3))
-    even_x = (place[0] & 1) == 0
-    even_y = (place[1] & 1) == 0
+    gx, gy = position()
+    even_x, even_y = (gx & 1) == 0, (gy & 1) == 0
     lane = iota((EXT, LANES), 1)
     for tile in range(6):
         pair, other = from_pair[tile], from_next[tile]
@@ -266,11 +289,11 @@
     dims = (EXT, WIDE)
     odd = odd_cells(dims, 0)
     row, column = iota(dims, 0), iota(dims, 1)
-    last_row = (row == HALO + ROWS - 1) & (place[0] == place[2] - 1)
-    before_row = (row == HALO - 1) & (place[0] == 0)
+    last_row = (row == HALO + ROWS - 1) & (gx == lax.axis_size("gx") - 1)
+    before_row = (row == HALO - 1) & (gx == 0)
     keep_x = jnp.where(last_row | before_row, 0.0, 0.5)
-    last_column = (column == LANES - 1) & (place[1] == place[3] - 1)
-    before_column = (column == WIDE - 1) & (place[1] == 0)
+    last_column = (column == LANES - 1) & (gy == lax.axis_size("gy") - 1)
+    before_column = (column == WIDE - 1) & (gy == 0)
     keep_y = jnp.where(last_column | before_column, 0.0, 0.5)
     for m in range(PAIRS):
         a, b = cond[0, m], cond[1, m]
@@ -346,6 +369,14 @@
             outer0[m], outer1[m] = outer[m, slice(16, 64)], out1[m, slice(8, 32)]
 
 
+def window_kernel(tiles, from_pair, from_next, window):
+    even = (position()[1] & 1) == 0
+    window[:, :LANES] = tiles[...]
+    a, b = from_pair[...], from_next[...]
+    right_first = (iota(a.shape, 1) < LANES // 2) == even
+    window[:, LANES:] = jnp.where(right_first, a, b)
+
+
 def spread_rows(level, low, high, into, m):
     rows = low.shape[0]
     bit = lane_bit(low.shape, level)
@@ -354,7 +385,7 @@
 
 
 def fourth_kernel(
-    place, gathered, sums_in,
+    mine, before, after, sib_mine, sib_before, sib_after, sums_in,
     source0, inv0, first0, east0, north0, inner0, outer0,
     source1, inv1, first1, east1, north1, inner1, outer1,
     source2, inv2, first2, east2, north2, inner2, outer2,
@@ -368,14 +399,18 @@
     work2, work1, work0a, work0b, va, vb, wa, wb = map(Wide, (work2, work1, work0a, work0b, va, vb, wa, wb))
     ua2, ub2, ua1, ub1 = map(Wide, (ua2, ub2, ua1, ub1))
     f32 = jnp.float32
-    for q in range(TILES):
-        for g in range(8):
-            whole[q, 4 * g : 4 * g + 4] = gathered[g, 4 * q : 4 * q + 4]
+    even = (position()[0] & 1) == 0
+    for slot, (same, sib) in enumerate(((before, sib_before), (mine, sib_mine), (after, sib_after))):
+        a, b = same[...], sib[...]
+        low, high = jnp.where(even, a, b), jnp.where(even, b, a)
+        for q in range(TILES):
+            whole[q, 8 * slot : 8 * slot + 4] = low[4 * q : 4 * q + 4]
+            whole[q, 8 * slot + 4 : 8 * slot + 8] = high[4 * q : 4 * q + 4]
     own_f, own_s = sums_in[0:1, 0:1], sums_in[1:2, 0:1]
     guess = own_f / own_s
     g0, g1, h0, i30, i31, e30, e31, n30, n31, in3, out3 = [whole[q] for q in range(TILES)]
     inv3, e3, n3 = (i30, i31), (e30, e31), (n30, n31)
-    odd3 = odd_cells((ROWS, WIDE), 3)
+    odd3 = odd_cells((24, WIDE), 3)
 
     def beside3(c, u):
         t = e3[c] * row_next(u) + row_prev(e3[1 - c] * u)
@@ -388,8 +423,7 @@
         a1, b1 = g1 + beside3(1, a0) * inv3[1], beside3(1, b0) * inv3[1]
         a0, b0 = g0 + beside3(0, a1) * inv3[0], beside3(0, b1) * inv3[0]
 
-    shift = lax.rem(35 - 4 * place[0], 32)
-    a0, a1, b0, b1 = [pltpu.roll(x, shift, 0)[:16] for x in (a0, a1, b0, b1)]
+    a0, a1, b0, b1 = [jnp.where(even, pltpu.roll(x, 19, 0), pltpu.roll(x, 15, 0))[:16] for x in (a0, a1, b0, b1)]
     dims3 = (16, WIDE)
     phase = iota(dims3, 1) & 7
     odd3 = odd_cells(dims3, 3, 1)
@@ -490,7 +524,7 @@
     sums[...] = jnp.broadcast_to(line, sums.shape)
 
 
-def last_kernel(place, sums, fields, solution_ref, residual_ref, norm_ref, *, cells):
+def last_kernel(sums, fields, solution_out, residual_out, norm_ref, solution_ref, residual_ref, sems, *, cells):
     x = sums[...]
 
     def column(q):
@@ -506,9 +540,11 @@
     s, t = step - 1.0, step * shift
     squares = total(dd - 2.0 * s * da + s * s * aa - 2.0 * t * db + 2.0 * s * t * ab + t * t * bb)
     norm_ref[...] = jnp.sqrt(jnp.maximum(squares, 0.0) / cells)
-    mine = place[0] * place[3] + place[1]
+    gx, gy = position()
+    mine = gx * lax.axis_size("gy") + gy
     here = total(jnp.where(iota(shift.shape, 0) == mine, shift, 0.0))
     odd = odd_cells((ROWS, LANES), 0)
+    copies = []
     for m in range(PAIRS):
         p0, p1, q0, q1, r0, r1, img_a, img_b = [fields[t, m] for t in range(8)]
         s0, s1 = step * (p0 + here * q0), step * (p1 + here * q1)
@@ -517,6 +553,12 @@
         solution_ref[2 * m + 1] = jnp.where(odd, s0, s1)
         residual_ref[2 * m] = jnp.where(odd, n1, n0)
         residual_ref[2 * m + 1] = jnp.where(odd, n0, n1)
+        layers = pl.ds(2 * m, 2)
+        for q, (ref, out) in enumerate(((solution_ref, solution_out), (residual_ref, residual_out))):
+            copies.append(pltpu.make_async_copy(ref.at[layers], out.at[layers], sems.at[q, m]))
+            copies[-1].start()
+    for copy in copies:
+        copy.wait()
 
 
 def level_dims(rows):
@@ -537,27 +579,30 @@
     return [(i, i + 1) for i in range(first, count - 1, 2)] + [(i + 1, i) for i in range(first, count - 1, 2)]
 
 
+def pair_exchange(x, axis):
+    count = lax.axis_size(axis)
+    return [lax.ppermute(x_i, axis, pairs_of(count, first)) for first, x_i in enumerate(x)]
+
+
 def shards(pressure, soil, vg_alpha, vg_n, sat_cond, storage, right_side):
     count_x, count_y = lax.axis_size("gx"), lax.axis_size("gy")
-    index_x, index_y = lax.axis_index("gx"), lax.axis_index("gy")
-    place = jnp.stack([index_x, index_y, jnp.int32(count_x), jnp.int32(count_y)])
-    table = jnp.stack([jnp.log(vg_alpha), vg_n, sat_cond])
-    table = jnp.pad(table, ((0, 5), (0, LANES - NSOIL)), constant_values=1.0)
-
-    slab = shape(6 * PAIRS, HALO, LANES)
+    block, slab = scratch(2 * PAIRS, ROWS, LANES), shape(6 * PAIRS, HALO, LANES)
+    arguments = (pressure, soil, storage, right_side, *[v.reshape(1, NSOIL) for v in (vg_alpha, vg_n, sat_cond)])
     packed, to_sibling, to_other = pl.pallas_call(
         first_kernel, out_shape=(shape(6 * PAIRS, ROWS, LANES), slab, slab),
-        in_specs=[SM, VM, VM, VM, VM, VM], out_specs=(VM, VM, VM), compiler_params=params(16), name="conductivity",
-    )(place, pressure, soil, table, storage, right_side)
-    from_sibling = lax.ppermute(to_sibling, "gx", pairs_of(count_x, 0))
-    from_other = lax.ppermute(to_other, "gx", pairs_of(count_x, 1))
+        in_specs=[HBM] * 7, out_specs=(VM, VM, VM),
+        scratch_shapes=[
+            block, pltpu.VMEM((2 * PAIRS, ROWS, LANES), jnp.int32), block, block, scratch(3, 1, NSOIL), pltpu.SemaphoreType.DMA((7,)),
+        ],
+        compiler_params=params(4), name="conductivity",
+    )(*[pltpu.with_memory_space_constraint(v, pltpu.MemorySpace.HBM) for v in arguments])
+    from_sibling, from_other = pair_exchange((to_sibling, to_other), "gx")
     slab = shape(6, EXT, LANES)
     to_pair, to_next = pl.pallas_call(
-        second_kernel, out_shape=(slab, slab), in_specs=[SM, VM, VM, VM], out_specs=(VM, VM),
-        compiler_params=params(16), name="slabs",
-    )(place, packed, from_sibling, from_other)
-    from_pair = lax.ppermute(to_pair, "gy", pairs_of(count_y, 0))
-    from_next = lax.ppermute(to_next, "gy", pairs_of(count_y, 1))
+        second_kernel, out_shape=(slab, slab), in_specs=[VM, VM, VM], out_specs=(VM, VM),
+        compiler_params=params(4), name="slabs",
+    )(packed, from_sibling, from_other)
+    from_pair, from_next = pair_exchange((to_pair, to_next), "gy")
 
     def sized(rows):
         return [scratch(*dims) for dims in level_dims(rows)]
@@ -569,45 +614,47 @@
     out = pl.pallas_call(
         third_kernel,
         out_shape=(*level_shapes(48), *level_shapes(24), *level_shapes(ROWS2), shape(4 * TILES, LANES), shape(8, LANES)),
-        in_specs=[SM] + [VM] * 5, out_specs=(VM,) * 23,
+        in_specs=[VM] * 5, out_specs=(VM,) * 23,
         scratch_shapes=[
             two, two, two, two, two, one, four, two, one, one, one,
             two1, two1, two1, two1, one1, four1, two1, one1, one1, one1,
             two2, one2, one2,
             two3, two3, two3, two3, one3, four3,
         ],
-        compiler_params=params(48), name="descent",
-    )(place, packed, from_sibling, from_other, from_pair, from_next)
+        compiler_params=params(12), name="descent",
+    )(packed, from_sibling, from_other, from_pair, from_next)
     levels, tiles, sums = out[:21], out[21], out[22]
 
-    tile_pair = lax.ppermute(tiles, "gy", pairs_of(count_y, 0))
-    tile_next = lax.ppermute(tiles, "gy", pairs_of(count_y, 1))
-    even = (index_y & 1) == 0
-    right, left = jnp.where(even, tile_pair, tile_next), jnp.where(even, tile_next, tile_pair)
-    beyond = jnp.where(iota(tiles.shape, 1) < LANES // 2, right, left)
-    window = jnp.concatenate([tiles, beyond], axis=1)
-    window = jnp.broadcast_to(window[None], (count_x, *window.shape))
-    gathered = lax.all_to_all(window, "gx", 0, 0, tiled=True)
+    tile_pair, tile_next = pair_exchange((tiles, tiles), "gy")
+    window = pl.pallas_call(
+        window_kernel, out_shape=shape(4 * TILES, WIDE), in_specs=[VM] * 3, out_specs=VM, compiler_params=params(2), name="window",
+    )(tiles, tile_pair, tile_next)
+    sibling = pairs_of(count_x, 0)
+    before = lax.ppermute(window, "gx", [(i, i + 2) for i in range(count_x - 2)])
+    after = lax.ppermute(window, "gx", [(i + 2, i) for i in range(count_x - 2)])
+    blocks = (window, before, after, *[lax.ppermute(x, "gx", sibling) for x in (window, before, after)])
 
     devices = count_x * count_y
     fields, partial = pl.pallas_call(
         fourth_kernel,
         out_shape=(shape(8, PAIRS, ROWS, LANES), shape(devices, 16)),
-        in_specs=[SM] + [VM] * 23, out_specs=(VM, VM),
+        in_specs=[VM] * 28, out_specs=(VM, VM),
         scratch_shapes=[
-            scratch(TILES, ROWS, WIDE), sized(ROWS2)[1], sized(24)[1],
+            scratch(TILES, 24, WIDE), sized(ROWS2)[1], sized(24)[1],
             *[sized(48)[1]] * 6, *[sized(24)[1]] * 4,
         ],
-        compiler_params=params(48), name="ascent",
-    )(place, gathered, sums, *levels)
+        compiler_params=params(8), name="ascent",
+    )(*blocks, sums, *levels)
     every = lax.all_to_all(partial, ("gx", "gy"), 0, 0, tiled=True)
 
     layers = 2 * PAIRS
+    out = shape(layers, ROWS, LANES)
     solution_out, residual_out, norm = pl.pallas_call(
         functools.partial(last_kernel, cells=float(layers * ROWS * LANES * devices)),
-        out_shape=(shape(layers, ROWS, LANES), shape(layers, ROWS, LANES), shape(1, 1)),
-        in_specs=[SM, VM, VM], out_specs=(VM, VM, VM), compiler_params=params(16), name="outputs",
-    )(place, every, fields)
+        out_shape=(out, out, shape(1, 1)), in_specs=[VM, VM], out_specs=(HBM, HBM, VM),
+        scratch_shapes=[scratch(*out.shape), scratch(*out.shape), pltpu.SemaphoreType.DMA((2, PAIRS))],
+        compiler_params=params(4), name="outputs",
+    )(every, fields)
     return solution_out, residual_out, norm.reshape(1)
 
 

time: 95.1 us -> 73.3 us (0.77)
  blocking collectives: 45.8 us -> 22.7 us
  starting transfers between devices: 10.2 us -> 27.9 us
  local copies, waits for them, and re-layouts: 14.2 us -> 0 us
  Pallas kernels: 16.2 us -> 12.6 us
  waiting for transfers between devices: 5.37 us -> 8.71 us
  other arithmetic: 1.67 us -> 0 us
    all_to_all x1 -> x0, blocking collectives: 22.6 us -> none  [shards(): gathered = lax.all_to_all(window, 'gx', 0, 0, tiled=True)]
    ppermute x6 -> x11, starting transfers between devices: 10.2 us -> 27.9 us  [the longest x1 13.1 us: shards(): lax.ppermute(window, 'gx', [(i, i + 2) for i in range(count_x - 2)])]
    unnamed x52 -> x0, local copies, waits for them, and re-layouts: 14.1 us -> none
    ppermute x6 -> x11, waiting for transfers between devices: 5.37 us -> 8.71 us  [the longest x6 6.32 us: pair_exchange(): lax.ppermute(x_i, axis, pairs_of(count, first))]
    pallas_call x1, Pallas kernels: 5.57 us -> 3.23 us  [shards(): pl.pallas_call(fourth_kernel, out_shape=(shape(8, PAIRS, ROWS, LANES), sh...]
    pallas_call x1, Pallas kernels: 6.65 us -> 5.08 us  [shards(): pl.pallas_call(third_kernel, out_shape=(*level_shapes(48), *level_shapes(...]
  transfers between devices with their start and end apart: 6 -> 11, of which waited for: 3 -> 5; matrix products, arithmetic and copies ran while one was open for 0% -> 0% of each run, Pallas kernels for 0% -> 0%
where the time goes in v2:
time: 73.3 us; the launch traced here: 72.7 us
  starting transfers between devices  27.9 us (38%)
  blocking collectives  22.7 us (31%)
  Pallas kernels  12.6 us (17%)
  waiting for transfers between devices  8.71 us (12%)
    all_to_all x1, blocking collectives, shards(): every = lax.all_to_all(partial, ('gx', 'gy'), 0, 0, tiled=True)  22.7 us
    ppermute x1, starting transfers between devices, shards(): lax.ppermute(window, 'gx', [(i, i + 2) for i in range(count_x - 2)])  13.1 us
    ppermute x6, starting transfers between devices, pair_exchange(): lax.ppermute(x_i, axis, pairs_of(count, first))  12.9 us
    ppermute x6, waiting for transfers between devices, pair_exchange(): lax.ppermute(x_i, axis, pairs_of(count, first))  6.32 us
    pallas_call x1, Pallas kernels, shards(): pl.pallas_call(third_kernel, out_shape=(*level_shapes(48), *level_shapes(...  5.08 us
    pallas_call x1, Pallas kernels, shards(): pl.pallas_call(fourth_kernel, out_shape=(shape(8, PAIRS, ROWS, LANES), sh...  3.23 us
    pallas_call x1, Pallas kernels, shards(): pl.pallas_call(functools.partial(last_kernel, cells=float(layers * ROWS *...  1.9 us
    pallas_call x1, Pallas kernels, shards(): pl.pallas_call(first_kernel, out_shape=(shape(6 * PAIRS, ROWS, LANES), sl...  1.71 us
  transfers between devices with their start and end apart: 11, of which 5 were waited for; matrix products, arithmetic and copies ran while one was open for 0% of the time, Pallas kernels for 0%

profile of v2, /device:TPU:0, one launch (start us, length us, event | category | flops | bytes accessed | tf_op | source)
XLA Modules:
  0.0 72.7 jit_solution(4462399608480464119)
XLA Ops:
  0.6 1.7 %conductivity.1 = (f32[30,32,128]{2,1,0:T(8,128)S(1)}, f32[30,24,128]{2,1,0:T(8,128)S(1)}, f32[30,24,128]{2,1,0:T(8,128)S(1)}) custom-call(f32[10,32,128]{2,1,0:T(8,128)} %pressure_in.1, s32[10,32,128]{2,1,0:T(8,128)} %soil_in.1, f32[10,32,128]{2,1,0:T(8,128)} %storage_in.1, f32[10,32,128]{2,1,0:T(8,128)} %source_in.1, f32[1,23]{1,0:T(1,128)} %bitcast.10, ...), custom_call_target="tpu_custom_call" | custom-call | tf_op jit(solution)/shard_map/conductivity/pallas_call | solution.py:591
  2.3 0.1 collective-permute-start
  2.4 0.7 collective-permute-start.1
  3.1 1.0 %collective-permute-done.from_sibling = f32[30,24,128]{2,1,0:T(8,128)S(1)} collective-permute-done((f32[30,24,128]{2,1,0:T(8,128)S(1)}, f32[30,24,128]{2,1,0:T(8,128)S(1)}, u32[]{:S(2)}, u32[]{:S(2)}) %collective-permute-start) | collective-permute-done | bytes 368672 | tf_op jit(solution)/shard_map/ppermute | solution.py:584
  4.1 0.0 collective-permute-done.1.from_other
  4.1 0.7 slabs.1
  4.8 2.1 %collective-permute-start.2 = (f32[6,80,128]{2,1,0:T(8,128)S(1)}, f32[6,80,128]{2,1,0:T(8,128)S(1)}, u32[]{:S(2)}, u32[]{:S(2)}) collective-permute-start(f32[6,80,128]{2,1,0:T(8,128)S(1)} %get-tuple-element.39), channel_id=1, source_target_pairs={{0,1},{2,3},{4,5},{6,7},{8,9},{10,11},{12,13},{14,15},{1,0},{3,2},... | collective-permute-start | bytes 737288 | tf_op jit(solution)/shard_map/ppermute | solution.py:584
  6.9 0.7 collective-permute-start.3
  7.5 3.5 %collective-permute-done.2.from_pair = f32[6,80,128]{2,1,0:T(8,128)S(1)} collective-permute-done((f32[6,80,128]{2,1,0:T(8,128)S(1)}, f32[6,80,128]{2,1,0:T(8,128)S(1)}, u32[]{:S(2)}, u32[]{:S(2)}) %collective-permute-start.2) | collective-permute-done | bytes 245792 | tf_op jit(solution)/shard_map/ppermute | solution.py:584
  11.1 5.1 %descent.1 = (f32[2,5,2,48,128]{4,3,2,1,0:T(8,128)S(1)}, f32[2,5,2,48,128]{4,3,2,1,0:T(8,128)S(1)}, f32[5,2,48,128]{3,2,1,0:T(8,128)S(1)}, f32[2,5,2,48,128]{4,3...) custom-call(f32[30,32,128]{2,1,0:T(8,128)S(1)} %get-tuple-element.36, ...), custom_call_target="tpu_custom_call" | custom-call | tf_op jit(solution)/shard_map/descent/pallas_call | solution.py:614
  16.2 0.7 collective-permute-start.5
  16.8 8.7 %collective-permute-start.4 = (f32[44,128]{1,0:T(8,128)S(1)}, f32[44,128]{1,0:T(8,128)S(1)}, u32[]{:S(2)}, u32[]{:S(2)}) collective-permute-start(f32[44,128]{1,0:T(8,128)S(1)} %get-tuple-element.41.tiles), channel_id=1, source_target_pairs={{0,1},{2,3},{4,5},{6,7},{8,9},{10,11},{12,13},{14,15},{1,0},{3,2},... | collective-permute-start | bytes 67592 | tf_op jit(solution)/shard_map/ppermute | solution.py:584
  25.6 0.0 collective-permute-done.5.from_next
  25.6 1.8 %collective-permute-done.4.from_pair = f32[44,128]{1,0:T(8,128)S(1)} collective-permute-done((f32[44,128]{1,0:T(8,128)S(1)}, f32[44,128]{1,0:T(8,128)S(1)}, u32[]{:S(2)}, u32[]{:S(2)}) %collective-permute-start.4) | collective-permute-done | bytes 22560 | tf_op jit(solution)/shard_map/ppermute | solution.py:584
  27.4 1.3 %collective-permute-start.7 = (f32[44,256]{1,0:T(8,128)S(1)}, f32[44,256]{1,0:T(8,128)S(1)}, u32[]{:S(2)}, u32[]{:S(2)}) collective-permute-start(f32[44,256]{1,0:T(8,128)S(1)} %window.1.mine), channel_id=1, source_target_pairs={{32,0},{48,16},{64,32},{80,48},{96,64},{112,80},{33,1},{49,17},{65... | collective-permute-start | bytes 135176 | tf_op jit(solution)/shard_map/ppermute | solution.py:634
  28.7 13.1 %collective-permute-start.6 = (f32[44,256]{1,0:T(8,128)S(1)}, f32[44,256]{1,0:T(8,128)S(1)}, u32[]{:S(2)}, u32[]{:S(2)}) collective-permute-start(f32[44,256]{1,0:T(8,128)S(1)} %window.1.mine), channel_id=1, source_target_pairs={{0,32},{16,48},{32,64},{48,80},{64,96},{80,112},{1,33},{17,49},{33... | collective-permute-start | bytes 135176 | tf_op jit(solution)/shard_map/ppermute | solution.py:633
  41.8 0.1 collective-permute-start.8
  41.9 0.0 collective-permute-done.7.after
  42.0 0.5 collective-permute-start.10
  42.4 1.1 %collective-permute-done.6.before = f32[44,256]{1,0:T(8,128)S(1)} collective-permute-done((f32[44,256]{1,0:T(8,128)S(1)}, f32[44,256]{1,0:T(8,128)S(1)}, u32[]{:S(2)}, u32[]{:S(2)}) %collective-permute-start.6) | collective-permute-done | bytes 45088 | tf_op jit(solution)/shard_map/ppermute | solution.py:633
  43.6 1.2 %collective-permute-done.9.sib_before = f32[44,256]{1,0:T(8,128)S(1)} collective-permute-done((f32[44,256]{1,0:T(8,128)S(1)}, f32[44,256]{1,0:T(8,128)S(1)}, u32[]{:S(2)}, u32[]{:S(2)}) %collective-permute-start.9) | collective-permute-done | bytes 45088 | tf_op jit(solution)/shard_map/ppermute | solution.py:635
  44.8 3.2 %ascent.1 = (f32[8,5,32,128]{3,2,1,0:T(8,128)S(1)}, f32[128,16]{1,0:T(8,128)S(1)}) custom-call(f32[44,256]{1,0:T(8,128)S(1)} %window.1.mine, f32[44,256]{1,0:T(8,128)S(1)} %collective-permute-done.6.before, f32[44,256]{1,0:T(8,128)S(1)} %collective-permute-done.7.after, f32[44,256]{1,0:T(8,128)S(1)} %collective-permute-done.8.sib_mine, ...), custom_call_target="tpu_custom_call" | custom-call | tf_op jit(solution)/shard_map/ascent/pallas_call | solution.py:638
  48.0 22.7 %all_to_all.11 = f32[128,1,16]{2,1,0:T(1,128)S(1)} all-to-all(f32[128,1,16]{2,1,0:T(1,128)S(1)} %bitcast.9), channel_id=1, replica_groups=mesh['gx'=8,'gy'=16] {'gx','gy'}, dimensions={0} | all-to-all | bytes 16384 | tf_op jit(solution)/shard_map/all_to_all | solution.py:648
  70.8 1.9 %outputs.1 = (f32[10,32,128]{2,1,0:T(8,128)}, f32[10,32,128]{2,1,0:T(8,128)}, f32[1,1]{1,0:T(1,128)}) custom-call(f32[128,16]{1,0:T(8,128)S(1)} %bitcast.8, f32[8,5,32,128]{3,2,1,0:T(8,128)S(1)} %get-tuple-element.65.fields), custom_call_target="tpu_custom_call" | custom-call | tf_op jit(solution)/shard_map/outputs/pallas_call | solution.py:652
  (5 shorter events, 0.0 us)
Async XLA Ops:
  2.3 1.8 %collective-permute-start = (f32[30,24,128]{2,1,0:T(8,128)S(1)}, f32[30,24,128]{2,1,0:T(8,128)S(1)}, u32[]{:S(2)}, u32[]{:S(2)}) collective-permute-start(f32[30,24,128]{2,1,0:T(8,128)S(1)} %get-tuple-element.37), channel_id=1, source_target_pairs={{0,16},{32,48},{64,80},{96,112},{16,0},{48,32},{80,64},{112,96},{1... | collective-permute-start | bytes 1105928 | tf_op jit(solution)/shard_map/ppermute | solution.py:584
  2.4 1.7 %collective-permute-start.1 = (f32[30,24,128]{2,1,0:T(8,128)S(1)}, f32[30,24,128]{2,1,0:T(8,128)S(1)}, u32[]{:S(2)}, u32[]{:S(2)}) collective-permute-start(f32[30,24,128]{2,1,0:T(8,128)S(1)} %get-tuple-element.38), channel_id=1, source_target_pairs={{16,32},{48,64},{80,96},{32,16},{64,48},{96,80},{17,33},{49,65},{8... | collective-permute-start | bytes 1105928 | tf_op jit(solution)/shard_map/ppermute | solution.py:584
  4.8 6.3 %collective-permute-start.2 = (f32[6,80,128]{2,1,0:T(8,128)S(1)}, f32[6,80,128]{2,1,0:T(8,128)S(1)}, u32[]{:S(2)}, u32[]{:S(2)}) collective-permute-start(f32[6,80,128]{2,1,0:T(8,128)S(1)} %get-tuple-element.39), channel_id=1, source_target_pairs={{0,1},{2,3},{4,5},{6,7},{8,9},{10,11},{12,13},{14,15},{1,0},{3,2},... | collective-permute-start | bytes 737288 | tf_op jit(solution)/shard_map/ppermute | solution.py:584
  6.9 4.2 %collective-permute-start.3 = (f32[6,80,128]{2,1,0:T(8,128)S(1)}, f32[6,80,128]{2,1,0:T(8,128)S(1)}, u32[]{:S(2)}, u32[]{:S(2)}) collective-permute-start(f32[6,80,128]{2,1,0:T(8,128)S(1)} %get-tuple-element.40), channel_id=1, source_target_pairs={{1,2},{3,4},{5,6},{7,8},{9,10},{11,12},{13,14},{2,1},{4,3},{6,5},{... | collective-permute-start | bytes 737288 | tf_op jit(solution)/shard_map/ppermute | solution.py:584
  16.2 9.4 %collective-permute-start.5 = (f32[44,128]{1,0:T(8,128)S(1)}, f32[44,128]{1,0:T(8,128)S(1)}, u32[]{:S(2)}, u32[]{:S(2)}) collective-permute-start(f32[44,128]{1,0:T(8,128)S(1)} %get-tuple-element.41.tiles), channel_id=1, source_target_pairs={{1,2},{3,4},{5,6},{7,8},{9,10},{11,12},{13,14},{2,1},{4,3},{6,5},{... | collective-permute-start | bytes 67592 | tf_op jit(solution)/shard_map/ppermute | solution.py:584
  16.8 10.6 %collective-permute-start.4 = (f32[44,128]{1,0:T(8,128)S(1)}, f32[44,128]{1,0:T(8,128)S(1)}, u32[]{:S(2)}, u32[]{:S(2)}) collective-permute-start(f32[44,128]{1,0:T(8,128)S(1)} %get-tuple-element.41.tiles), channel_id=1, source_target_pairs={{0,1},{2,3},{4,5},{6,7},{8,9},{10,11},{12,13},{14,15},{1,0},{3,2},... | collective-permute-start | bytes 67592 | tf_op jit(solution)/shard_map/ppermute | solution.py:584
  27.4 14.6 %collective-permute-start.7 = (f32[44,256]{1,0:T(8,128)S(1)}, f32[44,256]{1,0:T(8,128)S(1)}, u32[]{:S(2)}, u32[]{:S(2)}) collective-permute-start(f32[44,256]{1,0:T(8,128)S(1)} %window.1.mine), channel_id=1, source_target_pairs={{32,0},{48,16},{64,32},{80,48},{96,64},{112,80},{33,1},{49,17},{65... | collective-permute-start | bytes 135176 | tf_op jit(solution)/shard_map/ppermute | solution.py:634
  28.7 14.9 %collective-permute-start.6 = (f32[44,256]{1,0:T(8,128)S(1)}, f32[44,256]{1,0:T(8,128)S(1)}, u32[]{:S(2)}, u32[]{:S(2)}) collective-permute-start(f32[44,256]{1,0:T(8,128)S(1)} %window.1.mine), channel_id=1, source_target_pairs={{0,32},{16,48},{32,64},{48,80},{64,96},{80,112},{1,33},{17,49},{33... | collective-permute-start | bytes 135176 | tf_op jit(solution)/shard_map/ppermute | solution.py:633
  41.8 1.7 %collective-permute-start.8 = (f32[44,256]{1,0:T(8,128)S(1)}, f32[44,256]{1,0:T(8,128)S(1)}, u32[]{:S(2)}, u32[]{:S(2)}) collective-permute-start(f32[44,256]{1,0:T(8,128)S(1)} %window.1.mine), channel_id=1, source_target_pairs={{0,16},{32,48},{64,80},{96,112},{16,0},{48,32},{80,64},{112,96},{1... | collective-permute-start | bytes 135176 | tf_op jit(solution)/shard_map/ppermute | solution.py:635
  42.0 1.6 %collective-permute-start.10 = (f32[44,256]{1,0:T(8,128)S(1)}, f32[44,256]{1,0:T(8,128)S(1)}, u32[]{:S(2)}, u32[]{:S(2)}) collective-permute-start(f32[44,256]{1,0:T(8,128)S(1)} %collective-permute-done.7.after), channel_id=1, source_target_pairs={{0,16},{32,48},{64,80},{96,112},{16,0},{48,32},{80,64},{112,96},{1... | collective-permute-start | bytes 135176 | tf_op jit(solution)/shard_map/ppermute | solution.py:635
  43.6 1.2 %collective-permute-start.9 = (f32[44,256]{1,0:T(8,128)S(1)}, f32[44,256]{1,0:T(8,128)S(1)}, u32[]{:S(2)}, u32[]{:S(2)}) collective-permute-start(f32[44,256]{1,0:T(8,128)S(1)} %collective-permute-done.6.before), channel_id=1, source_target_pairs={{0,16},{32,48},{64,80},{96,112},{16,0},{48,32},{80,64},{112,96},{1... | collective-permute-start | bytes 135176 | tf_op jit(solution)/shard_map/ppermute | solution.py:635

commit v3 on v2

--- a/solution.py
+++ b/solution.py
@@ -13,7 +13,7 @@
 ROWS, LANES = 32, 128
 EXT = ROWS + 2 * HALO
 WIDE = 2 * LANES
-ROWS1, ROWS2 = 48, 24
+ROWS1, ROWS2 = EXT // 2, 24
 TILES = 11
 MIB = 1 << 20
 
@@ -46,9 +46,21 @@
     return pltpu.roll(x, step, 1)
 
 
+def by_halves(f, x):
+    return jnp.concatenate([f(x[:, start : start + LANES]) for start in range(0, x.shape[1], LANES)], axis=1)
+
+
+def near_next(x, step):
+    return by_halves(lambda h: lane_next(h, step), x)
+
+
+def near_prev(x, step):
+    return by_halves(lambda h: lane_prev(h, step), x)
+
+
 def pair_sum(x, level):
     step = 1 << level
-    return x + jnp.where(lane_bit(x.shape, level), lane_prev(x, step), lane_next(x, step))
+    return x + jnp.where(lane_bit(x.shape, level), near_prev(x, step), near_next(x, step))
 
 
 def beside(c, u, coeffs, m, odd, step):
@@ -98,7 +110,7 @@
 
 
 def first_kernel(
-    pressure_in, soil_in, storage_in, source_in, alpha_in, power_in, saturated_in, packed, to_sibling, to_other,
+    pressure_in, soil_in, storage_in, source_in, alpha_in, power_in, saturated_in, packed, to_sibling, to_other, to_pair, to_next,
     pressure, soil, storage, source, table, sems,
 ):
     copies = [
@@ -112,8 +124,10 @@
     ]
     for copy in copies:
         copy.start()
-    even = (position()[0] & 1) == 0
+    gx, gy = position()
+    even, even_y = (gx & 1) == 0, (gy & 1) == 0
     odd = odd_cells((ROWS, LANES), 0)
+    lane = iota((ROWS, LANES), 1)
     for copy in copies:
         copy.wait()
     rows = []
@@ -134,11 +148,16 @@
         outer = 1.0 - jnp.exp(exponent * (log_s - log_1s))
         return saturated * jnp.exp(-0.5 * exponent * log_1s) * outer * outer
 
-    def put(t, x):
+    def put(tile, m, x):
+        t = tile * PAIRS + m
         packed[t] = x
         high, low = x[ROWS - HALO :], x[:HALO]
         to_sibling[t] = jnp.where(even, high, low)
         to_other[t] = jnp.where(even, low, high)
+        left = pltpu.roll(x, HALO * m, 1) if m else x
+        right = pltpu.roll(x, (HALO * m - (LANES - HALO)) % LANES, 1)
+        for ref, y in ((to_pair, jnp.where(even_y, right, left)), (to_next, jnp.where(even_y, left, right))):
+            ref[tile] = y if m == 0 else jnp.where(lane >= HALO * m, y, ref[tile])
 
     for m in range(PAIRS):
         triples = (
@@ -147,27 +166,17 @@
             (source[2 * m], source[2 * m + 1]),
         )
         for q, (a, b) in enumerate(triples):
-            put(q * 10 + m, jnp.where(odd, b, a))
-            put(q * 10 + PAIRS + m, jnp.where(odd, a, b))
-
-
-def second_kernel(packed, from_sibling, from_other, to_pair, to_next):
-    gx, gy = position()
-    even_x, even_y = (gx & 1) == 0, (gy & 1) == 0
-    lane = iota((EXT, LANES), 1)
-    for tile in range(6):
-        pair, other = None, None
-        for m in range(PAIRS):
-            t = tile * PAIRS + m
-            sib, oth = from_sibling[t], from_other[t]
-            x = jnp.concatenate([jnp.where(even_x, oth, sib), packed[t], jnp.where(even_x, sib, oth)], axis=0)
-            left = pltpu.roll(x, HALO * m, 1) if m else x
-            right = pltpu.roll(x, (HALO * m - (LANES - HALO)) % LANES, 1)
-            a, b = jnp.where(even_y, right, left), jnp.where(even_y, left, right)
-            pair = a if pair is None else jnp.where(lane >= HALO * m, a, pair)
-            other = b if other is None else jnp.where(lane >= HALO * m, b, other)
-        to_pair[tile] = pair
-        to_next[tile] = other
+            put(2 * q, m, jnp.where(odd, b, a))
+            put(2 * q + 1, m, jnp.where(odd, a, b))
+
+
+def second_kernel(from_pair, from_next, to_sibling, to_other):
+    even = (position()[0] & 1) == 0
+    for q, ref in enumerate((from_pair, from_next)):
+        for tile in range(6):
+            high, low = ref[tile, ROWS - HALO :], ref[tile, :HALO]
+            to_sibling[6 * q + tile] = jnp.where(even, high, low)
+            to_other[6 * q + tile] = jnp.where(even, low, high)
 
 
 def coarsen_level(level, fine_rows, out_rows, fine, coarse):
@@ -185,24 +194,22 @@
     def odd_rows(ref, *ids):
         return ref[(*ids, pl.ds(1, half, stride=2))]
 
-    def put(ref, m, low, high):
-        ref[0, m, slice(0, half)] = jnp.where(odd, high, low)
-        ref[1, m, slice(0, half)] = jnp.where(odd, low, high)
+    swap = bit ^ odd
+
+    def put(ref, m, a, b):
+        ref[0, m, slice(0, half)] = a
+        ref[1, m, slice(0, half)] = b
 
     for m in range(PAIRS):
         u = even_rows(stor, 0, m) + odd_rows(stor, 1, m)
         v = even_rows(stor, 1, m) + odd_rows(stor, 0, m)
-        put(cstor, m, pair_sum(jnp.where(bit, v, u), level), pair_sum(jnp.where(bit, u, v), level))
+        put(cstor, m, pair_sum(jnp.where(swap, v, u), level), pair_sum(jnp.where(swap, u, v), level))
         e0, e1 = odd_rows(east, 0, m), odd_rows(east, 1, m)
-        put(ceast, m, pair_sum(jnp.where(bit, e0, e1), level), pair_sum(jnp.where(bit, e1, e0), level))
+        put(ceast, m, pair_sum(jnp.where(swap, e0, e1), level), pair_sum(jnp.where(swap, e1, e0), level))
         low = even_rows(north, 1, m) + odd_rows(north, 0, m)
         high = even_rows(north, 0, m) + odd_rows(north, 1, m)
-        put(
-            cnorth,
-            m,
-            jnp.where(bit, low, lane_next(low, step)),
-            jnp.where(bit, high, lane_next(high, step)),
-        )
+        a, b = jnp.where(odd, high, low), jnp.where(odd, low, high)
+        put(cnorth, m, jnp.where(bit, a, near_next(a, step)), jnp.where(bit, b, near_next(b, step)))
         cinner[m, slice(0, half)] = pair_sum(even_rows(inner, m) + odd_rows(inner, m), level)
         if m < PAIRS - 1:
             couter[m, slice(0, half)] = pair_sum(even_rows(outer, m) + odd_rows(outer, m), level)
@@ -213,13 +220,12 @@
     dims = (half, WIDE)
     bit = lane_bit(dims, level)
     odd = odd_cells(dims, level + 1, 1 if level == 2 else 0)
+    swap = bit ^ odd
     for m in range(PAIRS):
         a = residual[m, pl.ds(0, half, stride=2)]
         b = residual[m, pl.ds(1, half, stride=2)]
-        low = pair_sum(jnp.where(bit, b, a), level)
-        high = pair_sum(jnp.where(bit, a, b), level)
-        coarse_source[0, m, slice(0, half)] = jnp.where(odd, high, low)
-        coarse_source[1, m, slice(0, half)] = jnp.where(odd, low, high)
+        coarse_source[0, m, slice(0, half)] = pair_sum(jnp.where(swap, b, a), level)
+        coarse_source[1, m, slice(0, half)] = pair_sum(jnp.where(swap, a, b), level)
 
 
 def invert_diagonal(level, rows, coeffs, inverse):
@@ -248,7 +254,7 @@
 
 
 def third_kernel(
-    packed, from_sibling, from_other, from_pair, from_next,
+    packed, from_sibling, from_other, from_pair, from_next, corner_sibling, corner_other,
     source0, inv0, first0, east0, north0, inner0, outer0,
     source1, inv1, first1, east1, north1, inner1, outer1,
     source2, inv2, first2, east2, north2, inner2, outer2,
@@ -269,15 +275,20 @@
     gx, gy = position()
     even_x, even_y = (gx & 1) == 0, (gy & 1) == 0
     lane = iota((EXT, LANES), 1)
+
+    def rows_of(sib, oth, own):
+        return jnp.concatenate([jnp.where(even_x, oth, sib), own, jnp.where(even_x, sib, oth)], axis=0)
+
     for tile in range(6):
-        pair, other = from_pair[tile], from_next[tile]
+        pair, other = [
+            rows_of(corner_sibling[q + tile], corner_other[q + tile], ref[tile]) for q, ref in ((0, from_pair), (6, from_next))
+        ]
         right = jnp.where(even_y, pair, other)
         left = jnp.where(even_y, other, pair)
         ref = (cond, stor, src)[tile // 2]
         for m in range(PAIRS):
             t = tile * PAIRS + m
-            sib, oth = from_sibling[t], from_other[t]
-            x = jnp.concatenate([jnp.where(even_x, oth, sib), packed[t], jnp.where(even_x, sib, oth)], axis=0)
+            x = rows_of(from_sibling[t], from_other[t], packed[t])
             r = pltpu.roll(right, (-HALO * m) % LANES, 1) if m else right
             l = pltpu.roll(left, (LANES - HALO - HALO * m) % LANES, 1)
             h = jnp.where(lane < HALO, r, jnp.where(lane >= LANES - HALO, l, 0.0))
@@ -312,15 +323,15 @@
     invert_diagonal(0, EXT, level0, inv)
     descend_level(0, EXT, level0, inv, src, first, second, residual)
 
-    half = EXT // 2
-    for ref in (src1, e1, n1, in1, out1):
-        ref.ref[..., half:, :] = jnp.zeros((*ref.ref.shape[:-2], ROWS1 - half, LANES), jnp.float32)
-    stor1.ref[..., half:, :] = jnp.ones((2, PAIRS, 2, ROWS1 - half, LANES), jnp.float32)
     coarsen_level(0, EXT, ROWS1, level0, level1)
     restrict_level(0, EXT, residual, src1)
     invert_diagonal(1, ROWS1, level1, i1)
     descend_level(1, ROWS1, level1, i1, src1, f1, s1, r1)
 
+    half = ROWS1 // 2
+    for ref in (source2, east2, north2, inner2, outer2):
+        ref.ref[..., half:, :] = jnp.zeros((*ref.ref.shape[:-2], ROWS2 - half, LANES), jnp.float32)
+    stor2.ref[..., half:, :] = jnp.ones((2, PAIRS, 2, ROWS2 - half, LANES), jnp.float32)
     coarsen_level(1, ROWS1, ROWS2, level1, level2)
     restrict_level(1, ROWS1, r1, source2)
     invert_diagonal(2, ROWS2, level2, inv2)
@@ -384,8 +395,13 @@
     into[m, pl.ds(1, rows, stride=2)] = jnp.where(bit, low, high)
 
 
+def join_kernel(mine, sibling, both):
+    both[: 4 * TILES] = mine[...]
+    both[4 * TILES :] = sibling[...]
+
+
 def fourth_kernel(
-    mine, before, after, sib_mine, sib_before, sib_after, sums_in,
+    mine, sibling, received, passed_on, sums_in,
     source0, inv0, first0, east0, north0, inner0, outer0,
     source1, inv1, first1, east1, north1, inner1, outer1,
     source2, inv2, first2, east2, north2, inner2, outer2,
@@ -400,12 +416,16 @@
     ua2, ub2, ua1, ub1 = map(Wide, (ua2, ub2, ua1, ub1))
     f32 = jnp.float32
     even = (position()[0] & 1) == 0
-    for slot, (same, sib) in enumerate(((before, sib_before), (mine, sib_mine), (after, sib_after))):
-        a, b = same[...], sib[...]
-        low, high = jnp.where(even, a, b), jnp.where(even, b, a)
+    size = 4 * TILES
+    own, sib = mine[...], sibling[...]
+    direct, relayed = received[...], passed_on[...]
+    before, after = jnp.where(even, direct, relayed), jnp.where(even, relayed, direct)
+    blocks = (
+        before[size:], before[:size], jnp.where(even, own, sib), jnp.where(even, sib, own), after[:size], after[size:],
+    )
+    for slot, block in enumerate(blocks):
         for q in range(TILES):
-            whole[q, 8 * slot : 8 * slot + 4] = low[4 * q : 4 * q + 4]
-            whole[q, 8 * slot + 4 : 8 * slot + 8] = high[4 * q : 4 * q + 4]
+            whole[q, 4 * slot : 4 * slot + 4] = block[4 * q : 4 * q + 4]
     own_f, own_s = sums_in[0:1, 0:1], sums_in[1:2, 0:1]
     guess = own_f / own_s
     g0, g1, h0, i30, i31, e30, e31, n30, n31, in3, out3 = [whole[q] for q in range(TILES)]
@@ -430,10 +450,10 @@
     second_half = lane_bit(dims3, 1)
 
     def spread(x, m):
-        x = jnp.where(phase == 0, lane_next(x, m) if m else x, 0.0)
-        x = x + lane_prev(x, 1)
-        x = x + lane_prev(x, 2)
-        return x + lane_prev(x, 4)
+        x = jnp.where(phase == 0, near_next(x, m) if m else x, 0.0)
+        x = x + near_prev(x, 1)
+        x = x + near_prev(x, 2)
+        return x + near_prev(x, 4)
 
     for m in range(PAIRS):
         x0 = jnp.where(second_half, spread(b0, m), spread(a0, m))
@@ -458,8 +478,8 @@
     bit1, bit0 = lane_bit(dims2, 1), lane_bit(dims2, 0)
 
     def regroup2(x):
-        a = jnp.where(bit1, lane_prev(x, 2), x)
-        b = jnp.where(bit1, x, lane_next(x, 2))
+        a = jnp.where(bit1, near_prev(x, 2), x)
+        b = jnp.where(bit1, x, near_next(x, 2))
         return jnp.where(bit0, b, a)
 
     for m in range(PAIRS):
@@ -475,8 +495,8 @@
         x0, x1 = ua1[m], ub1[m]
         low, high = jnp.where(odd1, x1, x0), jnp.where(odd1, x0, x1)
         for work, pick in (
-            (work0a, lambda x: jnp.where(bit0, lane_prev(x, 1), x)),
-            (work0b, lambda x: jnp.where(bit0, x, lane_next(x, 1))),
+            (work0a, lambda x: jnp.where(bit0, near_prev(x, 1), x)),
+            (work0b, lambda x: jnp.where(bit0, x, near_next(x, 1))),
         ):
             spread_rows(0, pick(low), pick(high), work, m)
 
@@ -514,8 +534,8 @@
         acc = [x + y for x, y in zip(acc, terms, strict=True)]
         for t, x in enumerate((p0, p1, q0, q1, r0, r1, img_a, img_b)):
             fields[t, m] = x
-    lane = iota((1, 16), 1)
-    line = jnp.zeros((1, 16), f32)
+    lane = iota((1, LANES), 1)
+    line = jnp.zeros((1, LANES), f32)
     for q, x in enumerate(acc):
         line = jnp.where(lane == q, jnp.sum(x, keepdims=True), line)
     line = jnp.where(lane == 11, own_f, line)
@@ -524,8 +544,8 @@
     sums[...] = jnp.broadcast_to(line, sums.shape)
 
 
-def last_kernel(sums, fields, solution_out, residual_out, norm_ref, solution_ref, residual_ref, sems, *, cells):
-    x = sums[...]
+def last_kernel(sums, line, fields, solution_out, residual_out, norm_ref, solution_ref, residual_ref, sems, *, cells):
+    x = jnp.concatenate([sums[:, :16], sums[:, 16:]], axis=0)
 
     def column(q):
         return x[:, q : q + 1]
@@ -540,9 +560,7 @@
     s, t = step - 1.0, step * shift
     squares = total(dd - 2.0 * s * da + s * s * aa - 2.0 * t * db + 2.0 * s * t * ab + t * t * bb)
     norm_ref[...] = jnp.sqrt(jnp.maximum(squares, 0.0) / cells)
-    gx, gy = position()
-    mine = gx * lax.axis_size("gy") + gy
-    here = total(jnp.where(iota(shift.shape, 0) == mine, shift, 0.0))
+    here = mean - line[0:1, 13:14]
     odd = odd_cells((ROWS, LANES), 0)
     copies = []
     for m in range(PAIRS):
@@ -587,22 +605,21 @@
 def shards(pressure, soil, vg_alpha, vg_n, sat_cond, storage, right_side):
     count_x, count_y = lax.axis_size("gx"), lax.axis_size("gy")
     block, slab = scratch(2 * PAIRS, ROWS, LANES), shape(6 * PAIRS, HALO, LANES)
+    side, corner = shape(6, ROWS, LANES), shape(12, HALO, LANES)
     arguments = (pressure, soil, storage, right_side, *[v.reshape(1, NSOIL) for v in (vg_alpha, vg_n, sat_cond)])
-    packed, to_sibling, to_other = pl.pallas_call(
-        first_kernel, out_shape=(shape(6 * PAIRS, ROWS, LANES), slab, slab),
-        in_specs=[HBM] * 7, out_specs=(VM, VM, VM),
+    packed, *slabs = pl.pallas_call(
+        first_kernel, out_shape=(shape(6 * PAIRS, ROWS, LANES), slab, slab, side, side),
+        in_specs=[HBM] * 7, out_specs=(VM,) * 5,
         scratch_shapes=[
             block, pltpu.VMEM((2 * PAIRS, ROWS, LANES), jnp.int32), block, block, scratch(3, 1, NSOIL), pltpu.SemaphoreType.DMA((7,)),
         ],
         compiler_params=params(4), name="conductivity",
     )(*[pltpu.with_memory_space_constraint(v, pltpu.MemorySpace.HBM) for v in arguments])
-    from_sibling, from_other = pair_exchange((to_sibling, to_other), "gx")
-    slab = shape(6, EXT, LANES)
-    to_pair, to_next = pl.pallas_call(
-        second_kernel, out_shape=(slab, slab), in_specs=[VM, VM, VM], out_specs=(VM, VM),
-        compiler_params=params(4), name="slabs",
-    )(packed, from_sibling, from_other)
-    from_pair, from_next = pair_exchange((to_pair, to_next), "gy")
+    halos = pair_exchange(slabs[:2], "gx") + pair_exchange(slabs[2:], "gy")
+    corners = pl.pallas_call(
+        second_kernel, out_shape=(corner, corner), in_specs=[VM, VM], out_specs=(VM, VM), compiler_params=params(2), name="corners",
+    )(*halos[2:])
+    halos = halos + pair_exchange(corners, "gx")
 
     def sized(rows):
         return [scratch(*dims) for dims in level_dims(rows)]
@@ -614,7 +631,7 @@
     out = pl.pallas_call(
         third_kernel,
         out_shape=(*level_shapes(48), *level_shapes(24), *level_shapes(ROWS2), shape(4 * TILES, LANES), shape(8, LANES)),
-        in_specs=[VM] * 5, out_specs=(VM,) * 23,
+        in_specs=[VM] * 7, out_specs=(VM,) * 23,
         scratch_shapes=[
             two, two, two, two, two, one, four, two, one, one, one,
             two1, two1, two1, two1, one1, four1, two1, one1, one1, one1,
@@ -622,39 +639,45 @@
             two3, two3, two3, two3, one3, four3,
         ],
         compiler_params=params(12), name="descent",
-    )(packed, from_sibling, from_other, from_pair, from_next)
+    )(packed, *halos)
     levels, tiles, sums = out[:21], out[21], out[22]
 
     tile_pair, tile_next = pair_exchange((tiles, tiles), "gy")
     window = pl.pallas_call(
         window_kernel, out_shape=shape(4 * TILES, WIDE), in_specs=[VM] * 3, out_specs=VM, compiler_params=params(2), name="window",
     )(tiles, tile_pair, tile_next)
-    sibling = pairs_of(count_x, 0)
-    before = lax.ppermute(window, "gx", [(i, i + 2) for i in range(count_x - 2)])
-    after = lax.ppermute(window, "gx", [(i + 2, i) for i in range(count_x - 2)])
-    blocks = (window, before, after, *[lax.ppermute(x, "gx", sibling) for x in (window, before, after)])
+    sibling = lax.ppermute(window, "gx", pairs_of(count_x, 0))
+    both = pl.pallas_call(
+        join_kernel, out_shape=shape(8 * TILES, WIDE), in_specs=[VM] * 2, out_specs=VM, compiler_params=params(2), name="join",
+    )(window, sibling)
+    received = lax.ppermute(both, "gx", pairs_of(count_x, 1))
+    passed_on = lax.ppermute(received, "gx", pairs_of(count_x, 0))
+    blocks = (window, sibling, received, passed_on)
 
     devices = count_x * count_y
-    fields, partial = pl.pallas_call(
+    fields, line = pl.pallas_call(
         fourth_kernel,
-        out_shape=(shape(8, PAIRS, ROWS, LANES), shape(devices, 16)),
-        in_specs=[VM] * 28, out_specs=(VM, VM),
+        out_shape=(shape(8, PAIRS, ROWS, LANES), shape(8, LANES)),
+        in_specs=[VM] * 26, out_specs=(VM, VM),
         scratch_shapes=[
             scratch(TILES, 24, WIDE), sized(ROWS2)[1], sized(24)[1],
             *[sized(48)[1]] * 6, *[sized(24)[1]] * 4,
         ],
         compiler_params=params(8), name="ascent",
     )(*blocks, sums, *levels)
-    every = lax.all_to_all(partial, ("gx", "gy"), 0, 0, tiled=True)
+    both = jnp.concatenate([line[:1, :16], lax.ppermute(line, "gx", pairs_of(count_x, 0))[:1, :16]], axis=1)
+    kinds = [[x * count_y + y for x in range(c, count_x, 2) for y in range(count_y)] for c in range(2)]
+    both = jnp.broadcast_to(both, (devices // 2, 32))
+    every = lax.all_to_all(both, ("gx", "gy"), 0, 0, axis_index_groups=kinds, tiled=True)
 
     layers = 2 * PAIRS
     out = shape(layers, ROWS, LANES)
     solution_out, residual_out, norm = pl.pallas_call(
         functools.partial(last_kernel, cells=float(layers * ROWS * LANES * devices)),
-        out_shape=(out, out, shape(1, 1)), in_specs=[VM, VM], out_specs=(HBM, HBM, VM),
+        out_shape=(out, out, shape(1, 1)), in_specs=[VM, VM, VM], out_specs=(HBM, HBM, VM),
         scratch_shapes=[scratch(*out.shape), scratch(*out.shape), pltpu.SemaphoreType.DMA((2, PAIRS))],
         compiler_params=params(4), name="outputs",
-    )(every, fields)
+    )(every, line, fields)
     return solution_out, residual_out, norm.reshape(1)
 
 

time: 73.3 us -> 70.6 us (0.963)
  waiting for transfers between devices: 8.71 us -> 6.75 us
  blocking collectives: 22.7 us -> 21.9 us
    ppermute x6 -> x8, starting transfers between devices: 12.9 us -> 15.1 us  [pair_exchange(): lax.ppermute(x_i, axis, pairs_of(count, first))]
    ppermute x6 -> x8, waiting for transfers between devices: 6.32 us -> 4.11 us  [pair_exchange(): lax.ppermute(x_i, axis, pairs_of(count, first))]
    ppermute x5 -> x4, starting transfers between devices: 15 us -> 13.3 us  [the longest x1 6.66 us: shards(): passed_on = lax.ppermute(received, 'gx', pairs_of(count_x, 0))]
    all_to_all x1, blocking collectives: 22.7 us -> 21.9 us  [shards(): lax.all_to_all(both, ('gx', 'gy'), 0, 0, axis_index_groups=kinds, tiled=T...]
    ppermute x5 -> x4, waiting for transfers between devices: 2.4 us -> 2.64 us  [the longest x1 0.93 us: shards(): passed_on = lax.ppermute(received, 'gx', pairs_of(count_x, 0))]
  transfers between devices with their start and end apart: 11 -> 12, of which waited for: 5 -> 6; matrix products, arithmetic and copies ran while one was open for 0% -> 0% of each run, Pallas kernels for 0% -> 0%
where the time goes in v3:
time: 70.6 us; the launch traced here: 70.3 us
  starting transfers between devices  28.5 us (40%)
  blocking collectives  21.9 us (31%)
  Pallas kernels  12.3 us (17%)
  waiting for transfers between devices  6.75 us (10%)
  between operations  0.74 us (1%)
    all_to_all x1, blocking collectives, shards(): lax.all_to_all(both, ('gx', 'gy'), 0, 0, axis_index_groups=kinds, tiled=T...  21.9 us
    ppermute x8, starting transfers between devices, pair_exchange(): lax.ppermute(x_i, axis, pairs_of(count, first))  15.1 us
    ppermute x1, starting transfers between devices, shards(): passed_on = lax.ppermute(received, 'gx', pairs_of(count_x, 0))  6.66 us
    ppermute x1, starting transfers between devices, shards(): sibling = lax.ppermute(window, 'gx', pairs_of(count_x, 0))  5.56 us
    pallas_call x1, Pallas kernels, shards(): pl.pallas_call(third_kernel, out_shape=(*level_shapes(48), *level_shapes(...  4.87 us
    ppermute x8, waiting for transfers between devices, pair_exchange(): lax.ppermute(x_i, axis, pairs_of(count, first))  4.11 us
    pallas_call x1, Pallas kernels, shards(): pl.pallas_call(fourth_kernel, out_shape=(shape(8, PAIRS, ROWS, LANES), sh...  3.18 us
    pallas_call x1, Pallas kernels, shards(): pl.pallas_call(first_kernel, out_shape=(shape(6 * PAIRS, ROWS, LANES), sl...  2.18 us
  transfers between devices with their start and end apart: 12, of which 6 were waited for; matrix products, arithmetic and copies ran while one was open for 0% of the time, Pallas kernels for 0%

profile of v3, /device:TPU:0, one launch (start us, length us, event | category | flops | bytes accessed | tf_op | source)
XLA Modules:
  0.0 70.3 jit_solution(5396565752291879110)
XLA Ops:
  0.6 2.2 %conductivity.1 = (f32[30,32,128]{2,1,0:T(8,128)S(1)}, f32[30,24,128]{2,1,0:T(8,128)S(1)}, f32[30,24,128]{2,1,0:T(8,128)S(1)}, f32[6,32,128]{2,1,0:T(8,128)S(1)}, f32[6,32,128]{2,1,0:T(8,128)S(1)}) custom-call(f32[10,32,128]{2,1,0:T(8,128)} %pressure_in.1, s32[10,32,128]{2,1,0:T(8,128)} %soil_in.1, f32[10,32,128]{2,1,0:T(8,128)} %storage_in.1, ...), custom_call_target="tpu_custom_call" | custom-call | tf_op jit(solution)/shard_map/conductivity/pallas_call | solution.py:610
  2.8 0.1 collective-permute-start
  2.9 0.7 collective-permute-start.1
  3.6 2.1 %collective-permute-start.2 = (f32[6,32,128]{2,1,0:T(8,128)S(1)}, f32[6,32,128]{2,1,0:T(8,128)S(1)}, u32[]{:S(2)}, u32[]{:S(2)}) collective-permute-start(f32[6,32,128]{2,1,0:T(8,128)S(1)} %get-tuple-element.41), channel_id=1, source_target_pairs={{0,1},{2,3},{4,5},{6,7},{8,9},{10,11},{12,13},{14,15},{1,0},{3,2},... | collective-permute-start | bytes 294920 | tf_op jit(solution)/shard_map/ppermute | solution.py:602
  5.7 0.7 collective-permute-start.3
  6.4 2.0 %collective-permute-done.2.from_pair = f32[6,32,128]{2,1,0:T(8,128)S(1)} collective-permute-done((f32[6,32,128]{2,1,0:T(8,128)S(1)}, f32[6,32,128]{2,1,0:T(8,128)S(1)}, u32[]{:S(2)}, u32[]{:S(2)}) %collective-permute-start.2) | collective-permute-done | bytes 98336 | tf_op jit(solution)/shard_map/ppermute | solution.py:602
  8.3 2.1 %collective-permute-start.4 = (f32[12,24,128]{2,1,0:T(8,128)S(1)}, f32[12,24,128]{2,1,0:T(8,128)S(1)}, u32[]{:S(2)}, u32[]{:S(2)}) collective-permute-start(f32[12,24,128]{2,1,0:T(8,128)S(1)} %get-tuple-element.43), channel_id=1, source_target_pairs={{0,16},{32,48},{64,80},{96,112},{16,0},{48,32},{80,64},{112,96},{1... | collective-permute-start | bytes 442376 | tf_op jit(solution)/shard_map/ppermute | solution.py:602
  10.5 0.7 collective-permute-start.5
  11.1 0.3 collective-permute-done.4.corner_sibling
  11.5 4.9 %descent.1 = (f32[2,5,2,48,128]{4,3,2,1,0:T(8,128)S(1)}, f32[2,5,2,48,128]{4,3,2,1,0:T(8,128)S(1)}, f32[5,2,48,128]{3,2,1,0:T(8,128)S(1)}, f32[2,5,2,48,128]{4,3...) custom-call(f32[30,32,128]{2,1,0:T(8,128)S(1)} %get-tuple-element.38, ...), custom_call_target="tpu_custom_call" | custom-call | tf_op jit(solution)/shard_map/descent/pallas_call | solution.py:631
  16.3 0.7 collective-permute-start.7
  17.0 8.2 %collective-permute-start.6 = (f32[44,128]{1,0:T(8,128)S(1)}, f32[44,128]{1,0:T(8,128)S(1)}, u32[]{:S(2)}, u32[]{:S(2)}) collective-permute-start(f32[44,128]{1,0:T(8,128)S(1)} %get-tuple-element.45.tiles), channel_id=1, source_target_pairs={{0,1},{2,3},{4,5},{6,7},{8,9},{10,11},{12,13},{14,15},{1,0},{3,2},... | collective-permute-start | bytes 67592 | tf_op jit(solution)/shard_map/ppermute | solution.py:602
  25.2 1.8 %collective-permute-done.6.from_pair = f32[44,128]{1,0:T(8,128)S(1)} collective-permute-done((f32[44,128]{1,0:T(8,128)S(1)}, f32[44,128]{1,0:T(8,128)S(1)}, u32[]{:S(2)}, u32[]{:S(2)}) %collective-permute-start.6) | collective-permute-done | bytes 22560 | tf_op jit(solution)/shard_map/ppermute | solution.py:602
  27.0 5.6 %collective-permute-start.8 = (f32[44,256]{1,0:T(8,128)S(1)}, f32[44,256]{1,0:T(8,128)S(1)}, u32[]{:S(2)}, u32[]{:S(2)}) collective-permute-start(f32[44,256]{1,0:T(8,128)S(1)} %window.1.mine), channel_id=1, source_target_pairs={{0,16},{32,48},{64,80},{96,112},{16,0},{48,32},{80,64},{112,96},{1... | collective-permute-start | bytes 135176 | tf_op jit(solution)/shard_map/ppermute | solution.py:649
  32.6 0.9 %collective-permute-done.8.sibling = f32[44,256]{1,0:T(8,128)S(1)} collective-permute-done((f32[44,256]{1,0:T(8,128)S(1)}, f32[44,256]{1,0:T(8,128)S(1)}, u32[]{:S(2)}, u32[]{:S(2)}) %collective-permute-start.8) | collective-permute-done | bytes 45088 | tf_op jit(solution)/shard_map/ppermute | solution.py:649
  33.5 0.7 collective-permute-start.9
  34.2 6.7 %collective-permute-start.10 = (f32[88,256]{1,0:T(8,128)S(1)}, f32[88,256]{1,0:T(8,128)S(1)}, u32[]{:S(2)}, u32[]{:S(2)}) collective-permute-start(f32[88,256]{1,0:T(8,128)S(1)} %collective-permute-done.9.received), channel_id=1, source_target_pairs={{0,16},{32,48},{64,80},{96,112},{16,0},{48,32},{80,64},{112,96},{1... | collective-permute-start | bytes 270344 | tf_op jit(solution)/shard_map/ppermute | solution.py:654
  40.8 0.9 %collective-permute-done.10.passed_on = f32[88,256]{1,0:T(8,128)S(1)} collective-permute-done((f32[88,256]{1,0:T(8,128)S(1)}, f32[88,256]{1,0:T(8,128)S(1)}, u32[]{:S(2)}, u32[]{:S(2)}) %collective-permute-start.10) | collective-permute-done | bytes 90144 | tf_op jit(solution)/shard_map/ppermute | solution.py:654
  41.8 3.2 %ascent.1 = (f32[8,5,32,128]{3,2,1,0:T(8,128)S(1)}, f32[8,128]{1,0:T(8,128)S(1)}) custom-call(f32[44,256]{1,0:T(8,128)S(1)} %window.1.mine, f32[44,256]{1,0:T(8,128)S(1)} %collective-permute-done.8.sibling, f32[88,256]{1,0:T(8,128)S(1)} %collective-permute-done.9.received, f32[88,256]{1,0:T(8,128)S(1)} %collective-permute-done.10.passed_on, ...), custom_call_target="tpu_custom_call" | custom-call | tf_op jit(solution)/shard_map/ascent/pallas_call | solution.py:658
  45.0 0.4 collective-permute-start.11
  45.4 0.8 %collective-permute-done.11 = f32[8,128]{1,0:T(8,128)S(1)} collective-permute-done((f32[8,128]{1,0:T(8,128)S(1)}, f32[8,128]{1,0:T(8,128)S(1)}, u32[]{:S(2)}, u32[]{:S(2)}) %collective-permute-start.11) | collective-permute-done | bytes 4128 | tf_op jit(solution)/shard_map/ppermute | solution.py:668
  46.2 0.1 maximum_bitcast_fusion
  46.3 21.9 %all_to_all.8 = f32[64,1,32]{2,1,0:T(1,128)S(1)} all-to-all(f32[64,1,32]{2,1,0:T(1,128)S(1)} %broadcast_in_dim.2), channel_id=1, replica_groups={{0,1,2,3,4,5,6,7,8,9,10,11,12,13,14,15,32,33,34,35,36,37,38,39,40,41,42..., dimensions={0} | all-to-all | bytes 16384 | tf_op jit(solution)/shard_map/all_to_all | solution.py:671
  68.3 2.0 %outputs.1 = (f32[10,32,128]{2,1,0:T(8,128)}, f32[10,32,128]{2,1,0:T(8,128)}, f32[1,1]{1,0:T(1,128)}) custom-call(f32[64,32]{1,0:T(8,128)S(1)} %bitcast.7, f32[8,128]{1,0:T(8,128)S(1)} %get-tuple-element.68.line, f32[8,5,32,128]{3,2,1,0:T(8,128)S(1)} %get-tuple-element.69.fields), custom_call_target="tpu_custom_call" | custom-call | tf_op jit(solution)/shard_map/outputs/pallas_call | solution.py:675
  (12 shorter events, 0.1 us)
Async XLA Ops:
  2.8 8.6 %collective-permute-start = (f32[30,24,128]{2,1,0:T(8,128)S(1)}, f32[30,24,128]{2,1,0:T(8,128)S(1)}, u32[]{:S(2)}, u32[]{:S(2)}) collective-permute-start(f32[30,24,128]{2,1,0:T(8,128)S(1)} %get-tuple-element.39), channel_id=1, source_target_pairs={{0,16},{32,48},{64,80},{96,112},{16,0},{48,32},{80,64},{112,96},{1... | collective-permute-start | bytes 1105928 | tf_op jit(solution)/shard_map/ppermute | solution.py:602
  2.9 8.6 %collective-permute-start.1 = (f32[30,24,128]{2,1,0:T(8,128)S(1)}, f32[30,24,128]{2,1,0:T(8,128)S(1)}, u32[]{:S(2)}, u32[]{:S(2)}) collective-permute-start(f32[30,24,128]{2,1,0:T(8,128)S(1)} %get-tuple-element.40), channel_id=1, source_target_pairs={{16,32},{48,64},{80,96},{32,16},{64,48},{96,80},{17,33},{49,65},{8... | collective-permute-start | bytes 1105928 | tf_op jit(solution)/shard_map/ppermute | solution.py:602
  3.6 4.7 %collective-permute-start.2 = (f32[6,32,128]{2,1,0:T(8,128)S(1)}, f32[6,32,128]{2,1,0:T(8,128)S(1)}, u32[]{:S(2)}, u32[]{:S(2)}) collective-permute-start(f32[6,32,128]{2,1,0:T(8,128)S(1)} %get-tuple-element.41), channel_id=1, source_target_pairs={{0,1},{2,3},{4,5},{6,7},{8,9},{10,11},{12,13},{14,15},{1,0},{3,2},... | collective-permute-start | bytes 294920 | tf_op jit(solution)/shard_map/ppermute | solution.py:602
  5.7 2.6 %collective-permute-start.3 = (f32[6,32,128]{2,1,0:T(8,128)S(1)}, f32[6,32,128]{2,1,0:T(8,128)S(1)}, u32[]{:S(2)}, u32[]{:S(2)}) collective-permute-start(f32[6,32,128]{2,1,0:T(8,128)S(1)} %get-tuple-element.42), channel_id=1, source_target_pairs={{1,2},{3,4},{5,6},{7,8},{9,10},{11,12},{13,14},{2,1},{4,3},{6,5},{... | collective-permute-start | bytes 294920 | tf_op jit(solution)/shard_map/ppermute | solution.py:602
  8.3 3.1 %collective-permute-start.4 = (f32[12,24,128]{2,1,0:T(8,128)S(1)}, f32[12,24,128]{2,1,0:T(8,128)S(1)}, u32[]{:S(2)}, u32[]{:S(2)}) collective-permute-start(f32[12,24,128]{2,1,0:T(8,128)S(1)} %get-tuple-element.43), channel_id=1, source_target_pairs={{0,16},{32,48},{64,80},{96,112},{16,0},{48,32},{80,64},{112,96},{1... | collective-permute-start | bytes 442376 | tf_op jit(solution)/shard_map/ppermute | solution.py:602
  10.5 1.0 %collective-permute-start.5 = (f32[12,24,128]{2,1,0:T(8,128)S(1)}, f32[12,24,128]{2,1,0:T(8,128)S(1)}, u32[]{:S(2)}, u32[]{:S(2)}) collective-permute-start(f32[12,24,128]{2,1,0:T(8,128)S(1)} %get-tuple-element.44), channel_id=1, source_target_pairs={{16,32},{48,64},{80,96},{32,16},{64,48},{96,80},{17,33},{49,65},{8... | collective-permute-start | bytes 442376 | tf_op jit(solution)/shard_map/ppermute | solution.py:602
  16.3 8.9 %collective-permute-start.7 = (f32[44,128]{1,0:T(8,128)S(1)}, f32[44,128]{1,0:T(8,128)S(1)}, u32[]{:S(2)}, u32[]{:S(2)}) collective-permute-start(f32[44,128]{1,0:T(8,128)S(1)} %get-tuple-element.45.tiles), channel_id=1, source_target_pairs={{1,2},{3,4},{5,6},{7,8},{9,10},{11,12},{13,14},{2,1},{4,3},{6,5},{... | collective-permute-start | bytes 67592 | tf_op jit(solution)/shard_map/ppermute | solution.py:602
  17.0 10.0 %collective-permute-start.6 = (f32[44,128]{1,0:T(8,128)S(1)}, f32[44,128]{1,0:T(8,128)S(1)}, u32[]{:S(2)}, u32[]{:S(2)}) collective-permute-start(f32[44,128]{1,0:T(8,128)S(1)} %get-tuple-element.45.tiles), channel_id=1, source_target_pairs={{0,1},{2,3},{4,5},{6,7},{8,9},{10,11},{12,13},{14,15},{1,0},{3,2},... | collective-permute-start | bytes 67592 | tf_op jit(solution)/shard_map/ppermute | solution.py:602
  27.0 6.4 %collective-permute-start.8 = (f32[44,256]{1,0:T(8,128)S(1)}, f32[44,256]{1,0:T(8,128)S(1)}, u32[]{:S(2)}, u32[]{:S(2)}) collective-permute-start(f32[44,256]{1,0:T(8,128)S(1)} %window.1.mine), channel_id=1, source_target_pairs={{0,16},{32,48},{64,80},{96,112},{16,0},{48,32},{80,64},{112,96},{1... | collective-permute-start | bytes 135176 | tf_op jit(solution)/shard_map/ppermute | solution.py:649
  33.5 0.7 collective-permute-start.9
  34.2 7.6 %collective-permute-start.10 = (f32[88,256]{1,0:T(8,128)S(1)}, f32[88,256]{1,0:T(8,128)S(1)}, u32[]{:S(2)}, u32[]{:S(2)}) collective-permute-start(f32[88,256]{1,0:T(8,128)S(1)} %collective-permute-done.9.received), channel_id=1, source_target_pairs={{0,16},{32,48},{64,80},{96,112},{16,0},{48,32},{80,64},{112,96},{1... | collective-permute-start | bytes 270344 | tf_op jit(solution)/shard_map/ppermute | solution.py:654
  45.0 1.3 %collective-permute-start.11 = (f32[8,128]{1,0:T(8,128)S(1)}, f32[8,128]{1,0:T(8,128)S(1)}, u32[]{:S(2)}, u32[]{:S(2)}) collective-permute-start(f32[8,128]{1,0:T(8,128)S(1)} %get-tuple-element.68.line), channel_id=1, source_target_pairs={{0,16},{32,48},{64,80},{96,112},{16,0},{48,32},{80,64},{112,96},{1... | collective-permute-start | bytes 12296 | tf_op jit(solution)/shard_map/ppermute | solution.py:668

commit v4 on v3

--- a/solution.py
+++ b/solution.py
@@ -110,7 +110,7 @@
 
 
 def first_kernel(
-    pressure_in, soil_in, storage_in, source_in, alpha_in, power_in, saturated_in, packed, to_sibling, to_other, to_pair, to_next,
+    pressure_in, soil_in, storage_in, source_in, alpha_in, power_in, saturated_in, packed, to_pair, to_next,
     pressure, soil, storage, source, table, sems,
 ):
     copies = [
@@ -124,8 +124,7 @@
     ]
     for copy in copies:
         copy.start()
-    gx, gy = position()
-    even, even_y = (gx & 1) == 0, (gy & 1) == 0
+    even_y = (position()[1] & 1) == 0
     odd = odd_cells((ROWS, LANES), 0)
     lane = iota((ROWS, LANES), 1)
     for copy in copies:
@@ -151,9 +150,6 @@
     def put(tile, m, x):
         t = tile * PAIRS + m
         packed[t] = x
-        high, low = x[ROWS - HALO :], x[:HALO]
-        to_sibling[t] = jnp.where(even, high, low)
-        to_other[t] = jnp.where(even, low, high)
         left = pltpu.roll(x, HALO * m, 1) if m else x
         right = pltpu.roll(x, (HALO * m - (LANES - HALO)) % LANES, 1)
         for ref, y in ((to_pair, jnp.where(even_y, right, left)), (to_next, jnp.where(even_y, left, right))):
@@ -168,6 +164,14 @@
         for q, (a, b) in enumerate(triples):
             put(2 * q, m, jnp.where(odd, b, a))
             put(2 * q + 1, m, jnp.where(odd, a, b))
+
+
+def edge_kernel(packed, to_sibling, to_other):
+    even = (position()[0] & 1) == 0
+    for t in range(6 * PAIRS):
+        high, low = packed[t, ROWS - HALO :], packed[t, :HALO]
+        to_sibling[t] = jnp.where(even, high, low)
+        to_other[t] = jnp.where(even, low, high)
 
 
 def second_kernel(from_pair, from_next, to_sibling, to_other):
@@ -607,18 +611,22 @@
     block, slab = scratch(2 * PAIRS, ROWS, LANES), shape(6 * PAIRS, HALO, LANES)
     side, corner = shape(6, ROWS, LANES), shape(12, HALO, LANES)
     arguments = (pressure, soil, storage, right_side, *[v.reshape(1, NSOIL) for v in (vg_alpha, vg_n, sat_cond)])
-    packed, *slabs = pl.pallas_call(
-        first_kernel, out_shape=(shape(6 * PAIRS, ROWS, LANES), slab, slab, side, side),
-        in_specs=[HBM] * 7, out_specs=(VM,) * 5,
+    packed, *sides = pl.pallas_call(
+        first_kernel, out_shape=(shape(6 * PAIRS, ROWS, LANES), side, side),
+        in_specs=[HBM] * 7, out_specs=(VM,) * 3,
         scratch_shapes=[
             block, pltpu.VMEM((2 * PAIRS, ROWS, LANES), jnp.int32), block, block, scratch(3, 1, NSOIL), pltpu.SemaphoreType.DMA((7,)),
         ],
         compiler_params=params(4), name="conductivity",
     )(*[pltpu.with_memory_space_constraint(v, pltpu.MemorySpace.HBM) for v in arguments])
-    halos = pair_exchange(slabs[:2], "gx") + pair_exchange(slabs[2:], "gy")
+    beside_y = pair_exchange(sides, "gy")
+    slabs = pl.pallas_call(
+        edge_kernel, out_shape=(slab, slab), in_specs=[VM], out_specs=(VM, VM), compiler_params=params(2), name="edges",
+    )(packed)
+    halos = pair_exchange(slabs, "gx") + beside_y
     corners = pl.pallas_call(
         second_kernel, out_shape=(corner, corner), in_specs=[VM, VM], out_specs=(VM, VM), compiler_params=params(2), name="corners",
-    )(*halos[2:])
+    )(*beside_y)
     halos = halos + pair_exchange(corners, "gx")
 
     def sized(rows):
@@ -666,7 +674,7 @@
         compiler_params=params(8), name="ascent",
     )(*blocks, sums, *levels)
     both = jnp.concatenate([line[:1, :16], lax.ppermute(line, "gx", pairs_of(count_x, 0))[:1, :16]], axis=1)
-    kinds = [[x * count_y + y for x in range(c, count_x, 2) for y in range(count_y)] for c in range(2)]
+    kinds = [[x * count_y + y for x in range(c, count_x, 2) for y in range(count_y)][::-1] for c in range(2)]
     both = jnp.broadcast_to(both, (devices // 2, 32))
     every = lax.all_to_all(both, ("gx", "gy"), 0, 0, axis_index_groups=kinds, tiled=True)
 

time: 70.6 us -> 68.1 us (0.965)
  blocking collectives: 21.9 us -> 19.4 us
    all_to_all x1, blocking collectives: 21.9 us -> 19.4 us  [shards(): lax.all_to_all(both, ('gx', 'gy'), 0, 0, axis_index_groups=kinds, tiled=T...]
    pallas_call x1 -> x2, Pallas kernels: 2.18 us -> 2.24 us  [the longest x1 2.18 us: shards(): pl.pallas_call(first_kernel, out_shape=(shape(6 * PAIRS, ROWS, LANES), si...]
where the time goes in v4:
time: 68.1 us; the launch traced here: 67.8 us
  starting transfers between devices  28.5 us (42%)
  blocking collectives  19.4 us (28%)
  Pallas kernels  12.4 us (18%)
  waiting for transfers between devices  6.75 us (10%)
  between operations  0.75 us (1%)
    all_to_all x1, blocking collectives, shards(): lax.all_to_all(both, ('gx', 'gy'), 0, 0, axis_index_groups=kinds, tiled=T...  19.4 us
    ppermute x8, starting transfers between devices, pair_exchange(): lax.ppermute(x_i, axis, pairs_of(count, first))  15.1 us
    ppermute x1, starting transfers between devices, shards(): passed_on = lax.ppermute(received, 'gx', pairs_of(count_x, 0))  6.66 us
    ppermute x1, starting transfers between devices, shards(): sibling = lax.ppermute(window, 'gx', pairs_of(count_x, 0))  5.56 us
    pallas_call x1, Pallas kernels, shards(): pl.pallas_call(third_kernel, out_shape=(*level_shapes(48), *level_shapes(...  4.89 us
    ppermute x8, waiting for transfers between devices, pair_exchange(): lax.ppermute(x_i, axis, pairs_of(count, first))  4.11 us
    pallas_call x1, Pallas kernels, shards(): pl.pallas_call(fourth_kernel, out_shape=(shape(8, PAIRS, ROWS, LANES), sh...  3.18 us
    pallas_call x1, Pallas kernels, shards(): pl.pallas_call(first_kernel, out_shape=(shape(6 * PAIRS, ROWS, LANES), si...  2.18 us
  transfers between devices with their start and end apart: 12, of which 6 were waited for; matrix products, arithmetic and copies ran while one was open for 0% of the time, Pallas kernels for 0%

profile of v4, /device:TPU:0, one launch (start us, length us, event | category | flops | bytes accessed | tf_op | source)
XLA Modules:
  0.0 67.8 jit_solution(8666143380609096151)
XLA Ops:
  0.6 2.2 %conductivity.1 = (f32[30,32,128]{2,1,0:T(8,128)S(1)}, f32[6,32,128]{2,1,0:T(8,128)S(1)}, f32[6,32,128]{2,1,0:T(8,128)S(1)}) custom-call(f32[10,32,128]{2,1,0:T(8,128)} %pressure_in.1, s32[10,32,128]{2,1,0:T(8,128)} %soil_in.1, f32[10,32,128]{2,1,0:T(8,128)} %storage_in.1, f32[10,32,128]{2,1,0:T(8,128)} %source_in.1, f32[1,23]{1,0:T(1,128)} %bitcast.8, ...), custom_call_target="tpu_custom_call" | custom-call | tf_op jit(solution)/shard_map/conductivity/pallas_call | solution.py:614
  2.9 0.1 collective-permute-start
  3.0 0.7 %collective-permute-start.1 = (f32[30,24,128]{2,1,0:T(8,128)S(1)}, f32[30,24,128]{2,1,0:T(8,128)S(1)}, u32[]{:S(2)}, u32[]{:S(2)}) collective-permute-start(f32[30,24,128]{2,1,0:T(8,128)S(1)} %get-tuple-element.40), channel_id=1, source_target_pairs={{16,32},{48,64},{80,96},{32,16},{64,48},{96,80},{17,33},{49,65},{8... | collective-permute-start | bytes 1105928 | tf_op jit(solution)/shard_map/ppermute | solution.py:606
  3.7 2.1 %collective-permute-start.2 = (f32[6,32,128]{2,1,0:T(8,128)S(1)}, f32[6,32,128]{2,1,0:T(8,128)S(1)}, u32[]{:S(2)}, u32[]{:S(2)}) collective-permute-start(f32[6,32,128]{2,1,0:T(8,128)S(1)} %get-tuple-element.41), channel_id=1, source_target_pairs={{0,1},{2,3},{4,5},{6,7},{8,9},{10,11},{12,13},{14,15},{1,0},{3,2},... | collective-permute-start | bytes 294920 | tf_op jit(solution)/shard_map/ppermute | solution.py:606
  5.8 0.7 collective-permute-start.3
  6.4 2.0 %collective-permute-done.2.from_pair = f32[6,32,128]{2,1,0:T(8,128)S(1)} collective-permute-done((f32[6,32,128]{2,1,0:T(8,128)S(1)}, f32[6,32,128]{2,1,0:T(8,128)S(1)}, u32[]{:S(2)}, u32[]{:S(2)}) %collective-permute-start.2) | collective-permute-done | bytes 98336 | tf_op jit(solution)/shard_map/ppermute | solution.py:606
  8.4 2.1 %collective-permute-start.4 = (f32[12,24,128]{2,1,0:T(8,128)S(1)}, f32[12,24,128]{2,1,0:T(8,128)S(1)}, u32[]{:S(2)}, u32[]{:S(2)}) collective-permute-start(f32[12,24,128]{2,1,0:T(8,128)S(1)} %get-tuple-element.43), channel_id=1, source_target_pairs={{0,16},{32,48},{64,80},{96,112},{16,0},{48,32},{80,64},{112,96},{1... | collective-permute-start | bytes 442376 | tf_op jit(solution)/shard_map/ppermute | solution.py:606
  10.5 0.7 collective-permute-start.5
  11.2 0.3 collective-permute-done.4.corner_sibling
  11.5 4.9 %descent.1 = (f32[2,5,2,48,128]{4,3,2,1,0:T(8,128)S(1)}, f32[2,5,2,48,128]{4,3,2,1,0:T(8,128)S(1)}, f32[5,2,48,128]{3,2,1,0:T(8,128)S(1)}, f32[2,5,2,48,128]{4,3...) custom-call(f32[30,32,128]{2,1,0:T(8,128)S(1)} %get-tuple-element.38, ...), custom_call_target="tpu_custom_call" | custom-call | tf_op jit(solution)/shard_map/descent/pallas_call | solution.py:639
  16.4 0.7 collective-permute-start.7
  17.1 8.2 %collective-permute-start.6 = (f32[44,128]{1,0:T(8,128)S(1)}, f32[44,128]{1,0:T(8,128)S(1)}, u32[]{:S(2)}, u32[]{:S(2)}) collective-permute-start(f32[44,128]{1,0:T(8,128)S(1)} %get-tuple-element.45.tiles), channel_id=1, source_target_pairs={{0,1},{2,3},{4,5},{6,7},{8,9},{10,11},{12,13},{14,15},{1,0},{3,2},... | collective-permute-start | bytes 67592 | tf_op jit(solution)/shard_map/ppermute | solution.py:606
  25.3 1.8 %collective-permute-done.6.from_pair = f32[44,128]{1,0:T(8,128)S(1)} collective-permute-done((f32[44,128]{1,0:T(8,128)S(1)}, f32[44,128]{1,0:T(8,128)S(1)}, u32[]{:S(2)}, u32[]{:S(2)}) %collective-permute-start.6) | collective-permute-done | bytes 22560 | tf_op jit(solution)/shard_map/ppermute | solution.py:606
  27.1 5.6 %collective-permute-start.8 = (f32[44,256]{1,0:T(8,128)S(1)}, f32[44,256]{1,0:T(8,128)S(1)}, u32[]{:S(2)}, u32[]{:S(2)}) collective-permute-start(f32[44,256]{1,0:T(8,128)S(1)} %window.1.mine), channel_id=1, source_target_pairs={{0,16},{32,48},{64,80},{96,112},{16,0},{48,32},{80,64},{112,96},{1... | collective-permute-start | bytes 135176 | tf_op jit(solution)/shard_map/ppermute | solution.py:657
  32.7 0.9 %collective-permute-done.8.sibling = f32[44,256]{1,0:T(8,128)S(1)} collective-permute-done((f32[44,256]{1,0:T(8,128)S(1)}, f32[44,256]{1,0:T(8,128)S(1)}, u32[]{:S(2)}, u32[]{:S(2)}) %collective-permute-start.8) | collective-permute-done | bytes 45088 | tf_op jit(solution)/shard_map/ppermute | solution.py:657
  33.6 0.7 collective-permute-start.9
  34.3 6.7 %collective-permute-start.10 = (f32[88,256]{1,0:T(8,128)S(1)}, f32[88,256]{1,0:T(8,128)S(1)}, u32[]{:S(2)}, u32[]{:S(2)}) collective-permute-start(f32[88,256]{1,0:T(8,128)S(1)} %collective-permute-done.9.received), channel_id=1, source_target_pairs={{0,16},{32,48},{64,80},{96,112},{16,0},{48,32},{80,64},{112,96},{1... | collective-permute-start | bytes 270344 | tf_op jit(solution)/shard_map/ppermute | solution.py:662
  40.9 0.9 %collective-permute-done.10.passed_on = f32[88,256]{1,0:T(8,128)S(1)} collective-permute-done((f32[88,256]{1,0:T(8,128)S(1)}, f32[88,256]{1,0:T(8,128)S(1)}, u32[]{:S(2)}, u32[]{:S(2)}) %collective-permute-start.10) | collective-permute-done | bytes 90144 | tf_op jit(solution)/shard_map/ppermute | solution.py:662
  41.9 3.2 %ascent.1 = (f32[8,5,32,128]{3,2,1,0:T(8,128)S(1)}, f32[8,128]{1,0:T(8,128)S(1)}) custom-call(f32[44,256]{1,0:T(8,128)S(1)} %window.1.mine, f32[44,256]{1,0:T(8,128)S(1)} %collective-permute-done.8.sibling, f32[88,256]{1,0:T(8,128)S(1)} %collective-permute-done.9.received, f32[88,256]{1,0:T(8,128)S(1)} %collective-permute-done.10.passed_on, ...), custom_call_target="tpu_custom_call" | custom-call | tf_op jit(solution)/shard_map/ascent/pallas_call | solution.py:666
  45.1 0.4 collective-permute-start.11
  45.5 0.8 %collective-permute-done.11 = f32[8,128]{1,0:T(8,128)S(1)} collective-permute-done((f32[8,128]{1,0:T(8,128)S(1)}, f32[8,128]{1,0:T(8,128)S(1)}, u32[]{:S(2)}, u32[]{:S(2)}) %collective-permute-start.11) | collective-permute-done | bytes 4128 | tf_op jit(solution)/shard_map/ppermute | solution.py:676
  46.3 0.1 maximum_bitcast_fusion
  46.4 19.4 %all_to_all.8 = f32[64,1,32]{2,1,0:T(1,128)S(1)} all-to-all(f32[64,1,32]{2,1,0:T(1,128)S(1)} %broadcast_in_dim.2), channel_id=1, replica_groups={{111,110,109,108,107,106,105,104,103,102,101,100,99,98,97,96,79,78,77,7..., dimensions={0} | all-to-all | bytes 16384 | tf_op jit(solution)/shard_map/all_to_all | solution.py:679
  65.8 2.0 %outputs.1 = (f32[10,32,128]{2,1,0:T(8,128)}, f32[10,32,128]{2,1,0:T(8,128)}, f32[1,1]{1,0:T(1,128)}) custom-call(f32[64,32]{1,0:T(8,128)S(1)} %bitcast.7, f32[8,128]{1,0:T(8,128)S(1)} %get-tuple-element.68.line, f32[8,5,32,128]{3,2,1,0:T(8,128)S(1)} %get-tuple-element.69.fields), custom_call_target="tpu_custom_call" | custom-call | tf_op jit(solution)/shard_map/outputs/pallas_call | solution.py:683
  (13 shorter events, 0.2 us)
Async XLA Ops:
  2.9 8.6 %collective-permute-start = (f32[30,24,128]{2,1,0:T(8,128)S(1)}, f32[30,24,128]{2,1,0:T(8,128)S(1)}, u32[]{:S(2)}, u32[]{:S(2)}) collective-permute-start(f32[30,24,128]{2,1,0:T(8,128)S(1)} %get-tuple-element.39), channel_id=1, source_target_pairs={{0,16},{32,48},{64,80},{96,112},{16,0},{48,32},{80,64},{112,96},{1... | collective-permute-start | bytes 1105928 | tf_op jit(solution)/shard_map/ppermute | solution.py:606
  3.0 8.6 %collective-permute-start.1 = (f32[30,24,128]{2,1,0:T(8,128)S(1)}, f32[30,24,128]{2,1,0:T(8,128)S(1)}, u32[]{:S(2)}, u32[]{:S(2)}) collective-permute-start(f32[30,24,128]{2,1,0:T(8,128)S(1)} %get-tuple-element.40), channel_id=1, source_target_pairs={{16,32},{48,64},{80,96},{32,16},{64,48},{96,80},{17,33},{49,65},{8... | collective-permute-start | bytes 1105928 | tf_op jit(solution)/shard_map/ppermute | solution.py:606
  3.7 4.7 %collective-permute-start.2 = (f32[6,32,128]{2,1,0:T(8,128)S(1)}, f32[6,32,128]{2,1,0:T(8,128)S(1)}, u32[]{:S(2)}, u32[]{:S(2)}) collective-permute-start(f32[6,32,128]{2,1,0:T(8,128)S(1)} %get-tuple-element.41), channel_id=1, source_target_pairs={{0,1},{2,3},{4,5},{6,7},{8,9},{10,11},{12,13},{14,15},{1,0},{3,2},... | collective-permute-start | bytes 294920 | tf_op jit(solution)/shard_map/ppermute | solution.py:606
  5.8 2.6 %collective-permute-start.3 = (f32[6,32,128]{2,1,0:T(8,128)S(1)}, f32[6,32,128]{2,1,0:T(8,128)S(1)}, u32[]{:S(2)}, u32[]{:S(2)}) collective-permute-start(f32[6,32,128]{2,1,0:T(8,128)S(1)} %get-tuple-element.42), channel_id=1, source_target_pairs={{1,2},{3,4},{5,6},{7,8},{9,10},{11,12},{13,14},{2,1},{4,3},{6,5},{... | collective-permute-start | bytes 294920 | tf_op jit(solution)/shard_map/ppermute | solution.py:606
  8.4 3.1 %collective-permute-start.4 = (f32[12,24,128]{2,1,0:T(8,128)S(1)}, f32[12,24,128]{2,1,0:T(8,128)S(1)}, u32[]{:S(2)}, u32[]{:S(2)}) collective-permute-start(f32[12,24,128]{2,1,0:T(8,128)S(1)} %get-tuple-element.43), channel_id=1, source_target_pairs={{0,16},{32,48},{64,80},{96,112},{16,0},{48,32},{80,64},{112,96},{1... | collective-permute-start | bytes 442376 | tf_op jit(solution)/shard_map/ppermute | solution.py:606
  10.5 1.0 %collective-permute-start.5 = (f32[12,24,128]{2,1,0:T(8,128)S(1)}, f32[12,24,128]{2,1,0:T(8,128)S(1)}, u32[]{:S(2)}, u32[]{:S(2)}) collective-permute-start(f32[12,24,128]{2,1,0:T(8,128)S(1)} %get-tuple-element.44), channel_id=1, source_target_pairs={{16,32},{48,64},{80,96},{32,16},{64,48},{96,80},{17,33},{49,65},{8... | collective-permute-start | bytes 442376 | tf_op jit(solution)/shard_map/ppermute | solution.py:606
  16.4 8.9 %collective-permute-start.7 = (f32[44,128]{1,0:T(8,128)S(1)}, f32[44,128]{1,0:T(8,128)S(1)}, u32[]{:S(2)}, u32[]{:S(2)}) collective-permute-start(f32[44,128]{1,0:T(8,128)S(1)} %get-tuple-element.45.tiles), channel_id=1, source_target_pairs={{1,2},{3,4},{5,6},{7,8},{9,10},{11,12},{13,14},{2,1},{4,3},{6,5},{... | collective-permute-start | bytes 67592 | tf_op jit(solution)/shard_map/ppermute | solution.py:606
  17.1 10.0 %collective-permute-start.6 = (f32[44,128]{1,0:T(8,128)S(1)}, f32[44,128]{1,0:T(8,128)S(1)}, u32[]{:S(2)}, u32[]{:S(2)}) collective-permute-start(f32[44,128]{1,0:T(8,128)S(1)} %get-tuple-element.45.tiles), channel_id=1, source_target_pairs={{0,1},{2,3},{4,5},{6,7},{8,9},{10,11},{12,13},{14,15},{1,0},{3,2},... | collective-permute-start | bytes 67592 | tf_op jit(solution)/shard_map/ppermute | solution.py:606
  27.1 6.4 %collective-permute-start.8 = (f32[44,256]{1,0:T(8,128)S(1)}, f32[44,256]{1,0:T(8,128)S(1)}, u32[]{:S(2)}, u32[]{:S(2)}) collective-permute-start(f32[44,256]{1,0:T(8,128)S(1)} %window.1.mine), channel_id=1, source_target_pairs={{0,16},{32,48},{64,80},{96,112},{16,0},{48,32},{80,64},{112,96},{1... | collective-permute-start | bytes 135176 | tf_op jit(solution)/shard_map/ppermute | solution.py:657
  33.6 0.7 collective-permute-start.9
  34.3 7.6 %collective-permute-start.10 = (f32[88,256]{1,0:T(8,128)S(1)}, f32[88,256]{1,0:T(8,128)S(1)}, u32[]{:S(2)}, u32[]{:S(2)}) collective-permute-start(f32[88,256]{1,0:T(8,128)S(1)} %collective-permute-done.9.received), channel_id=1, source_target_pairs={{0,16},{32,48},{64,80},{96,112},{16,0},{48,32},{80,64},{112,96},{1... | collective-permute-start | bytes 270344 | tf_op jit(solution)/shard_map/ppermute | solution.py:662
  45.1 1.3 %collective-permute-start.11 = (f32[8,128]{1,0:T(8,128)S(1)}, f32[8,128]{1,0:T(8,128)S(1)}, u32[]{:S(2)}, u32[]{:S(2)}) collective-permute-start(f32[8,128]{1,0:T(8,128)S(1)} %get-tuple-element.68.line), channel_id=1, source_target_pairs={{0,16},{32,48},{64,80},{96,112},{16,0},{48,32},{80,64},{112,96},{1... | collective-permute-start | bytes 12296 | tf_op jit(solution)/shard_map/ppermute | solution.py:676

commit v5 on v4

--- a/solution.py
+++ b/solution.py
@@ -174,7 +174,7 @@
         to_other[t] = jnp.where(even, low, high)
 
 
-def second_kernel(from_pair, from_next, to_sibling, to_other):
+def second_kernel(from_next, from_pair, to_sibling, to_other):
     even = (position()[0] & 1) == 0
     for q, ref in enumerate((from_pair, from_next)):
         for tile in range(6):
@@ -258,7 +258,7 @@
 
 
 def third_kernel(
-    packed, from_sibling, from_other, from_pair, from_next, corner_sibling, corner_other,
+    packed, corner_sibling, corner_other, from_next, from_pair, from_sibling, from_other,
     source0, inv0, first0, east0, north0, inner0, outer0,
     source1, inv1, first1, east1, north1, inner1, outer1,
     source2, inv2, first2, east2, north2, inner2, outer2,
@@ -626,8 +626,8 @@
     halos = pair_exchange(slabs, "gx") + beside_y
     corners = pl.pallas_call(
         second_kernel, out_shape=(corner, corner), in_specs=[VM, VM], out_specs=(VM, VM), compiler_params=params(2), name="corners",
-    )(*beside_y)
-    halos = halos + pair_exchange(corners, "gx")
+    )(*beside_y[::-1])
+    halos = pair_exchange(corners, "gx") + beside_y[::-1] + halos[:2]
 
     def sized(rows):
         return [scratch(*dims) for dims in level_dims(rows)]
@@ -674,7 +674,7 @@
         compiler_params=params(8), name="ascent",
     )(*blocks, sums, *levels)
     both = jnp.concatenate([line[:1, :16], lax.ppermute(line, "gx", pairs_of(count_x, 0))[:1, :16]], axis=1)
-    kinds = [[x * count_y + y for x in range(c, count_x, 2) for y in range(count_y)][::-1] for c in range(2)]
+    kinds = [[x * count_y + y for y in range(count_y) for x in range(c, count_x, 2)][::-1] for c in range(2)]
     both = jnp.broadcast_to(both, (devices // 2, 32))
     every = lax.all_to_all(both, ("gx", "gy"), 0, 0, axis_index_groups=kinds, tiled=True)
 

time: 68.1 us -> 67.7 us (level)
  starting transfers between devices: 28.5 us -> 26.5 us
  blocking collectives: 19.4 us -> 20.3 us
    ppermute x8, starting transfers between devices: 15.1 us -> 13.2 us  [pair_exchange(): lax.ppermute(x_i, axis, pairs_of(count, first))]
    all_to_all x1, blocking collectives: 19.4 us -> 20.3 us  [shards(): lax.all_to_all(both, ('gx', 'gy'), 0, 0, axis_index_groups=kinds, tiled=T...]
where the time goes in v5:
time: 67.7 us; the launch traced here: 67.4 us
  starting transfers between devices  26.5 us (39%)
  blocking collectives  20.3 us (30%)
  Pallas kernels  12.4 us (18%)
  waiting for transfers between devices  7.39 us (11%)
  between operations  0.74 us (1%)
    all_to_all x1, blocking collectives, shards(): lax.all_to_all(both, ('gx', 'gy'), 0, 0, axis_index_groups=kinds, tiled=T...  20.3 us
    ppermute x8, starting transfers between devices, pair_exchange(): lax.ppermute(x_i, axis, pairs_of(count, first))  13.2 us
    ppermute x1, starting transfers between devices, shards(): passed_on = lax.ppermute(received, 'gx', pairs_of(count_x, 0))  6.61 us
    ppermute x1, starting transfers between devices, shards(): sibling = lax.ppermute(window, 'gx', pairs_of(count_x, 0))  5.56 us
    pallas_call x1, Pallas kernels, shards(): pl.pallas_call(third_kernel, out_shape=(*level_shapes(48), *level_shapes(...  4.91 us
    ppermute x8, waiting for transfers between devices, pair_exchange(): lax.ppermute(x_i, axis, pairs_of(count, first))  4.75 us
    pallas_call x1, Pallas kernels, shards(): pl.pallas_call(fourth_kernel, out_shape=(shape(8, PAIRS, ROWS, LANES), sh...  3.18 us
    pallas_call x1, Pallas kernels, shards(): pl.pallas_call(first_kernel, out_shape=(shape(6 * PAIRS, ROWS, LANES), si...  2.18 us
  transfers between devices with their start and end apart: 12, of which 6 were waited for; matrix products, arithmetic and copies ran while one was open for 0% of the time, Pallas kernels for 0%

profile of v5, /device:TPU:0, one launch (start us, length us, event | category | flops | bytes accessed | tf_op | source)
XLA Modules:
  0.0 67.4 jit_solution(17842683299001769167)
XLA Ops:
  0.6 2.2 %conductivity.1 = (f32[30,32,128]{2,1,0:T(8,128)S(1)}, f32[6,32,128]{2,1,0:T(8,128)S(1)}, f32[6,32,128]{2,1,0:T(8,128)S(1)}) custom-call(f32[10,32,128]{2,1,0:T(8,128)} %pressure_in.1, s32[10,32,128]{2,1,0:T(8,128)} %soil_in.1, f32[10,32,128]{2,1,0:T(8,128)} %storage_in.1, f32[10,32,128]{2,1,0:T(8,128)} %source_in.1, f32[1,23]{1,0:T(1,128)} %bitcast.8, ...), custom_call_target="tpu_custom_call" | custom-call | tf_op jit(solution)/shard_map/conductivity/pallas_call | solution.py:614
  2.9 0.1 collective-permute-start.4
  3.0 0.7 %collective-permute-start.5 = (f32[30,24,128]{2,1,0:T(8,128)S(1)}, f32[30,24,128]{2,1,0:T(8,128)S(1)}, u32[]{:S(2)}, u32[]{:S(2)}) collective-permute-start(f32[30,24,128]{2,1,0:T(8,128)S(1)} %get-tuple-element.44), channel_id=1, source_target_pairs={{16,32},{48,64},{80,96},{32,16},{64,48},{96,80},{17,33},{49,65},{8... | collective-permute-start | bytes 1105928 | tf_op jit(solution)/shard_map/ppermute | solution.py:606
  3.7 0.7 collective-permute-start
  4.4 5.2 %collective-permute-start.1 = (f32[6,32,128]{2,1,0:T(8,128)S(1)}, f32[6,32,128]{2,1,0:T(8,128)S(1)}, u32[]{:S(2)}, u32[]{:S(2)}) collective-permute-start(f32[6,32,128]{2,1,0:T(8,128)S(1)} %get-tuple-element.40), channel_id=1, source_target_pairs={{0,1},{2,3},{4,5},{6,7},{8,9},{10,11},{12,13},{14,15},{1,0},{3,2},... | collective-permute-start | bytes 294920 | tf_op jit(solution)/shard_map/ppermute | solution.py:606
  9.6 2.6 %collective-permute-done.1.from_pair = f32[6,32,128]{2,1,0:T(8,128)S(1)} collective-permute-done((f32[6,32,128]{2,1,0:T(8,128)S(1)}, f32[6,32,128]{2,1,0:T(8,128)S(1)}, u32[]{:S(2)}, u32[]{:S(2)}) %collective-permute-start.1) | collective-permute-done | bytes 98336 | tf_op jit(solution)/shard_map/ppermute | solution.py:606
  12.2 1.8 %collective-permute-start.2 = (f32[12,24,128]{2,1,0:T(8,128)S(1)}, f32[12,24,128]{2,1,0:T(8,128)S(1)}, u32[]{:S(2)}, u32[]{:S(2)}) collective-permute-start(f32[12,24,128]{2,1,0:T(8,128)S(1)} %get-tuple-element.41), channel_id=1, source_target_pairs={{0,16},{32,48},{64,80},{96,112},{16,0},{48,32},{80,64},{112,96},{1... | collective-permute-start | bytes 442376 | tf_op jit(solution)/shard_map/ppermute | solution.py:606
  14.1 0.7 collective-permute-start.3
  14.7 0.3 collective-permute-done.2.corner_sibling
  15.1 4.9 %descent.1 = (f32[2,5,2,48,128]{4,3,2,1,0:T(8,128)S(1)}, f32[2,5,2,48,128]{4,3,2,1,0:T(8,128)S(1)}, f32[5,2,48,128]{3,2,1,0:T(8,128)S(1)}, f32[2,5,2,48,128]{4,3...) custom-call(f32[30,32,128]{2,1,0:T(8,128)S(1)} %get-tuple-element.38, ...), custom_call_target="tpu_custom_call" | custom-call | tf_op jit(solution)/shard_map/descent/pallas_call | solution.py:639
  20.0 0.7 collective-permute-start.7
  20.7 3.4 %collective-permute-start.6 = (f32[44,128]{1,0:T(8,128)S(1)}, f32[44,128]{1,0:T(8,128)S(1)}, u32[]{:S(2)}, u32[]{:S(2)}) collective-permute-start(f32[44,128]{1,0:T(8,128)S(1)} %get-tuple-element.45.tiles), channel_id=1, source_target_pairs={{0,1},{2,3},{4,5},{6,7},{8,9},{10,11},{12,13},{14,15},{1,0},{3,2},... | collective-permute-start | bytes 67592 | tf_op jit(solution)/shard_map/ppermute | solution.py:606
  24.0 1.8 %collective-permute-done.6.from_pair = f32[44,128]{1,0:T(8,128)S(1)} collective-permute-done((f32[44,128]{1,0:T(8,128)S(1)}, f32[44,128]{1,0:T(8,128)S(1)}, u32[]{:S(2)}, u32[]{:S(2)}) %collective-permute-start.6) | collective-permute-done | bytes 22560 | tf_op jit(solution)/shard_map/ppermute | solution.py:606
  25.9 5.6 %collective-permute-start.8 = (f32[44,256]{1,0:T(8,128)S(1)}, f32[44,256]{1,0:T(8,128)S(1)}, u32[]{:S(2)}, u32[]{:S(2)}) collective-permute-start(f32[44,256]{1,0:T(8,128)S(1)} %window.1.mine), channel_id=1, source_target_pairs={{0,16},{32,48},{64,80},{96,112},{16,0},{48,32},{80,64},{112,96},{1... | collective-permute-start | bytes 135176 | tf_op jit(solution)/shard_map/ppermute | solution.py:657
  31.4 0.9 %collective-permute-done.8.sibling = f32[44,256]{1,0:T(8,128)S(1)} collective-permute-done((f32[44,256]{1,0:T(8,128)S(1)}, f32[44,256]{1,0:T(8,128)S(1)}, u32[]{:S(2)}, u32[]{:S(2)}) %collective-permute-start.8) | collective-permute-done | bytes 45088 | tf_op jit(solution)/shard_map/ppermute | solution.py:657
  32.3 0.7 collective-permute-start.9
  33.0 6.6 %collective-permute-start.10 = (f32[88,256]{1,0:T(8,128)S(1)}, f32[88,256]{1,0:T(8,128)S(1)}, u32[]{:S(2)}, u32[]{:S(2)}) collective-permute-start(f32[88,256]{1,0:T(8,128)S(1)} %collective-permute-done.9.received), channel_id=1, source_target_pairs={{0,16},{32,48},{64,80},{96,112},{16,0},{48,32},{80,64},{112,96},{1... | collective-permute-start | bytes 270344 | tf_op jit(solution)/shard_map/ppermute | solution.py:662
  39.6 0.9 %collective-permute-done.10.passed_on = f32[88,256]{1,0:T(8,128)S(1)} collective-permute-done((f32[88,256]{1,0:T(8,128)S(1)}, f32[88,256]{1,0:T(8,128)S(1)}, u32[]{:S(2)}, u32[]{:S(2)}) %collective-permute-start.10) | collective-permute-done | bytes 90144 | tf_op jit(solution)/shard_map/ppermute | solution.py:662
  40.5 3.2 %ascent.1 = (f32[8,5,32,128]{3,2,1,0:T(8,128)S(1)}, f32[8,128]{1,0:T(8,128)S(1)}) custom-call(f32[44,256]{1,0:T(8,128)S(1)} %window.1.mine, f32[44,256]{1,0:T(8,128)S(1)} %collective-permute-done.8.sibling, f32[88,256]{1,0:T(8,128)S(1)} %collective-permute-done.9.received, f32[88,256]{1,0:T(8,128)S(1)} %collective-permute-done.10.passed_on, ...), custom_call_target="tpu_custom_call" | custom-call | tf_op jit(solution)/shard_map/ascent/pallas_call | solution.py:666
  43.7 0.4 collective-permute-start.11
  44.2 0.8 %collective-permute-done.11 = f32[8,128]{1,0:T(8,128)S(1)} collective-permute-done((f32[8,128]{1,0:T(8,128)S(1)}, f32[8,128]{1,0:T(8,128)S(1)}, u32[]{:S(2)}, u32[]{:S(2)}) %collective-permute-start.11) | collective-permute-done | bytes 4128 | tf_op jit(solution)/shard_map/ppermute | solution.py:676
  45.0 0.1 maximum_bitcast_fusion
  45.1 20.3 %all_to_all.8 = f32[64,1,32]{2,1,0:T(1,128)S(1)} all-to-all(f32[64,1,32]{2,1,0:T(1,128)S(1)} %broadcast_in_dim.2), channel_id=1, replica_groups={{111,79,47,15,110,78,46,14,109,77,45,13,108,76,44,12,107,75,43,11,106,7..., dimensions={0} | all-to-all | bytes 16384 | tf_op jit(solution)/shard_map/all_to_all | solution.py:679
  65.4 2.0 %outputs.1 = (f32[10,32,128]{2,1,0:T(8,128)}, f32[10,32,128]{2,1,0:T(8,128)}, f32[1,1]{1,0:T(1,128)}) custom-call(f32[64,32]{1,0:T(8,128)S(1)} %bitcast.7, f32[8,128]{1,0:T(8,128)S(1)} %get-tuple-element.68.line, f32[8,5,32,128]{3,2,1,0:T(8,128)S(1)} %get-tuple-element.69.fields), custom_call_target="tpu_custom_call" | custom-call | tf_op jit(solution)/shard_map/outputs/pallas_call | solution.py:683
  (13 shorter events, 0.1 us)
Async XLA Ops:
  2.9 12.2 %collective-permute-start.4 = (f32[30,24,128]{2,1,0:T(8,128)S(1)}, f32[30,24,128]{2,1,0:T(8,128)S(1)}, u32[]{:S(2)}, u32[]{:S(2)}) collective-permute-start(f32[30,24,128]{2,1,0:T(8,128)S(1)} %get-tuple-element.43), channel_id=1, source_target_pairs={{0,16},{32,48},{64,80},{96,112},{16,0},{48,32},{80,64},{112,96},{1... | collective-permute-start | bytes 1105928 | tf_op jit(solution)/shard_map/ppermute | solution.py:606
  3.0 12.1 %collective-permute-start.5 = (f32[30,24,128]{2,1,0:T(8,128)S(1)}, f32[30,24,128]{2,1,0:T(8,128)S(1)}, u32[]{:S(2)}, u32[]{:S(2)}) collective-permute-start(f32[30,24,128]{2,1,0:T(8,128)S(1)} %get-tuple-element.44), channel_id=1, source_target_pairs={{16,32},{48,64},{80,96},{32,16},{64,48},{96,80},{17,33},{49,65},{8... | collective-permute-start | bytes 1105928 | tf_op jit(solution)/shard_map/ppermute | solution.py:606
  3.7 5.9 %collective-permute-start = (f32[6,32,128]{2,1,0:T(8,128)S(1)}, f32[6,32,128]{2,1,0:T(8,128)S(1)}, u32[]{:S(2)}, u32[]{:S(2)}) collective-permute-start(f32[6,32,128]{2,1,0:T(8,128)S(1)} %get-tuple-element.39), channel_id=1, source_target_pairs={{1,2},{3,4},{5,6},{7,8},{9,10},{11,12},{13,14},{2,1},{4,3},{6,5},{... | collective-permute-start | bytes 294920 | tf_op jit(solution)/shard_map/ppermute | solution.py:606
  4.4 7.8 %collective-permute-start.1 = (f32[6,32,128]{2,1,0:T(8,128)S(1)}, f32[6,32,128]{2,1,0:T(8,128)S(1)}, u32[]{:S(2)}, u32[]{:S(2)}) collective-permute-start(f32[6,32,128]{2,1,0:T(8,128)S(1)} %get-tuple-element.40), channel_id=1, source_target_pairs={{0,1},{2,3},{4,5},{6,7},{8,9},{10,11},{12,13},{14,15},{1,0},{3,2},... | collective-permute-start | bytes 294920 | tf_op jit(solution)/shard_map/ppermute | solution.py:606
  12.2 2.9 %collective-permute-start.2 = (f32[12,24,128]{2,1,0:T(8,128)S(1)}, f32[12,24,128]{2,1,0:T(8,128)S(1)}, u32[]{:S(2)}, u32[]{:S(2)}) collective-permute-start(f32[12,24,128]{2,1,0:T(8,128)S(1)} %get-tuple-element.41), channel_id=1, source_target_pairs={{0,16},{32,48},{64,80},{96,112},{16,0},{48,32},{80,64},{112,96},{1... | collective-permute-start | bytes 442376 | tf_op jit(solution)/shard_map/ppermute | solution.py:606
  14.1 1.0 %collective-permute-start.3 = (f32[12,24,128]{2,1,0:T(8,128)S(1)}, f32[12,24,128]{2,1,0:T(8,128)S(1)}, u32[]{:S(2)}, u32[]{:S(2)}) collective-permute-start(f32[12,24,128]{2,1,0:T(8,128)S(1)} %get-tuple-element.42), channel_id=1, source_target_pairs={{16,32},{48,64},{80,96},{32,16},{64,48},{96,80},{17,33},{49,65},{8... | collective-permute-start | bytes 442376 | tf_op jit(solution)/shard_map/ppermute | solution.py:606
  20.0 4.0 %collective-permute-start.7 = (f32[44,128]{1,0:T(8,128)S(1)}, f32[44,128]{1,0:T(8,128)S(1)}, u32[]{:S(2)}, u32[]{:S(2)}) collective-permute-start(f32[44,128]{1,0:T(8,128)S(1)} %get-tuple-element.45.tiles), channel_id=1, source_target_pairs={{1,2},{3,4},{5,6},{7,8},{9,10},{11,12},{13,14},{2,1},{4,3},{6,5},{... | collective-permute-start | bytes 67592 | tf_op jit(solution)/shard_map/ppermute | solution.py:606
  20.7 5.2 %collective-permute-start.6 = (f32[44,128]{1,0:T(8,128)S(1)}, f32[44,128]{1,0:T(8,128)S(1)}, u32[]{:S(2)}, u32[]{:S(2)}) collective-permute-start(f32[44,128]{1,0:T(8,128)S(1)} %get-tuple-element.45.tiles), channel_id=1, source_target_pairs={{0,1},{2,3},{4,5},{6,7},{8,9},{10,11},{12,13},{14,15},{1,0},{3,2},... | collective-permute-start | bytes 67592 | tf_op jit(solution)/shard_map/ppermute | solution.py:606
  25.9 6.4 %collective-permute-start.8 = (f32[44,256]{1,0:T(8,128)S(1)}, f32[44,256]{1,0:T(8,128)S(1)}, u32[]{:S(2)}, u32[]{:S(2)}) collective-permute-start(f32[44,256]{1,0:T(8,128)S(1)} %window.1.mine), channel_id=1, source_target_pairs={{0,16},{32,48},{64,80},{96,112},{16,0},{48,32},{80,64},{112,96},{1... | collective-permute-start | bytes 135176 | tf_op jit(solution)/shard_map/ppermute | solution.py:657
  32.3 0.7 %collective-permute-start.9 = (f32[88,256]{1,0:T(8,128)S(1)}, f32[88,256]{1,0:T(8,128)S(1)}, u32[]{:S(2)}, u32[]{:S(2)}) collective-permute-start(f32[88,256]{1,0:T(8,128)S(1)} %join.1), channel_id=1, source_target_pairs={{16,32},{48,64},{80,96},{32,16},{64,48},{96,80},{17,33},{49,65},{8... | collective-permute-start | bytes 270344 | tf_op jit(solution)/shard_map/ppermute | solution.py:661
  33.0 7.5 %collective-permute-start.10 = (f32[88,256]{1,0:T(8,128)S(1)}, f32[88,256]{1,0:T(8,128)S(1)}, u32[]{:S(2)}, u32[]{:S(2)}) collective-permute-start(f32[88,256]{1,0:T(8,128)S(1)} %collective-permute-done.9.received), channel_id=1, source_target_pairs={{0,16},{32,48},{64,80},{96,112},{16,0},{48,32},{80,64},{112,96},{1... | collective-permute-start | bytes 270344 | tf_op jit(solution)/shard_map/ppermute | solution.py:662
  43.7 1.3 %collective-permute-start.11 = (f32[8,128]{1,0:T(8,128)S(1)}, f32[8,128]{1,0:T(8,128)S(1)}, u32[]{:S(2)}, u32[]{:S(2)}) collective-permute-start(f32[8,128]{1,0:T(8,128)S(1)} %get-tuple-element.68.line), channel_id=1, source_target_pairs={{0,16},{32,48},{64,80},{96,112},{16,0},{48,32},{80,64},{112,96},{1... | collective-permute-start | bytes 12296 | tf_op jit(solution)/shard_map/ppermute | solution.py:676

commit v6 on v5

--- a/solution.py
+++ b/solution.py
@@ -384,7 +384,7 @@
             outer0[m], outer1[m] = outer[m, slice(16, 64)], out1[m, slice(8, 32)]
 
 
-def window_kernel(tiles, from_pair, from_next, window):
+def window_kernel(tiles, from_next, from_pair, window):
     even = (position()[1] & 1) == 0
     window[:, :LANES] = tiles[...]
     a, b = from_pair[...], from_next[...]
@@ -549,13 +549,14 @@
 
 
 def last_kernel(sums, line, fields, solution_out, residual_out, norm_ref, solution_ref, residual_ref, sems, *, cells):
-    x = jnp.concatenate([sums[:, :16], sums[:, 16:]], axis=0)
+    wide = jnp.concatenate([sums[...], jnp.zeros((sums.shape[0], LANES - sums.shape[1]), jnp.float32)], axis=1).T
+    x = jnp.concatenate([wide[:16], wide[16:32]], axis=1)
 
     def column(q):
-        return x[:, q : q + 1]
+        return x[q : q + 1]
 
     def total(v):
-        return jnp.sum(v, axis=0, keepdims=True)
+        return jnp.sum(v, axis=1, keepdims=True)
 
     rp, rq, pa, pb, qb, dd, da, aa, db, ab, bb = [column(q) for q in range(11)]
     mean = total(column(11)) / total(column(12))
@@ -653,7 +654,7 @@
     tile_pair, tile_next = pair_exchange((tiles, tiles), "gy")
     window = pl.pallas_call(
         window_kernel, out_shape=shape(4 * TILES, WIDE), in_specs=[VM] * 3, out_specs=VM, compiler_params=params(2), name="window",
-    )(tiles, tile_pair, tile_next)
+    )(tiles, tile_next, tile_pair)
     sibling = lax.ppermute(window, "gx", pairs_of(count_x, 0))
     both = pl.pallas_call(
         join_kernel, out_shape=shape(8 * TILES, WIDE), in_specs=[VM] * 2, out_specs=VM, compiler_params=params(2), name="join",

time: 67.7 us -> 67.6 us (level)
  blocking collectives: 20.3 us -> 22.5 us
  starting transfers between devices: 26.5 us -> 24.8 us
    all_to_all x1, blocking collectives: 20.3 us -> 22.5 us  [shards(): lax.all_to_all(both, ('gx', 'gy'), 0, 0, axis_index_groups=kinds, tiled=T...]
    ppermute x8, starting transfers between devices: 13.2 us -> 11.6 us  [pair_exchange(): lax.ppermute(x_i, axis, pairs_of(count, first))]
where the time goes in v6:
time: 67.6 us; the launch traced here: 67.3 us
  starting transfers between devices  24.8 us (37%)
  blocking collectives  22.5 us (33%)
  Pallas kernels  12.2 us (18%)
  waiting for transfers between devices  7.01 us (10%)
  between operations  0.75 us (1%)
    all_to_all x1, blocking collectives, shards(): lax.all_to_all(both, ('gx', 'gy'), 0, 0, axis_index_groups=kinds, tiled=T...  22.5 us
    ppermute x8, starting transfers between devices, pair_exchange(): lax.ppermute(x_i, axis, pairs_of(count, first))  11.6 us
    ppermute x1, starting transfers between devices, shards(): passed_on = lax.ppermute(received, 'gx', pairs_of(count_x, 0))  6.44 us
    ppermute x1, starting transfers between devices, shards(): sibling = lax.ppermute(window, 'gx', pairs_of(count_x, 0))  5.56 us
    pallas_call x1, Pallas kernels, shards(): pl.pallas_call(third_kernel, out_shape=(*level_shapes(48), *level_shapes(...  4.91 us
    ppermute x8, waiting for transfers between devices, pair_exchange(): lax.ppermute(x_i, axis, pairs_of(count, first))  4.38 us
    pallas_call x1, Pallas kernels, shards(): pl.pallas_call(fourth_kernel, out_shape=(shape(8, PAIRS, ROWS, LANES), sh...  3.18 us
    pallas_call x1, Pallas kernels, shards(): pl.pallas_call(first_kernel, out_shape=(shape(6 * PAIRS, ROWS, LANES), si...  2.18 us
  transfers between devices with their start and end apart: 12, of which 6 were waited for; matrix products, arithmetic and copies ran while one was open for 0% of the time, Pallas kernels for 0%

profile of v6, /device:TPU:0, one launch (start us, length us, event | category | flops | bytes accessed | tf_op | source)
XLA Modules:
  0.0 67.3 jit_solution(8181625074310844579)
XLA Ops:
  0.6 2.2 %conductivity.1 = (f32[30,32,128]{2,1,0:T(8,128)S(1)}, f32[6,32,128]{2,1,0:T(8,128)S(1)}, f32[6,32,128]{2,1,0:T(8,128)S(1)}) custom-call(f32[10,32,128]{2,1,0:T(8,128)} %pressure_in.1, s32[10,32,128]{2,1,0:T(8,128)} %soil_in.1, f32[10,32,128]{2,1,0:T(8,128)} %storage_in.1, f32[10,32,128]{2,1,0:T(8,128)} %source_in.1, f32[1,23]{1,0:T(1,128)} %bitcast.8, ...), custom_call_target="tpu_custom_call" | custom-call | tf_op jit(solution)/shard_map/conductivity/pallas_call | solution.py:615
  2.9 0.1 collective-permute-start.4
  3.0 0.7 %collective-permute-start.5 = (f32[30,24,128]{2,1,0:T(8,128)S(1)}, f32[30,24,128]{2,1,0:T(8,128)S(1)}, u32[]{:S(2)}, u32[]{:S(2)}) collective-permute-start(f32[30,24,128]{2,1,0:T(8,128)S(1)} %get-tuple-element.44), channel_id=1, source_target_pairs={{16,32},{48,64},{80,96},{32,16},{64,48},{96,80},{17,33},{49,65},{8... | collective-permute-start | bytes 1105928 | tf_op jit(solution)/shard_map/ppermute | solution.py:607
  3.7 0.7 collective-permute-start
  4.4 5.2 %collective-permute-start.1 = (f32[6,32,128]{2,1,0:T(8,128)S(1)}, f32[6,32,128]{2,1,0:T(8,128)S(1)}, u32[]{:S(2)}, u32[]{:S(2)}) collective-permute-start(f32[6,32,128]{2,1,0:T(8,128)S(1)} %get-tuple-element.40), channel_id=1, source_target_pairs={{0,1},{2,3},{4,5},{6,7},{8,9},{10,11},{12,13},{14,15},{1,0},{3,2},... | collective-permute-start | bytes 294920 | tf_op jit(solution)/shard_map/ppermute | solution.py:607
  9.6 2.6 %collective-permute-done.1.from_pair = f32[6,32,128]{2,1,0:T(8,128)S(1)} collective-permute-done((f32[6,32,128]{2,1,0:T(8,128)S(1)}, f32[6,32,128]{2,1,0:T(8,128)S(1)}, u32[]{:S(2)}, u32[]{:S(2)}) %collective-permute-start.1) | collective-permute-done | bytes 98336 | tf_op jit(solution)/shard_map/ppermute | solution.py:607
  12.2 1.8 %collective-permute-start.2 = (f32[12,24,128]{2,1,0:T(8,128)S(1)}, f32[12,24,128]{2,1,0:T(8,128)S(1)}, u32[]{:S(2)}, u32[]{:S(2)}) collective-permute-start(f32[12,24,128]{2,1,0:T(8,128)S(1)} %get-tuple-element.41), channel_id=1, source_target_pairs={{0,16},{32,48},{64,80},{96,112},{16,0},{48,32},{80,64},{112,96},{1... | collective-permute-start | bytes 442376 | tf_op jit(solution)/shard_map/ppermute | solution.py:607
  14.1 0.7 collective-permute-start.3
  14.7 0.3 collective-permute-done.2.corner_sibling
  15.1 4.9 %descent.1 = (f32[2,5,2,48,128]{4,3,2,1,0:T(8,128)S(1)}, f32[2,5,2,48,128]{4,3,2,1,0:T(8,128)S(1)}, f32[5,2,48,128]{3,2,1,0:T(8,128)S(1)}, f32[2,5,2,48,128]{4,3...) custom-call(f32[30,32,128]{2,1,0:T(8,128)S(1)} %get-tuple-element.38, ...), custom_call_target="tpu_custom_call" | custom-call | tf_op jit(solution)/shard_map/descent/pallas_call | solution.py:640
  20.0 1.8 %collective-permute-start.7 = (f32[44,128]{1,0:T(8,128)S(1)}, f32[44,128]{1,0:T(8,128)S(1)}, u32[]{:S(2)}, u32[]{:S(2)}) collective-permute-start(f32[44,128]{1,0:T(8,128)S(1)} %get-tuple-element.45.tiles), channel_id=1, source_target_pairs={{0,1},{2,3},{4,5},{6,7},{8,9},{10,11},{12,13},{14,15},{1,0},{3,2},... | collective-permute-start | bytes 67592 | tf_op jit(solution)/shard_map/ppermute | solution.py:607
  21.8 0.7 collective-permute-start.6
  22.5 1.4 %collective-permute-done.7.from_pair = f32[44,128]{1,0:T(8,128)S(1)} collective-permute-done((f32[44,128]{1,0:T(8,128)S(1)}, f32[44,128]{1,0:T(8,128)S(1)}, u32[]{:S(2)}, u32[]{:S(2)}) %collective-permute-start.7) | collective-permute-done | bytes 22560 | tf_op jit(solution)/shard_map/ppermute | solution.py:607
  23.9 5.6 %collective-permute-start.8 = (f32[44,256]{1,0:T(8,128)S(1)}, f32[44,256]{1,0:T(8,128)S(1)}, u32[]{:S(2)}, u32[]{:S(2)}) collective-permute-start(f32[44,256]{1,0:T(8,128)S(1)} %window.1.mine), channel_id=1, source_target_pairs={{0,16},{32,48},{64,80},{96,112},{16,0},{48,32},{80,64},{112,96},{1... | collective-permute-start | bytes 135176 | tf_op jit(solution)/shard_map/ppermute | solution.py:658
  29.5 0.9 %collective-permute-done.8.sibling = f32[44,256]{1,0:T(8,128)S(1)} collective-permute-done((f32[44,256]{1,0:T(8,128)S(1)}, f32[44,256]{1,0:T(8,128)S(1)}, u32[]{:S(2)}, u32[]{:S(2)}) %collective-permute-start.8) | collective-permute-done | bytes 45088 | tf_op jit(solution)/shard_map/ppermute | solution.py:658
  30.4 0.7 collective-permute-start.9
  31.1 6.4 %collective-permute-start.10 = (f32[88,256]{1,0:T(8,128)S(1)}, f32[88,256]{1,0:T(8,128)S(1)}, u32[]{:S(2)}, u32[]{:S(2)}) collective-permute-start(f32[88,256]{1,0:T(8,128)S(1)} %collective-permute-done.9.received), channel_id=1, source_target_pairs={{0,16},{32,48},{64,80},{96,112},{16,0},{48,32},{80,64},{112,96},{1... | collective-permute-start | bytes 270344 | tf_op jit(solution)/shard_map/ppermute | solution.py:663
  37.5 0.9 %collective-permute-done.10.passed_on = f32[88,256]{1,0:T(8,128)S(1)} collective-permute-done((f32[88,256]{1,0:T(8,128)S(1)}, f32[88,256]{1,0:T(8,128)S(1)}, u32[]{:S(2)}, u32[]{:S(2)}) %collective-permute-start.10) | collective-permute-done | bytes 90144 | tf_op jit(solution)/shard_map/ppermute | solution.py:663
  38.4 3.2 %ascent.1 = (f32[8,5,32,128]{3,2,1,0:T(8,128)S(1)}, f32[8,128]{1,0:T(8,128)S(1)}) custom-call(f32[44,256]{1,0:T(8,128)S(1)} %window.1.mine, f32[44,256]{1,0:T(8,128)S(1)} %collective-permute-done.8.sibling, f32[88,256]{1,0:T(8,128)S(1)} %collective-permute-done.9.received, f32[88,256]{1,0:T(8,128)S(1)} %collective-permute-done.10.passed_on, ...), custom_call_target="tpu_custom_call" | custom-call | tf_op jit(solution)/shard_map/ascent/pallas_call | solution.py:667
  41.6 0.4 collective-permute-start.11
  42.1 0.8 %collective-permute-done.11 = f32[8,128]{1,0:T(8,128)S(1)} collective-permute-done((f32[8,128]{1,0:T(8,128)S(1)}, f32[8,128]{1,0:T(8,128)S(1)}, u32[]{:S(2)}, u32[]{:S(2)}) %collective-permute-start.11) | collective-permute-done | bytes 4128 | tf_op jit(solution)/shard_map/ppermute | solution.py:677
  42.9 0.1 maximum_bitcast_fusion
  43.0 22.5 %all_to_all.8 = f32[64,1,32]{2,1,0:T(1,128)S(1)} all-to-all(f32[64,1,32]{2,1,0:T(1,128)S(1)} %broadcast_in_dim.2), channel_id=1, replica_groups={{111,79,47,15,110,78,46,14,109,77,45,13,108,76,44,12,107,75,43,11,106,7..., dimensions={0} | all-to-all | bytes 16384 | tf_op jit(solution)/shard_map/all_to_all | solution.py:680
  65.5 1.8 %outputs.1 = (f32[10,32,128]{2,1,0:T(8,128)}, f32[10,32,128]{2,1,0:T(8,128)}, f32[1,1]{1,0:T(1,128)}) custom-call(f32[64,32]{1,0:T(8,128)S(1)} %bitcast.7, f32[8,128]{1,0:T(8,128)S(1)} %get-tuple-element.68.line, f32[8,5,32,128]{3,2,1,0:T(8,128)S(1)} %get-tuple-element.69.fields), custom_call_target="tpu_custom_call" | custom-call | tf_op jit(solution)/shard_map/outputs/pallas_call | solution.py:684
  (13 shorter events, 0.1 us)
Async XLA Ops:
  2.9 12.2 %collective-permute-start.4 = (f32[30,24,128]{2,1,0:T(8,128)S(1)}, f32[30,24,128]{2,1,0:T(8,128)S(1)}, u32[]{:S(2)}, u32[]{:S(2)}) collective-permute-start(f32[30,24,128]{2,1,0:T(8,128)S(1)} %get-tuple-element.43), channel_id=1, source_target_pairs={{0,16},{32,48},{64,80},{96,112},{16,0},{48,32},{80,64},{112,96},{1... | collective-permute-start | bytes 1105928 | tf_op jit(solution)/shard_map/ppermute | solution.py:607
  3.0 12.1 %collective-permute-start.5 = (f32[30,24,128]{2,1,0:T(8,128)S(1)}, f32[30,24,128]{2,1,0:T(8,128)S(1)}, u32[]{:S(2)}, u32[]{:S(2)}) collective-permute-start(f32[30,24,128]{2,1,0:T(8,128)S(1)} %get-tuple-element.44), channel_id=1, source_target_pairs={{16,32},{48,64},{80,96},{32,16},{64,48},{96,80},{17,33},{49,65},{8... | collective-permute-start | bytes 1105928 | tf_op jit(solution)/shard_map/ppermute | solution.py:607
  3.7 5.9 %collective-permute-start = (f32[6,32,128]{2,1,0:T(8,128)S(1)}, f32[6,32,128]{2,1,0:T(8,128)S(1)}, u32[]{:S(2)}, u32[]{:S(2)}) collective-permute-start(f32[6,32,128]{2,1,0:T(8,128)S(1)} %get-tuple-element.39), channel_id=1, source_target_pairs={{1,2},{3,4},{5,6},{7,8},{9,10},{11,12},{13,14},{2,1},{4,3},{6,5},{... | collective-permute-start | bytes 294920 | tf_op jit(solution)/shard_map/ppermute | solution.py:607
  4.4 7.8 %collective-permute-start.1 = (f32[6,32,128]{2,1,0:T(8,128)S(1)}, f32[6,32,128]{2,1,0:T(8,128)S(1)}, u32[]{:S(2)}, u32[]{:S(2)}) collective-permute-start(f32[6,32,128]{2,1,0:T(8,128)S(1)} %get-tuple-element.40), channel_id=1, source_target_pairs={{0,1},{2,3},{4,5},{6,7},{8,9},{10,11},{12,13},{14,15},{1,0},{3,2},... | collective-permute-start | bytes 294920 | tf_op jit(solution)/shard_map/ppermute | solution.py:607
  12.2 2.9 %collective-permute-start.2 = (f32[12,24,128]{2,1,0:T(8,128)S(1)}, f32[12,24,128]{2,1,0:T(8,128)S(1)}, u32[]{:S(2)}, u32[]{:S(2)}) collective-permute-start(f32[12,24,128]{2,1,0:T(8,128)S(1)} %get-tuple-element.41), channel_id=1, source_target_pairs={{0,16},{32,48},{64,80},{96,112},{16,0},{48,32},{80,64},{112,96},{1... | collective-permute-start | bytes 442376 | tf_op jit(solution)/shard_map/ppermute | solution.py:607
  14.1 1.0 %collective-permute-start.3 = (f32[12,24,128]{2,1,0:T(8,128)S(1)}, f32[12,24,128]{2,1,0:T(8,128)S(1)}, u32[]{:S(2)}, u32[]{:S(2)}) collective-permute-start(f32[12,24,128]{2,1,0:T(8,128)S(1)} %get-tuple-element.42), channel_id=1, source_target_pairs={{16,32},{48,64},{80,96},{32,16},{64,48},{96,80},{17,33},{49,65},{8... | collective-permute-start | bytes 442376 | tf_op jit(solution)/shard_map/ppermute | solution.py:607
  20.0 3.9 %collective-permute-start.7 = (f32[44,128]{1,0:T(8,128)S(1)}, f32[44,128]{1,0:T(8,128)S(1)}, u32[]{:S(2)}, u32[]{:S(2)}) collective-permute-start(f32[44,128]{1,0:T(8,128)S(1)} %get-tuple-element.45.tiles), channel_id=1, source_target_pairs={{0,1},{2,3},{4,5},{6,7},{8,9},{10,11},{12,13},{14,15},{1,0},{3,2},... | collective-permute-start | bytes 67592 | tf_op jit(solution)/shard_map/ppermute | solution.py:607
  21.8 2.1 %collective-permute-start.6 = (f32[44,128]{1,0:T(8,128)S(1)}, f32[44,128]{1,0:T(8,128)S(1)}, u32[]{:S(2)}, u32[]{:S(2)}) collective-permute-start(f32[44,128]{1,0:T(8,128)S(1)} %get-tuple-element.45.tiles), channel_id=1, source_target_pairs={{1,2},{3,4},{5,6},{7,8},{9,10},{11,12},{13,14},{2,1},{4,3},{6,5},{... | collective-permute-start | bytes 67592 | tf_op jit(solution)/shard_map/ppermute | solution.py:607
  23.9 6.4 %collective-permute-start.8 = (f32[44,256]{1,0:T(8,128)S(1)}, f32[44,256]{1,0:T(8,128)S(1)}, u32[]{:S(2)}, u32[]{:S(2)}) collective-permute-start(f32[44,256]{1,0:T(8,128)S(1)} %window.1.mine), channel_id=1, source_target_pairs={{0,16},{32,48},{64,80},{96,112},{16,0},{48,32},{80,64},{112,96},{1... | collective-permute-start | bytes 135176 | tf_op jit(solution)/shard_map/ppermute | solution.py:658
  30.4 0.7 %collective-permute-start.9 = (f32[88,256]{1,0:T(8,128)S(1)}, f32[88,256]{1,0:T(8,128)S(1)}, u32[]{:S(2)}, u32[]{:S(2)}) collective-permute-start(f32[88,256]{1,0:T(8,128)S(1)} %join.1), channel_id=1, source_target_pairs={{16,32},{48,64},{80,96},{32,16},{64,48},{96,80},{17,33},{49,65},{8... | collective-permute-start | bytes 270344 | tf_op jit(solution)/shard_map/ppermute | solution.py:662
  31.1 7.4 %collective-permute-start.10 = (f32[88,256]{1,0:T(8,128)S(1)}, f32[88,256]{1,0:T(8,128)S(1)}, u32[]{:S(2)}, u32[]{:S(2)}) collective-permute-start(f32[88,256]{1,0:T(8,128)S(1)} %collective-permute-done.9.received), channel_id=1, source_target_pairs={{0,16},{32,48},{64,80},{96,112},{16,0},{48,32},{80,64},{112,96},{1... | collective-permute-start | bytes 270344 | tf_op jit(solution)/shard_map/ppermute | solution.py:663
  41.6 1.3 %collective-permute-start.11 = (f32[8,128]{1,0:T(8,128)S(1)}, f32[8,128]{1,0:T(8,128)S(1)}, u32[]{:S(2)}, u32[]{:S(2)}) collective-permute-start(f32[8,128]{1,0:T(8,128)S(1)} %get-tuple-element.68.line), channel_id=1, source_target_pairs={{0,16},{32,48},{64,80},{96,112},{16,0},{48,32},{80,64},{112,96},{1... | collective-permute-start | bytes 12296 | tf_op jit(solution)/shard_map/ppermute | solution.py:677

commit v7 on v6

--- a/solution.py
+++ b/solution.py
@@ -166,21 +166,13 @@
             put(2 * q + 1, m, jnp.where(odd, a, b))
 
 
-def edge_kernel(packed, to_sibling, to_other):
+def edge_kernel(packed, from_next, from_pair, to_sibling, to_other):
     even = (position()[0] & 1) == 0
-    for t in range(6 * PAIRS):
-        high, low = packed[t, ROWS - HALO :], packed[t, :HALO]
+    for t in range(6 * PAIRS + 12):
+        ref, at = (packed, t) if t < 30 else (from_pair, t - 30) if t < 36 else (from_next, t - 36)
+        high, low = ref[at, ROWS - HALO :], ref[at, :HALO]
         to_sibling[t] = jnp.where(even, high, low)
         to_other[t] = jnp.where(even, low, high)
-
-
-def second_kernel(from_next, from_pair, to_sibling, to_other):
-    even = (position()[0] & 1) == 0
-    for q, ref in enumerate((from_pair, from_next)):
-        for tile in range(6):
-            high, low = ref[tile, ROWS - HALO :], ref[tile, :HALO]
-            to_sibling[6 * q + tile] = jnp.where(even, high, low)
-            to_other[6 * q + tile] = jnp.where(even, low, high)
 
 
 def coarsen_level(level, fine_rows, out_rows, fine, coarse):
@@ -258,7 +250,7 @@
 
 
 def third_kernel(
-    packed, corner_sibling, corner_other, from_next, from_pair, from_sibling, from_other,
+    packed, from_sibling, from_other, from_next, from_pair,
     source0, inv0, first0, east0, north0, inner0, outer0,
     source1, inv1, first1, east1, north1, inner1, outer1,
     source2, inv2, first2, east2, north2, inner2, outer2,
@@ -285,7 +277,7 @@
 
     for tile in range(6):
         pair, other = [
-            rows_of(corner_sibling[q + tile], corner_other[q + tile], ref[tile]) for q, ref in ((0, from_pair), (6, from_next))
+            rows_of(from_sibling[q + tile], from_other[q + tile], ref[tile]) for q, ref in ((30, from_pair), (36, from_next))
         ]
         right = jnp.where(even_y, pair, other)
         left = jnp.where(even_y, other, pair)
@@ -384,7 +376,7 @@
             outer0[m], outer1[m] = outer[m, slice(16, 64)], out1[m, slice(8, 32)]
 
 
-def window_kernel(tiles, from_next, from_pair, window):
+def window_kernel(tiles, from_pair, from_next, window):
     even = (position()[1] & 1) == 0
     window[:, :LANES] = tiles[...]
     a, b = from_pair[...], from_next[...]
@@ -609,8 +601,8 @@
 
 def shards(pressure, soil, vg_alpha, vg_n, sat_cond, storage, right_side):
     count_x, count_y = lax.axis_size("gx"), lax.axis_size("gy")
-    block, slab = scratch(2 * PAIRS, ROWS, LANES), shape(6 * PAIRS, HALO, LANES)
-    side, corner = shape(6, ROWS, LANES), shape(12, HALO, LANES)
+    block = scratch(2 * PAIRS, ROWS, LANES)
+    side = shape(6, ROWS, LANES)
     arguments = (pressure, soil, storage, right_side, *[v.reshape(1, NSOIL) for v in (vg_alpha, vg_n, sat_cond)])
     packed, *sides = pl.pallas_call(
         first_kernel, out_shape=(shape(6 * PAIRS, ROWS, LANES), side, side),
@@ -621,14 +613,11 @@
         compiler_params=params(4), name="conductivity",
     )(*[pltpu.with_memory_space_constraint(v, pltpu.MemorySpace.HBM) for v in arguments])
     beside_y = pair_exchange(sides, "gy")
+    slab = shape(6 * PAIRS + 12, HALO, LANES)
     slabs = pl.pallas_call(
-        edge_kernel, out_shape=(slab, slab), in_specs=[VM], out_specs=(VM, VM), compiler_params=params(2), name="edges",
-    )(packed)
-    halos = pair_exchange(slabs, "gx") + beside_y
-    corners = pl.pallas_call(
-        second_kernel, out_shape=(corner, corner), in_specs=[VM, VM], out_specs=(VM, VM), compiler_params=params(2), name="corners",
-    )(*beside_y[::-1])
-    halos = pair_exchange(corners, "gx") + beside_y[::-1] + halos[:2]
+        edge_kernel, out_shape=(slab, slab), in_specs=[VM] * 3, out_specs=(VM, VM), compiler_params=params(2), name="edges",
+    )(packed, *beside_y[::-1])
+    halos = pair_exchange(slabs, "gx") + beside_y[::-1]
 
     def sized(rows):
         return [scratch(*dims) for dims in level_dims(rows)]
@@ -640,7 +629,7 @@
     out = pl.pallas_call(
         third_kernel,
         out_shape=(*level_shapes(48), *level_shapes(24), *level_shapes(ROWS2), shape(4 * TILES, LANES), shape(8, LANES)),
-        in_specs=[VM] * 7, out_specs=(VM,) * 23,
+        in_specs=[VM] * 5, out_specs=(VM,) * 23,
         scratch_shapes=[
             two, two, two, two, two, one, four, two, one, one, one,
             two1, two1, two1, two1, one1, four1, two1, one1, one1, one1,
@@ -654,7 +643,7 @@
     tile_pair, tile_next = pair_exchange((tiles, tiles), "gy")
     window = pl.pallas_call(
         window_kernel, out_shape=shape(4 * TILES, WIDE), in_specs=[VM] * 3, out_specs=VM, compiler_params=params(2), name="window",
-    )(tiles, tile_next, tile_pair)
+    )(tiles, tile_pair, tile_next)
     sibling = lax.ppermute(window, "gx", pairs_of(count_x, 0))
     both = pl.pallas_call(
         join_kernel, out_shape=shape(8 * TILES, WIDE), in_specs=[VM] * 2, out_specs=VM, compiler_params=params(2), name="join",

time: 67.6 us -> 67.9 us (level)
  blocking collectives: 22.5 us -> 20.4 us
  waiting for transfers between devices: 7.01 us -> 8.23 us
  starting transfers between devices: 24.8 us -> 26 us
    ppermute x1, starting transfers between devices: 5.56 us -> 8.12 us  [shards(): sibling = lax.ppermute(window, 'gx', pairs_of(count_x, 0))]
    all_to_all x1, blocking collectives: 22.5 us -> 20.4 us  [shards(): lax.all_to_all(both, ('gx', 'gy'), 0, 0, axis_index_groups=kinds, tiled=T...]
    ppermute x8 -> x6, waiting for transfers between devices: 4.38 us -> 5.59 us  [pair_exchange(): lax.ppermute(x_i, axis, pairs_of(count, first))]
    ppermute x8 -> x6, starting transfers between devices: 11.6 us -> 10.8 us  [pair_exchange(): lax.ppermute(x_i, axis, pairs_of(count, first))]
  transfers between devices with their start and end apart: 12 -> 10, of which waited for: 6 -> 6; matrix products, arithmetic and copies ran while one was open for 0% -> 0% of each run, Pallas kernels for 0% -> 0%
where the time goes in v7:
time: 67.9 us; the launch traced here: 67.6 us
  starting transfers between devices  26 us (38%)
  blocking collectives  20.4 us (30%)
  Pallas kernels  12.2 us (18%)
  waiting for transfers between devices  8.23 us (12%)
  between operations  0.72 us (1%)
    all_to_all x1, blocking collectives, shards(): lax.all_to_all(both, ('gx', 'gy'), 0, 0, axis_index_groups=kinds, tiled=T...  20.4 us
    ppermute x6, starting transfers between devices, pair_exchange(): lax.ppermute(x_i, axis, pairs_of(count, first))  10.8 us
    ppermute x1, starting transfers between devices, shards(): sibling = lax.ppermute(window, 'gx', pairs_of(count_x, 0))  8.12 us
    ppermute x1, starting transfers between devices, shards(): passed_on = lax.ppermute(received, 'gx', pairs_of(count_x, 0))  5.95 us
    ppermute x6, waiting for transfers between devices, pair_exchange(): lax.ppermute(x_i, axis, pairs_of(count, first))  5.59 us
    pallas_call x1, Pallas kernels, shards(): pl.pallas_call(third_kernel, out_shape=(*level_shapes(48), *level_shapes(...  4.9 us
    pallas_call x1, Pallas kernels, shards(): pl.pallas_call(fourth_kernel, out_shape=(shape(8, PAIRS, ROWS, LANES), sh...  3.18 us
    pallas_call x1, Pallas kernels, shards(): pl.pallas_call(first_kernel, out_shape=(shape(6 * PAIRS, ROWS, LANES), si...  2.18 us
  transfers between devices with their start and end apart: 10, of which 6 were waited for; matrix products, arithmetic and copies ran while one was open for 0% of the time, Pallas kernels for 0%

profile of v7, /device:TPU:0, one launch (start us, length us, event | category | flops | bytes accessed | tf_op | source)
XLA Modules:
  0.0 67.6 jit_solution(10850049856120132175)
XLA Ops:
  0.6 2.2 %conductivity.1 = (f32[30,32,128]{2,1,0:T(8,128)S(1)}, f32[6,32,128]{2,1,0:T(8,128)S(1)}, f32[6,32,128]{2,1,0:T(8,128)S(1)}) custom-call(f32[10,32,128]{2,1,0:T(8,128)} %pressure_in.1, s32[10,32,128]{2,1,0:T(8,128)} %soil_in.1, f32[10,32,128]{2,1,0:T(8,128)} %storage_in.1, f32[10,32,128]{2,1,0:T(8,128)} %source_in.1, f32[1,23]{1,0:T(1,128)} %bitcast.8, ...), custom_call_target="tpu_custom_call" | custom-call | tf_op jit(solution)/shard_map/conductivity/pallas_call | solution.py:607
  2.8 0.7 collective-permute-start
  3.5 5.2 %collective-permute-start.1 = (f32[6,32,128]{2,1,0:T(8,128)S(1)}, f32[6,32,128]{2,1,0:T(8,128)S(1)}, u32[]{:S(2)}, u32[]{:S(2)}) collective-permute-start(f32[6,32,128]{2,1,0:T(8,128)S(1)} %get-tuple-element.38), channel_id=1, source_target_pairs={{0,1},{2,3},{4,5},{6,7},{8,9},{10,11},{12,13},{14,15},{1,0},{3,2},... | collective-permute-start | bytes 294920 | tf_op jit(solution)/shard_map/ppermute | solution.py:599
  8.7 2.6 %collective-permute-done.1.from_pair = f32[6,32,128]{2,1,0:T(8,128)S(1)} collective-permute-done((f32[6,32,128]{2,1,0:T(8,128)S(1)}, f32[6,32,128]{2,1,0:T(8,128)S(1)}, u32[]{:S(2)}, u32[]{:S(2)}) %collective-permute-start.1) | collective-permute-done | bytes 98336 | tf_op jit(solution)/shard_map/ppermute | solution.py:599
  11.3 0.1 edges.1
  11.4 0.1 collective-permute-start.2
  11.5 0.7 %collective-permute-start.3 = (f32[42,24,128]{2,1,0:T(8,128)S(1)}, f32[42,24,128]{2,1,0:T(8,128)S(1)}, u32[]{:S(2)}, u32[]{:S(2)}) collective-permute-start(f32[42,24,128]{2,1,0:T(8,128)S(1)} %get-tuple-element.40), channel_id=1, source_target_pairs={{16,32},{48,64},{80,96},{32,16},{64,48},{96,80},{17,33},{49,65},{8... | collective-permute-start | bytes 1548296 | tf_op jit(solution)/shard_map/ppermute | solution.py:599
  12.2 1.2 %collective-permute-done.2.from_sibling = f32[42,24,128]{2,1,0:T(8,128)S(1)} collective-permute-done((f32[42,24,128]{2,1,0:T(8,128)S(1)}, f32[42,24,128]{2,1,0:T(8,128)S(1)}, u32[]{:S(2)}, u32[]{:S(2)}) %collective-permute-start.2) | collective-permute-done | bytes 516128 | tf_op jit(solution)/shard_map/ppermute | solution.py:599
  13.4 4.9 %descent.1 = (f32[2,5,2,48,128]{4,3,2,1,0:T(8,128)S(1)}, f32[2,5,2,48,128]{4,3,2,1,0:T(8,128)S(1)}, f32[5,2,48,128]{3,2,1,0:T(8,128)S(1)}, f32[2,5,2,48,128]{4,3...) custom-call(f32[30,32,128]{2,1,0:T(8,128)S(1)} %get-tuple-element.36, ...), custom_call_target="tpu_custom_call" | custom-call | tf_op jit(solution)/shard_map/descent/pallas_call | solution.py:629
  18.3 0.7 collective-permute-start.5
  19.0 3.5 %collective-permute-start.4 = (f32[44,128]{1,0:T(8,128)S(1)}, f32[44,128]{1,0:T(8,128)S(1)}, u32[]{:S(2)}, u32[]{:S(2)}) collective-permute-start(f32[44,128]{1,0:T(8,128)S(1)} %get-tuple-element.41.tiles), channel_id=1, source_target_pairs={{0,1},{2,3},{4,5},{6,7},{8,9},{10,11},{12,13},{14,15},{1,0},{3,2},... | collective-permute-start | bytes 67592 | tf_op jit(solution)/shard_map/ppermute | solution.py:599
  22.4 1.8 %collective-permute-done.4.from_pair = f32[44,128]{1,0:T(8,128)S(1)} collective-permute-done((f32[44,128]{1,0:T(8,128)S(1)}, f32[44,128]{1,0:T(8,128)S(1)}, u32[]{:S(2)}, u32[]{:S(2)}) %collective-permute-start.4) | collective-permute-done | bytes 22560 | tf_op jit(solution)/shard_map/ppermute | solution.py:599
  24.3 8.1 %collective-permute-start.6 = (f32[44,256]{1,0:T(8,128)S(1)}, f32[44,256]{1,0:T(8,128)S(1)}, u32[]{:S(2)}, u32[]{:S(2)}) collective-permute-start(f32[44,256]{1,0:T(8,128)S(1)} %window.1.mine), channel_id=1, source_target_pairs={{0,16},{32,48},{64,80},{96,112},{16,0},{48,32},{80,64},{112,96},{1... | collective-permute-start | bytes 135176 | tf_op jit(solution)/shard_map/ppermute | solution.py:647
  32.4 0.9 %collective-permute-done.6.sibling = f32[44,256]{1,0:T(8,128)S(1)} collective-permute-done((f32[44,256]{1,0:T(8,128)S(1)}, f32[44,256]{1,0:T(8,128)S(1)}, u32[]{:S(2)}, u32[]{:S(2)}) %collective-permute-start.6) | collective-permute-done | bytes 45088 | tf_op jit(solution)/shard_map/ppermute | solution.py:647
  33.3 0.7 collective-permute-start.7
  33.9 0.0 collective-permute-done.7.received
  34.0 6.0 %collective-permute-start.8 = (f32[88,256]{1,0:T(8,128)S(1)}, f32[88,256]{1,0:T(8,128)S(1)}, u32[]{:S(2)}, u32[]{:S(2)}) collective-permute-start(f32[88,256]{1,0:T(8,128)S(1)} %collective-permute-done.7.received), channel_id=1, source_target_pairs={{0,16},{32,48},{64,80},{96,112},{16,0},{48,32},{80,64},{112,96},{1... | collective-permute-start | bytes 270344 | tf_op jit(solution)/shard_map/ppermute | solution.py:652
  39.9 0.9 %collective-permute-done.8.passed_on = f32[88,256]{1,0:T(8,128)S(1)} collective-permute-done((f32[88,256]{1,0:T(8,128)S(1)}, f32[88,256]{1,0:T(8,128)S(1)}, u32[]{:S(2)}, u32[]{:S(2)}) %collective-permute-start.8) | collective-permute-done | bytes 90144 | tf_op jit(solution)/shard_map/ppermute | solution.py:652
  40.8 3.2 %ascent.1 = (f32[8,5,32,128]{3,2,1,0:T(8,128)S(1)}, f32[8,128]{1,0:T(8,128)S(1)}) custom-call(f32[44,256]{1,0:T(8,128)S(1)} %window.1.mine, f32[44,256]{1,0:T(8,128)S(1)} %collective-permute-done.6.sibling, f32[88,256]{1,0:T(8,128)S(1)} %collective-permute-done.7.received, f32[88,256]{1,0:T(8,128)S(1)} %collective-permute-done.8.passed_on, ...), custom_call_target="tpu_custom_call" | custom-call | tf_op jit(solution)/shard_map/ascent/pallas_call | solution.py:656
  44.0 0.4 collective-permute-start.9
  44.5 0.8 %collective-permute-done.9 = f32[8,128]{1,0:T(8,128)S(1)} collective-permute-done((f32[8,128]{1,0:T(8,128)S(1)}, f32[8,128]{1,0:T(8,128)S(1)}, u32[]{:S(2)}, u32[]{:S(2)}) %collective-permute-start.9) | collective-permute-done | bytes 4128 | tf_op jit(solution)/shard_map/ppermute | solution.py:666
  45.3 0.1 maximum_bitcast_fusion
  45.4 20.4 %all_to_all.8 = f32[64,1,32]{2,1,0:T(1,128)S(1)} all-to-all(f32[64,1,32]{2,1,0:T(1,128)S(1)} %broadcast_in_dim.2), channel_id=1, replica_groups={{111,79,47,15,110,78,46,14,109,77,45,13,108,76,44,12,107,75,43,11,106,7..., dimensions={0} | all-to-all | bytes 16384 | tf_op jit(solution)/shard_map/all_to_all | solution.py:669
  65.8 1.8 %outputs.1 = (f32[10,32,128]{2,1,0:T(8,128)}, f32[10,32,128]{2,1,0:T(8,128)}, f32[1,1]{1,0:T(1,128)}) custom-call(f32[64,32]{1,0:T(8,128)S(1)} %bitcast.7, f32[8,128]{1,0:T(8,128)S(1)} %get-tuple-element.64.line, f32[8,5,32,128]{3,2,1,0:T(8,128)S(1)} %get-tuple-element.65.fields), custom_call_target="tpu_custom_call" | custom-call | tf_op jit(solution)/shard_map/outputs/pallas_call | solution.py:673
  (8 shorter events, 0.1 us)
Async XLA Ops:
  2.8 5.9 %collective-permute-start = (f32[6,32,128]{2,1,0:T(8,128)S(1)}, f32[6,32,128]{2,1,0:T(8,128)S(1)}, u32[]{:S(2)}, u32[]{:S(2)}) collective-permute-start(f32[6,32,128]{2,1,0:T(8,128)S(1)} %get-tuple-element.37), channel_id=1, source_target_pairs={{1,2},{3,4},{5,6},{7,8},{9,10},{11,12},{13,14},{2,1},{4,3},{6,5},{... | collective-permute-start | bytes 294920 | tf_op jit(solution)/shard_map/ppermute | solution.py:599
  3.5 7.8 %collective-permute-start.1 = (f32[6,32,128]{2,1,0:T(8,128)S(1)}, f32[6,32,128]{2,1,0:T(8,128)S(1)}, u32[]{:S(2)}, u32[]{:S(2)}) collective-permute-start(f32[6,32,128]{2,1,0:T(8,128)S(1)} %get-tuple-element.38), channel_id=1, source_target_pairs={{0,1},{2,3},{4,5},{6,7},{8,9},{10,11},{12,13},{14,15},{1,0},{3,2},... | collective-permute-start | bytes 294920 | tf_op jit(solution)/shard_map/ppermute | solution.py:599
  11.4 2.0 %collective-permute-start.2 = (f32[42,24,128]{2,1,0:T(8,128)S(1)}, f32[42,24,128]{2,1,0:T(8,128)S(1)}, u32[]{:S(2)}, u32[]{:S(2)}) collective-permute-start(f32[42,24,128]{2,1,0:T(8,128)S(1)} %get-tuple-element.39), channel_id=1, source_target_pairs={{0,16},{32,48},{64,80},{96,112},{16,0},{48,32},{80,64},{112,96},{1... | collective-permute-start | bytes 1548296 | tf_op jit(solution)/shard_map/ppermute | solution.py:599
  11.5 1.9 %collective-permute-start.3 = (f32[42,24,128]{2,1,0:T(8,128)S(1)}, f32[42,24,128]{2,1,0:T(8,128)S(1)}, u32[]{:S(2)}, u32[]{:S(2)}) collective-permute-start(f32[42,24,128]{2,1,0:T(8,128)S(1)} %get-tuple-element.40), channel_id=1, source_target_pairs={{16,32},{48,64},{80,96},{32,16},{64,48},{96,80},{17,33},{49,65},{8... | collective-permute-start | bytes 1548296 | tf_op jit(solution)/shard_map/ppermute | solution.py:599
  18.3 4.1 %collective-permute-start.5 = (f32[44,128]{1,0:T(8,128)S(1)}, f32[44,128]{1,0:T(8,128)S(1)}, u32[]{:S(2)}, u32[]{:S(2)}) collective-permute-start(f32[44,128]{1,0:T(8,128)S(1)} %get-tuple-element.41.tiles), channel_id=1, source_target_pairs={{1,2},{3,4},{5,6},{7,8},{9,10},{11,12},{13,14},{2,1},{4,3},{6,5},{... | collective-permute-start | bytes 67592 | tf_op jit(solution)/shard_map/ppermute | solution.py:599
  19.0 5.3 %collective-permute-start.4 = (f32[44,128]{1,0:T(8,128)S(1)}, f32[44,128]{1,0:T(8,128)S(1)}, u32[]{:S(2)}, u32[]{:S(2)}) collective-permute-start(f32[44,128]{1,0:T(8,128)S(1)} %get-tuple-element.41.tiles), channel_id=1, source_target_pairs={{0,1},{2,3},{4,5},{6,7},{8,9},{10,11},{12,13},{14,15},{1,0},{3,2},... | collective-permute-start | bytes 67592 | tf_op jit(solution)/shard_map/ppermute | solution.py:599
  24.3 9.0 %collective-permute-start.6 = (f32[44,256]{1,0:T(8,128)S(1)}, f32[44,256]{1,0:T(8,128)S(1)}, u32[]{:S(2)}, u32[]{:S(2)}) collective-permute-start(f32[44,256]{1,0:T(8,128)S(1)} %window.1.mine), channel_id=1, source_target_pairs={{0,16},{32,48},{64,80},{96,112},{16,0},{48,32},{80,64},{112,96},{1... | collective-permute-start | bytes 135176 | tf_op jit(solution)/shard_map/ppermute | solution.py:647
  33.3 0.7 %collective-permute-start.7 = (f32[88,256]{1,0:T(8,128)S(1)}, f32[88,256]{1,0:T(8,128)S(1)}, u32[]{:S(2)}, u32[]{:S(2)}) collective-permute-start(f32[88,256]{1,0:T(8,128)S(1)} %join.1), channel_id=1, source_target_pairs={{16,32},{48,64},{80,96},{32,16},{64,48},{96,80},{17,33},{49,65},{8... | collective-permute-start | bytes 270344 | tf_op jit(solution)/shard_map/ppermute | solution.py:651
  34.0 6.9 %collective-permute-start.8 = (f32[88,256]{1,0:T(8,128)S(1)}, f32[88,256]{1,0:T(8,128)S(1)}, u32[]{:S(2)}, u32[]{:S(2)}) collective-permute-start(f32[88,256]{1,0:T(8,128)S(1)} %collective-permute-done.7.received), channel_id=1, source_target_pairs={{0,16},{32,48},{64,80},{96,112},{16,0},{48,32},{80,64},{112,96},{1... | collective-permute-start | bytes 270344 | tf_op jit(solution)/shard_map/ppermute | solution.py:652
  44.0 1.3 %collective-permute-start.9 = (f32[8,128]{1,0:T(8,128)S(1)}, f32[8,128]{1,0:T(8,128)S(1)}, u32[]{:S(2)}, u32[]{:S(2)}) collective-permute-start(f32[8,128]{1,0:T(8,128)S(1)} %get-tuple-element.64.line), channel_id=1, source_target_pairs={{0,16},{32,48},{64,80},{96,112},{16,0},{48,32},{80,64},{112,96},{1... | collective-permute-start | bytes 12296 | tf_op jit(solution)/shard_map/ppermute | solution.py:666
